TPU v7x, 32 devices: a whole 2x2x4 slice. The times are simulated.
32 devices in a mesh: snap: 8 (over z, x), row: 4 (over y, core).
Axes of the slice: x: 2, y: 2, z: 4, core: 2. Of those that a mesh axis runs over, the one named last changes fastest.
Arguments:
- snapshots: float32 [512, 131072], P('snap', 'row'), may hold values from -200 to 200, as said below
Outputs:
- modes: float32 [512, 131072], P(None, ('row', 'snap'))
- factor: float32 [512, 512], replicated
Inputs may be any that keep to these rules, and one draw needn't show every extreme that they name: `snapshots`: finite snapshot values.
All inputs are finite; a program needn't handle non-finite values.
Results may differ from a plain program's by a relative error of at most 0.00007.
Values sent between devices are 32-bit elements; how exact they have to be, the bound alone decides.
No kernel may reach another device: no remote copies, remote signals or barrier semaphores. Data moves between devices by JAX's collectives and lax.ppermute only.
A program may use at most 128 MiB of HBM per device.

v0:
```python
import math

import jax
import jax.numpy as jnp
from jax import lax
from jax.sharding import PartitionSpec as P


def local(snapshots):
    gathered = lax.all_to_all(snapshots, "snap", split_axis=1, concat_axis=0, tiled=True)
    local_gram = lax.dot_general(
        gathered,
        gathered,
        (((1,), (1,)), ((), ())),
        precision=lax.Precision.HIGHEST,
        preferred_element_type=jnp.float32,
    )
    full_gram = lax.psum(local_gram, ("snap", "row"))
    factor_full = jnp.linalg.cholesky(full_gram)
    solved = jax.scipy.linalg.solve_triangular(factor_full, gathered, lower=True)
    cell_count = gathered.shape[1] * lax.axis_size("snap") * lax.axis_size("row")
    root_cells = math.sqrt(cell_count)
    return (solved * root_cells, factor_full / root_cells)


def solution(mesh):
    in_specs = (P("snap", "row"),)
    out_specs = (P(None, ("row", "snap")), P())
    return jax.shard_map(local, mesh=mesh, in_specs=in_specs, out_specs=out_specs, check_vma=False)
```

profile of v0, /device:TPU:0, one launch (start us, length us, event | category | flops | bytes accessed | tf_op | source)
XLA Modules:
  0.0 531.8 jit_solution(1351545891176304342)
XLA Ops:
  7.2 7.8 %copy.20 = f32[8,8,8,4096]{3,2,0,1:T(8,128)} copy(f32[8,8,8,4096]{3,2,1,0:T(8,128)} %bitcast.63) | data formatting | bytes 16777216 | tf_op jit(solution)/shard_map/all_to_all | solution.py:10
  14.9 7.3 %all-to-all-start = ((f32[64,8,4096]{2,0,1:T(8,128)}), f32[64,8,4096]{2,0,1:T(8,128)}, u32[]{:S(2)}, u32[]{:S(2)}) async-start(f32[64,8,4096]{2,0,1:T(8,128)} %bitcast.62), calls=%async_computation | async-start | bytes 16777216 | tf_op jit(solution)/shard_map/all_to_all | solution.py:10
  22.3 183.1 %all-to-all-done = f32[64,8,4096]{2,0,1:T(8,128)} async-done(((f32[64,8,4096]{2,0,1:T(8,128)}), f32[64,8,4096]{2,0,1:T(8,128)}, u32[]{:S(2)}, u32[]{:S(2)}) %all-to-all-start) | async-done | bytes 8388640 | tf_op jit(solution)/shard_map/all_to_all | solution.py:10
  205.4 17.4 %fusion.37 = f32[512,512]{0,1:T(8,128)} fusion(f32[512,4096]{1,0:T(8,128)} %bitcast.1), kind=kOutput, calls=%fused_computation.71 | convolution fusion | flops 12884901888 | bytes 9437184 | tf_op jit(solution)/shard_map/dot_general | solution.py:11
  222.8 6.3 %fusion.36 = (f32[2,64,4096]{2,1,0:T(8,128)}, f32[2,64,4096]{2,1,0:T(8,128)}, f32[2,64,4096]{2,1,0:T(8,128)S(1)}, f32[2,64,4096]{2,1,0:T(8,128)}) fusion(f32[8,64,4096]{2,1,0:T(8,128)} %bitcast), kind=kLoop, calls=%fused_computation.70 | loop fusion | bytes 16777216 | tf_op jit(solution)/shard_map/jit(_solve_triangular)/triangular_solve | solution.py:20
  229.1 122.7 %all-reduce.3.cloned.1.call-done = f32[512,512]{0,1:T(8,128)} async-done(((f32[512,512]{0,1:T(8,128)}), f32[512,512]{0,1:T(8,128)}) %all-reduce.3.cloned.1.call-update) | async-done | bytes 1048592 | tf_op jit(solution)/shard_map/psum | solution.py:18
  351.8 2.6 copy.16
  354.5 1.4 fusion.12
  355.9 1.0 copy-done.3
  356.9 11.7 %cholesky.104 = f32[128,128]{1,0:T(8,128)S(1)} custom-call(f32[128,128]{1,0:T(8,128)S(1)} %cholesky.266), custom_call_target="Cholesky" | custom-call | tf_op jit(solution)/shard_map/jit(cholesky)/cholesky | solution.py:19
  368.7 0.1 cholesky.224
  368.8 9.8 %custom-call.31 = f32[1,128,128]{1,2,0:T(8,128)S(1)} custom-call(f32[1,128,128]{2,1,0:T(8,128)S(1)} %get-tuple-element.35), custom_call_target="InvertDiagBlocksLowerTriangular" | custom-call | tf_op jit(solution)/shard_map/jit(cholesky)/cholesky | solution.py:19
  378.6 1.2 constant_dynamic-update-slice_fusion.3
  379.8 1.3 convolution_subtract_fusion.2
  381.1 11.7 %cholesky.217 = f32[128,128]{1,0:T(8,128)S(1)} custom-call(f32[128,128]{1,0:T(8,128)S(1)} %cholesky.270), custom_call_target="Cholesky" | custom-call | tf_op jit(solution)/shard_map/jit(cholesky)/cholesky | solution.py:19
  392.9 10.2 %custom-call.32 = f32[1,128,128]{1,2,0:T(8,128)S(1)} custom-call(f32[1,128,128]{2,1,0:T(8,128)S(1)} %get-tuple-element.32), custom_call_target="InvertDiagBlocksLowerTriangular" | custom-call | tf_op jit(solution)/shard_map/jit(cholesky)/cholesky | solution.py:19
  403.0 0.3 convolution_dynamic-update-slice_fusion
  403.3 1.3 convolution_subtract_fusion.3
  404.6 11.7 %cholesky.238 = f32[128,128]{1,0:T(8,128)S(1)} custom-call(f32[128,128]{1,0:T(8,128)S(1)} %cholesky.275), custom_call_target="Cholesky" | custom-call | tf_op jit(solution)/shard_map/jit(cholesky)/cholesky | solution.py:19
  416.3 9.8 %custom-call.33 = f32[1,128,128]{1,2,0:T(8,128)S(1)} custom-call(f32[1,128,128]{2,1,0:T(8,128)S(1)} %get-tuple-element.29), custom_call_target="InvertDiagBlocksLowerTriangular" | custom-call | tf_op jit(solution)/shard_map/jit(cholesky)/cholesky | solution.py:19
  426.2 0.2 convolution_dynamic-update-slice_fusion.1
  426.4 1.2 convolution_subtract_fusion.4
  427.6 11.8 %cholesky.255 = f32[128,128]{1,0:T(8,128)S(1)} custom-call(f32[128,128]{1,0:T(8,128)S(1)} %convolution_subtract_fusion.4), custom_call_target="Cholesky" | custom-call | tf_op jit(solution)/shard_map/jit(cholesky)/cholesky | solution.py:19
  439.5 0.7 compare_reduce_fusion.1
  440.2 0.7 compare_reduce_fusion
  440.9 0.7 compare_reduce_fusion.2
  444.1 1.6 fusion.14
  445.7 14.2 %while.1 = (s32[]{:T(128)}, f32[512,512]{1,0:T(8,128)}, s32[4,2]{0,1:T(2,128)S(1)}, f32[4,128,128]{2,1,0:T(8,128)}, s32[]{:T(128)}) while((s32[]{:T(128)}, f32[512,512]{1,0:T(8,128)}, s32[4,2]{0,1:T(2,128)S(1)}, f32[4,128,128]{2,1,0:T(8,128)}, s32[]{:T(128)}) %tuple.35), condition=%wide.while_cond, body=%wide.while_body.sunk | while | flops 2 | bytes 132205 | solution.py:20
  445.7 0.1 constant_dynamic-slice_fusion.2
  445.8 0.6 fusion.47
  446.4 2.9 bitcast_dynamic-update-slice_fusion.2
  449.3 0.1 constant_dynamic-slice_fusion.2
  449.4 0.6 fusion.47
  449.9 2.9 bitcast_dynamic-update-slice_fusion.2
  452.8 0.1 constant_dynamic-slice_fusion.2
  452.9 0.6 fusion.47
  453.5 2.9 bitcast_dynamic-update-slice_fusion.2
  456.5 0.6 fusion.47
  457.0 2.8 bitcast_dynamic-update-slice_fusion.2
  459.9 40.1 %custom-call.34 = f32[4,128,128]{1,2,0:T(8,128)S(1)} custom-call(f32[4,128,128]{2,1,0:T(8,128)} %get-tuple-element.9), custom_call_target="InvertDiagBlocksLowerTriangular" | custom-call | tf_op jit(solution)/shard_map/jit(_solve_triangular)/triangular_solve | solution.py:20
  500.0 3.5 fusion.27
  503.5 2.8 convolution_subtract_fusion.1
  506.3 1.9 fusion.26
  508.3 3.3 convolution_subtract_fusion
  511.6 1.9 fusion.24
  513.5 5.0 fusion.6
  518.6 1.9 fusion.23
  520.5 4.2 maximum_multiply_fusion
  (20 shorter events, 0.3 us)
Async XLA Ops:
  14.9 190.4 %all-to-all-start = ((f32[64,8,4096]{2,0,1:T(8,128)}), f32[64,8,4096]{2,0,1:T(8,128)}, u32[]{:S(2)}, u32[]{:S(2)}) async-start(f32[64,8,4096]{2,0,1:T(8,128)} %bitcast.62), calls=%async_computation | async-start | bytes 16777216 | tf_op jit(solution)/shard_map/all_to_all | solution.py:10
  22.2 329.7 %all-reduce.3.cloned.1.call-start = ((), (), s32[]{:S(2)}) async-start(), calls=%async_computation.1 | async-start | bytes 2097152 | tf_op jit(solution)/shard_map/psum | solution.py:18
  351.8 2.6 copy-start.2
  355.9 1.0 copy-start.3
  506.3 2.0 copy-start.1
  511.6 2.0 copy-start
Sparse Core Ops, SparseCore 0:
  222.9 128.9 all-reduce.2
where the time goes:
time: 536 us; the launch traced here: 532 us
  waiting for transfers between devices  306 us (57%)
  other arithmetic  126 us (24%)
  matrix products  43.3 us (8%)
  local copies, waits for them, and re-layouts  32 us (6%)
  between operations  17 us (3%)
  starting transfers between devices  7.29 us (1%)
    all_to_all x1, waiting for transfers between devices, local(): lax.all_to_all(snapshots, 'snap', split_axis=1, concat_axis=0, tiled=True)  183 us
    psum x1, waiting for transfers between devices, local(): full_gram = lax.psum(local_gram, ('snap', 'row'))  123 us
    another operation x14, other arithmetic, local(): factor_full = jnp.linalg.cholesky(full_gram)  79 us
    another operation x2, other arithmetic, local(): jax.scipy.linalg.solve_triangular(factor_full, gathered, lower=True)  40.1 us
    another operation x7, matrix products, local(): jax.scipy.linalg.solve_triangular(factor_full, gathered, lower=True)  20.4 us
    dot_general x1, matrix products, local(): lax.dot_general(gathered, gathered, (((1,), (1,)), ((), ())), precision=l...  17.4 us
    another operation x12, local copies, waits for them, and re-layouts  14.1 us
  transfers between devices with their start and end apart: 2, of which 2 were waited for; matrix products, arithmetic and copies ran while one was open for 1% of the time, Pallas kernels for 0%

commit v1 on v0

v1 whole, which is shorter than its diff:
```python
import functools
import math

import jax
import jax.numpy as jnp
from jax import lax
from jax.experimental import pallas as pl
from jax.experimental.pallas import tpu as pltpu
from jax.sharding import PartitionSpec as P

BLK = 128
SUB = 8
FULL = lax.Precision.HIGHEST
VMEM = pl.BlockSpec(memory_space=pltpu.VMEM)


def lower_blocks(size):
    return [(i, j) for i in range(size // BLK) for j in range(i + 1)]


def split(x):
    hi = x.astype(jnp.bfloat16)
    return hi, (x - hi.astype(jnp.float32)).astype(jnp.bfloat16)


def gram_kernel(s_ref, out_ref, acc):
    size = s_ref.shape[0]
    hi, lo = split(s_ref[...])
    part = lax.dot_general(
        hi, jnp.concatenate([hi, lo], axis=0), (((1,), (1,)), ((), ())), preferred_element_type=jnp.float32
    )

    @pl.when(pl.program_id(0) == 0)
    def _():
        acc[...] = part

    @pl.when(pl.program_id(0) > 0)
    def _():
        acc[...] += part

    @pl.when(pl.program_id(0) == pl.num_programs(0) - 1)
    def _():
        for n, (i, j) in enumerate(lower_blocks(size)):
            high = acc[i * BLK : (i + 1) * BLK, j * BLK : (j + 1) * BLK]
            mixed = acc[i * BLK : (i + 1) * BLK, size + j * BLK : size + (j + 1) * BLK]
            other = acc[j * BLK : (j + 1) * BLK, size + i * BLK : size + (i + 1) * BLK]
            out_ref[n * BLK : (n + 1) * BLK, :] = high + mixed + other.T


def gram(s, tile):
    size, cells = s.shape
    rows = len(lower_blocks(size)) * BLK
    return pl.pallas_call(
        gram_kernel,
        grid=(cells // tile,),
        out_shape=jax.ShapeDtypeStruct((rows, BLK), jnp.float32),
        in_specs=[pl.BlockSpec((size, tile), lambda i: (0, i))],
        out_specs=pl.BlockSpec((rows, BLK), lambda i: (0, 0)),
        scratch_shapes=[pltpu.VMEM((size, 2 * size), jnp.float32)],
        compiler_params=pltpu.CompilerParams(vmem_limit_bytes=32 * 2**20),
        cost_estimate=pl.CostEstimate(flops=4 * size * size * cells, bytes_accessed=4 * size * cells, transcendentals=0),
        name="gram",
    )(s)


def exchange(x, axis, bit):
    n = lax.axis_size(axis)
    return lax.ppermute(x, axis, [(i, i ^ bit) for i in range(n)])


def bits(axis):
    n = lax.axis_size(axis)
    return [1 << b for b in range(n.bit_length() - 1)]


def sum_all(x):
    for bit in bits("row"):
        upper = (lax.axis_index("row") & bit) > 0
        half = x.shape[0] // 2
        first, second = x[:half], x[half:]
        x = jnp.where(upper, second, first) + exchange(jnp.where(upper, first, second), "row", bit)
    for bit in bits("snap"):
        x = x + exchange(x, "snap", bit)
    for bit in reversed(bits("row")):
        upper = (lax.axis_index("row") & bit) > 0
        got = exchange(x, "row", bit)
        x = jnp.where(upper, jnp.concatenate([got, x]), jnp.concatenate([x, got]))
    return x


def recip(d):
    r = pl.reciprocal(d, approx=True)
    return r * (2.0 - d * r)


def factor_block(load, store_x, store_u):
    groups = BLK // SUB
    lane = lax.broadcasted_iota(jnp.int32, (SUB, BLK), 1)
    sub = lax.broadcasted_iota(jnp.int32, (SUB, BLK), 0)
    rows = [load(i) for i in range(groups)]
    for k in range(groups):
        base = SUB * k
        panel = rows[k]

        def columns(x):
            return [jnp.broadcast_to(x[:, base + j : base + j + 1], (SUB, BLK)) for j in range(SUB)]

        spread = columns(panel)
        cell = {(i, j): jnp.broadcast_to(spread[j][i : i + 1, :], (SUB, BLK)) for i in range(SUB) for j in range(i + 1)}
        inv, ratio = [], {}
        for j in range(SUB):
            inv.append(recip(cell[j, j]))
            for i in range(j + 1, SUB):
                ratio[i, j] = cell[i, j] * inv[j]
            for i in range(j + 1, SUB):
                for c in range(j + 1, i + 1):
                    cell[i, c] = cell[i, c] - ratio[i, j] * cell[c, j]

        def multipliers(cols):
            out = []
            for j in range(SUB):
                for c in range(j + 1, SUB):
                    cols[c] = cols[c] - cols[j] * ratio[c, j]
                out.append(cols[j] * inv[j])
            return out

        own = [jnp.where(sub > j, m, 0.0) for j, m in enumerate(multipliers(list(spread)))]
        in_block = (lane >= base) & (lane < base + SUB)
        aug = jnp.where(in_block, jnp.where(lane - base == sub, 1.0, 0.0), panel)
        up = panel
        pivots = jnp.zeros((SUB, BLK), jnp.float32)
        pivot_rows = []
        for j in range(SUB):
            row = jnp.broadcast_to(aug[j : j + 1, :], (SUB, BLK))
            pivot_rows.append(row)
            if j < SUB - 1:
                aug = aug - own[j] * row
                up = up - own[j] * jnp.broadcast_to(up[j : j + 1, :], (SUB, BLK))
            pivots = jnp.where(sub == j, cell[j, j], pivots)
        for i in range(k + 1, groups):
            m = multipliers(columns(rows[i]))
            acc = [m[j] * pivot_rows[j] for j in range(SUB)]
            while len(acc) > 1:
                acc = [acc[2 * t] + acc[2 * t + 1] for t in range(len(acc) // 2)]
            rows[i] = jnp.where(in_block, 0.0, rows[i]) - acc[0]
        scale = lax.rsqrt(pivots)
        store_x(k, jnp.where(lane <= base + sub, aug * scale, 0.0))
        store_u(k, jnp.where(lane >= base + sub, up * scale, 0.0))


def factor_kernel(root, gram_ref, lower_ref, white_ref, work, xs, us, left):
    size = lower_ref.shape[0]
    for n, (i, j) in enumerate(lower_blocks(size)):
        block = gram_ref[n * BLK : (n + 1) * BLK, :]
        work[i * BLK : (i + 1) * BLK, j * BLK : (j + 1) * BLK] = block
        if i != j:
            work[j * BLK : (j + 1) * BLK, i * BLK : (i + 1) * BLK] = block.T
    col = lax.broadcasted_iota(jnp.int32, (BLK, size), 1)
    eye = jnp.where(
        lax.broadcasted_iota(jnp.int32, (BLK, BLK), 0) == lax.broadcasted_iota(jnp.int32, (BLK, BLK), 1), 1.0, 0.0
    )

    def outer(b, carry):
        at = pl.multiple_of(b * BLK, BLK)
        here = pl.ds(at, BLK)

        def load(i):
            return work[pl.ds(pl.multiple_of(at + SUB * i, SUB), SUB), here]

        def store_x(k, v):
            xs[pl.ds(SUB * k, SUB), :] = v

        def store_u(k, v):
            us[pl.ds(SUB * k, SUB), :] = v

        factor_block(load, store_x, store_u)
        work[here, here] = eye
        y = jnp.dot(xs[...], work[here, :], precision=FULL, preferred_element_type=jnp.float32)
        work[here, :] = y
        white_ref[here, :] = jnp.where(col < at + BLK, y, 0.0) * root
        left[...] = jnp.where(col >= at + BLK, y, 0.0).T
        lower_ref[:, here] = left[...] * (1.0 / root)
        lower_ref[here, here] = us[...].T * (1.0 / root)
        for i in range(1, size // BLK):

            @pl.when(i > b)
            def _(i=i):
                sl = pl.ds(i * BLK, BLK)
                work[sl, here] = jnp.zeros((BLK, BLK), jnp.float32)
                work[sl, :] = work[sl, :] - jnp.dot(left[sl, :], y, precision=FULL, preferred_element_type=jnp.float32)

        return carry

    lax.fori_loop(0, size // BLK, outer, 0)


def factorize(packed, size, root):
    out = jax.ShapeDtypeStruct((size, size), jnp.float32)
    return pl.pallas_call(
        functools.partial(factor_kernel, root),
        out_shape=(out, out),
        in_specs=[VMEM],
        out_specs=(VMEM, VMEM),
        scratch_shapes=[
            pltpu.VMEM((size, size), jnp.float32),
            pltpu.VMEM((BLK, BLK), jnp.float32),
            pltpu.VMEM((BLK, BLK), jnp.float32),
            pltpu.VMEM((size, BLK), jnp.float32),
        ],
        compiler_params=pltpu.CompilerParams(vmem_limit_bytes=24 * 2**20),
        name="factor",
    )(packed)


def modes_kernel(w_ref, s_ref, out_ref, w_hi, w_lo):
    size = w_ref.shape[0]

    @pl.when(pl.program_id(0) == 0)
    def _():
        w_hi[...], w_lo[...] = split(w_ref[...])

    hi, lo = split(s_ref[...])
    half = size // 2
    for rows, depth in ((slice(0, half), half), (slice(half, size), size)):
        a, b = w_hi[rows, :depth], w_lo[rows, :depth]
        out_ref[rows, :] = (
            jnp.dot(a, hi[:depth], preferred_element_type=jnp.float32)
            + jnp.dot(a, lo[:depth], preferred_element_type=jnp.float32)
            + jnp.dot(b, hi[:depth], preferred_element_type=jnp.float32)
        )


def whiten(w, s, tile):
    size, cells = s.shape
    return pl.pallas_call(
        modes_kernel,
        grid=(cells // tile,),
        out_shape=jax.ShapeDtypeStruct((size, cells), jnp.float32),
        in_specs=[pl.BlockSpec((size, size), lambda i: (0, 0)), pl.BlockSpec((size, tile), lambda i: (0, i))],
        out_specs=pl.BlockSpec((size, tile), lambda i: (0, i)),
        scratch_shapes=[pltpu.VMEM((size, size), jnp.bfloat16), pltpu.VMEM((size, size), jnp.bfloat16)],
        compiler_params=pltpu.CompilerParams(vmem_limit_bytes=32 * 2**20),
        name="modes",
    )(w, s)


def local(snapshots):
    gathered = lax.all_to_all(snapshots, "snap", split_axis=1, concat_axis=0, tiled=True)
    size, cells = gathered.shape
    root = math.sqrt(cells * lax.axis_size("snap") * lax.axis_size("row"))
    packed = sum_all(gram(gathered, cells // 4))
    factor, white = factorize(packed, size, root)
    return whiten(white, gathered, cells // 8), factor


def solution(mesh):
    in_specs = (P("snap", "row"),)
    out_specs = (P(None, ("row", "snap")), P())
    return jax.shard_map(local, mesh=mesh, in_specs=in_specs, out_specs=out_specs, check_vma=False)
```

time: 536 us -> 278 us (0.52)
  other arithmetic: 126 us -> 0.26 us
  waiting for transfers between devices: 306 us -> 211 us
  Pallas kernels: 0 us -> 44.8 us
  matrix products: 43.3 us -> 0 us
  local copies, waits for them, and re-layouts: 32 us -> 7.77 us
  between operations: 17 us -> 0.71 us
  starting transfers between devices: 7.29 us -> 13 us
    psum x1 -> x0, waiting for transfers between devices: 123 us -> none  [local(): full_gram = lax.psum(local_gram, ('snap', 'row'))]
    another operation x16 -> x0, other arithmetic: 119 us -> none  [the longest x14 79 us: local(): factor_full = jnp.linalg.cholesky(full_gram)]
    pallas_call x0 -> x3, Pallas kernels: none -> 44.8 us  [the longest x1 25.5 us: factorize(): pl.pallas_call(functools.partial(factor_kernel, root), out_shape=(out, ou...]
    ppermute x0 -> x7, waiting for transfers between devices: none -> 27.7 us  [exchange(): return lax.ppermute(x, axis, [(i, i ^ bit) for i in range(n)])]
    another operation x13 -> x0, matrix products: 25.9 us -> none  [the longest x7 20.4 us: local(): jax.scipy.linalg.solve_triangular(factor_full, gathered, lower=True)]
    another operation x18 -> x0, local copies, waits for them, and re-layouts: 20.6 us -> none
    dot_general x1 -> x0, matrix products: 17.4 us -> none  [local(): lax.dot_general(gathered, gathered, (((1,), (1,)), ((), ())), precision=l...]
    ppermute x0 -> x7, starting transfers between devices: none -> 5.79 us  [exchange(): return lax.ppermute(x, axis, [(i, i ^ bit) for i in range(n)])]
  transfers between devices with their start and end apart: 2 -> 8, of which waited for: 2 -> 8; matrix products, arithmetic and copies ran while one was open for 1% -> 0% of each run, Pallas kernels for 0% -> 0%
where the time goes in v1:
time: 278 us; the launch traced here: 277 us
  waiting for transfers between devices  211 us (76%)
  Pallas kernels  44.8 us (16%)
  starting transfers between devices  13 us (5%)
  local copies, waits for them, and re-layouts  7.77 us (3%)
    all_to_all x1, waiting for transfers between devices, local(): lax.all_to_all(snapshots, 'snap', split_axis=1, concat_axis=0, tiled=True)  183 us
    ppermute x7, waiting for transfers between devices, exchange(): return lax.ppermute(x, axis, [(i, i ^ bit) for i in range(n)])  27.7 us
    pallas_call x1, Pallas kernels, factorize(): pl.pallas_call(functools.partial(factor_kernel, root), out_shape=(out, ou...  25.5 us
    pallas_call x1, Pallas kernels, whiten(): pl.pallas_call(modes_kernel, grid=(cells // tile,), out_shape=jax.ShapeDt...  11.4 us
    pallas_call x1, Pallas kernels, gram(): pl.pallas_call(gram_kernel, grid=(cells // tile,), out_shape=jax.ShapeDty...  7.87 us
    all_to_all x1, local copies, waits for them, and re-layouts, local(): lax.all_to_all(snapshots, 'snap', split_axis=1, concat_axis=0, tiled=True)  7.77 us
    all_to_all x1, starting transfers between devices, local(): lax.all_to_all(snapshots, 'snap', split_axis=1, concat_axis=0, tiled=True)  7.25 us
    ppermute x7, starting transfers between devices, exchange(): return lax.ppermute(x, axis, [(i, i ^ bit) for i in range(n)])  5.79 us
  transfers between devices with their start and end apart: 8, of which 8 were waited for; matrix products, arithmetic and copies ran while one was open for 0% of the time, Pallas kernels for 0%

profile of v1, /device:TPU:0, one launch (start us, length us, event | category | flops | bytes accessed | tf_op | source)
XLA Modules:
  0.0 277.4 jit_solution(276006441401528378)
XLA Ops:
  0.6 7.8 %copy.6 = f32[8,8,8,4096]{3,2,0,1:T(8,128)} copy(f32[8,8,8,4096]{3,2,1,0:T(8,128)} %bitcast.8) | data formatting | bytes 16777216 | tf_op jit(solution)/shard_map/all_to_all | solution.py:248
  8.4 7.3 %all-to-all-start = ((f32[64,8,4096]{2,0,1:T(8,128)}), f32[64,8,4096]{2,0,1:T(8,128)}, u32[]{:S(2)}, u32[]{:S(2)}) async-start(f32[64,8,4096]{2,0,1:T(8,128)} %bitcast.7), calls=%async_computation | async-start | bytes 16777216 | tf_op jit(solution)/shard_map/all_to_all | solution.py:248
  15.7 183.2 %all-to-all-done = f32[64,8,4096]{2,0,1:T(8,128)} async-done(((f32[64,8,4096]{2,0,1:T(8,128)}), f32[64,8,4096]{2,0,1:T(8,128)}, u32[]{:S(2)}, u32[]{:S(2)}) %all-to-all-start) | async-done | bytes 8388640 | tf_op jit(solution)/shard_map/all_to_all | solution.py:248
  198.8 7.9 %gram.1 = f32[1280,128]{1,0:T(8,128)S(1)} custom-call(f32[512,4096]{1,0:T(8,128)} %bitcast.1.s_ref), custom_call_target="tpu_custom_call" | custom-call | flops 4294967296 | bytes 8388608 | tf_op jit(solution)/shard_map/gram/pallas_call | solution.py:53
  206.7 0.1 collective-permute-start
  206.8 1.6 collective-permute-done
  208.5 1.6 collective-permute-start.1
  210.1 4.7 %collective-permute-done.1 = f32[320,128]{1,0:T(8,128)S(1)} collective-permute-done((f32[320,128]{1,0:T(8,128)S(1)}, f32[320,128]{1,0:T(8,128)S(1)}, u32[]{:S(2)}, u32[]{:S(2)}) %collective-permute-start.1) | collective-permute-done | bytes 163872 | tf_op jit(solution)/shard_map/ppermute | solution.py:68
  214.9 1.5 collective-permute-start.2
  216.4 4.0 %collective-permute-done.2 = f32[320,128]{1,0:T(8,128)S(1)} collective-permute-done((f32[320,128]{1,0:T(8,128)S(1)}, f32[320,128]{1,0:T(8,128)S(1)}, u32[]{:S(2)}, u32[]{:S(2)}) %collective-permute-start.2) | collective-permute-done | bytes 163872 | tf_op jit(solution)/shard_map/ppermute | solution.py:68
  220.4 0.1 collective-permute-start.3
  220.4 5.3 %collective-permute-done.3 = f32[320,128]{1,0:T(8,128)S(1)} collective-permute-done((f32[320,128]{1,0:T(8,128)S(1)}, f32[320,128]{1,0:T(8,128)S(1)}, u32[]{:S(2)}, u32[]{:S(2)}) %collective-permute-start.3) | collective-permute-done | bytes 163872 | tf_op jit(solution)/shard_map/ppermute | solution.py:68
  225.8 0.9 collective-permute-start.4
  226.6 6.7 %collective-permute-done.4 = f32[320,128]{1,0:T(8,128)S(1)} collective-permute-done((f32[320,128]{1,0:T(8,128)S(1)}, f32[320,128]{1,0:T(8,128)S(1)}, u32[]{:S(2)}, u32[]{:S(2)}) %collective-permute-start.4) | collective-permute-done | bytes 163872 | tf_op jit(solution)/shard_map/ppermute | solution.py:68
  233.3 1.6 collective-permute-start.5
  234.9 3.8 %collective-permute-done.5 = f32[320,128]{1,0:T(8,128)S(1)} collective-permute-done((f32[320,128]{1,0:T(8,128)S(1)}, f32[320,128]{1,0:T(8,128)S(1)}, u32[]{:S(2)}, u32[]{:S(2)}) %collective-permute-start.5) | collective-permute-done | bytes 163872 | tf_op jit(solution)/shard_map/ppermute | solution.py:68
  238.7 0.1 collective-permute-start.6
  238.8 1.6 collective-permute-done.6
  240.5 25.5 %factor.1 = (f32[512,512]{1,0:T(8,128)}, f32[512,512]{1,0:T(8,128)S(1)}) custom-call(f32[1280,128]{1,0:T(8,128)S(1)} %maximum_select_fusion.gram_ref), custom_call_target="tpu_custom_call" | custom-call | tf_op jit(solution)/shard_map/factor/pallas_call | solution.py:199
  266.0 11.4 %modes.1 = f32[512,4096]{1,0:T(8,128)} custom-call(f32[512,512]{1,0:T(8,128)S(1)} %get-tuple-element.4.w_ref, f32[512,4096]{1,0:T(8,128)} %bitcast.1.s_ref), custom_call_target="tpu_custom_call" | custom-call | tf_op jit(solution)/shard_map/modes/pallas_call | solution.py:235
  (9 shorter events, 0.3 us)
Async XLA Ops:
  8.4 190.4 %all-to-all-start = ((f32[64,8,4096]{2,0,1:T(8,128)}), f32[64,8,4096]{2,0,1:T(8,128)}, u32[]{:S(2)}, u32[]{:S(2)}) async-start(f32[64,8,4096]{2,0,1:T(8,128)} %bitcast.7), calls=%async_computation | async-start | bytes 16777216 | tf_op jit(solution)/shard_map/all_to_all | solution.py:248
  206.7 1.7 collective-permute-start
  208.5 6.3 %collective-permute-start.1 = (f32[320,128]{1,0:T(8,128)S(1)}, f32[320,128]{1,0:T(8,128)S(1)}, u32[]{:S(2)}, u32[]{:S(2)}) collective-permute-start(f32[320,128]{1,0:T(8,128)S(1)} %slice_select_fusion.1), channel_id=1, source_target_pairs={{0,2},{1,3},{2,0},{3,1},{4,6},{5,7},{6,4},{7,5},{8,10},{9,11},{10,... | collective-permute-start | bytes 491528 | tf_op jit(solution)/shard_map/ppermute | solution.py:68
  214.9 5.5 %collective-permute-start.2 = (f32[320,128]{1,0:T(8,128)S(1)}, f32[320,128]{1,0:T(8,128)S(1)}, u32[]{:S(2)}, u32[]{:S(2)}) collective-permute-start(f32[320,128]{1,0:T(8,128)S(1)} %select_add_fusion.1), channel_id=1, source_target_pairs={{0,4},{4,0},{8,12},{12,8},{16,20},{20,16},{24,28},{28,24},{1,5},{5... | collective-permute-start | bytes 491528 | tf_op jit(solution)/shard_map/ppermute | solution.py:68
  220.4 5.4 %collective-permute-start.3 = (f32[320,128]{1,0:T(8,128)S(1)}, f32[320,128]{1,0:T(8,128)S(1)}, u32[]{:S(2)}, u32[]{:S(2)}) collective-permute-start(f32[320,128]{1,0:T(8,128)S(1)} %add.17), channel_id=1, source_target_pairs={{0,8},{4,12},{8,0},{12,4},{16,24},{20,28},{24,16},{28,20},{1,9},{5... | collective-permute-start | bytes 491528 | tf_op jit(solution)/shard_map/ppermute | solution.py:68
  225.8 7.5 %collective-permute-start.4 = (f32[320,128]{1,0:T(8,128)S(1)}, f32[320,128]{1,0:T(8,128)S(1)}, u32[]{:S(2)}, u32[]{:S(2)}) collective-permute-start(f32[320,128]{1,0:T(8,128)S(1)} %add.18), channel_id=1, source_target_pairs={{0,16},{4,20},{8,24},{12,28},{16,0},{20,4},{24,8},{28,12},{1,17},{... | collective-permute-start | bytes 491528 | tf_op jit(solution)/shard_map/ppermute | solution.py:68
  233.3 5.4 %collective-permute-start.5 = (f32[320,128]{1,0:T(8,128)S(1)}, f32[320,128]{1,0:T(8,128)S(1)}, u32[]{:S(2)}, u32[]{:S(2)}) collective-permute-start(f32[320,128]{1,0:T(8,128)S(1)} %add.19), channel_id=1, source_target_pairs={{0,2},{1,3},{2,0},{3,1},{4,6},{5,7},{6,4},{7,5},{8,10},{9,11},{10,... | collective-permute-start | bytes 491528 | tf_op jit(solution)/shard_map/ppermute | solution.py:68
  238.7 1.7 collective-permute-start.6

commit v2 on v1

--- a/solution.py
+++ b/solution.py
@@ -23,12 +23,17 @@
     return hi, (x - hi.astype(jnp.float32)).astype(jnp.bfloat16)
 
 
-def gram_kernel(s_ref, out_ref, acc):
-    size = s_ref.shape[0]
-    hi, lo = split(s_ref[...])
-    part = lax.dot_general(
-        hi, jnp.concatenate([hi, lo], axis=0), (((1,), (1,)), ((), ())), preferred_element_type=jnp.float32
-    )
+def gram_kernel(places, first, *refs):
+    places_ref, refs = refs[0], refs[1:]
+    parts, refs = refs[:places], refs[places:]
+    before, (out_ref, hi_ref, lo_ref, acc) = (None, refs) if first else (refs[0], refs[3:])
+    rows, size = parts[0].shape[0], hi_ref.shape[0]
+    for d, part in enumerate(parts):
+        at = pl.ds(pl.multiple_of(places_ref[d] * rows, rows), rows)
+        hi_ref[at, :], lo_ref[at, :] = split(part[...])
+    hi = hi_ref[...]
+    both = jnp.concatenate([hi, lo_ref[...]], axis=0)
+    part = lax.dot_general(hi, both, (((1,), (1,)), ((), ())), preferred_element_type=jnp.float32)
 
     @pl.when(pl.program_id(0) == 0)
     def _():
@@ -44,28 +49,37 @@
             high = acc[i * BLK : (i + 1) * BLK, j * BLK : (j + 1) * BLK]
             mixed = acc[i * BLK : (i + 1) * BLK, size + j * BLK : size + (j + 1) * BLK]
             other = acc[j * BLK : (j + 1) * BLK, size + i * BLK : size + (i + 1) * BLK]
-            out_ref[n * BLK : (n + 1) * BLK, :] = high + mixed + other.T
-
-
-def gram(s, tile):
-    size, cells = s.shape
-    rows = len(lower_blocks(size)) * BLK
+            total = high + mixed + other.T
+            if not first:
+                total = total + before[n * BLK : (n + 1) * BLK, :]
+            out_ref[n * BLK : (n + 1) * BLK, :] = total
+
+
+def gram(places, parts, cells, start, tile, earlier=()):
+    rows, here = parts[0].shape
+    size = rows * len(parts)
+    blocks = len(lower_blocks(size)) * BLK
+    packed = jax.ShapeDtypeStruct((blocks, BLK), jnp.float32)
+    kept = jax.ShapeDtypeStruct((size, cells), jnp.bfloat16)
+    any_place = pl.BlockSpec(memory_space=pl.ANY)
+    column = pl.BlockSpec((size, tile), lambda i, p: (0, i + start // tile))
+    whole = pl.BlockSpec((blocks, BLK), lambda i, p: (0, 0))
+    n = len(parts)
     return pl.pallas_call(
-        gram_kernel,
-        grid=(cells // tile,),
-        out_shape=jax.ShapeDtypeStruct((rows, BLK), jnp.float32),
-        in_specs=[pl.BlockSpec((size, tile), lambda i: (0, i))],
-        out_specs=pl.BlockSpec((rows, BLK), lambda i: (0, 0)),
-        scratch_shapes=[pltpu.VMEM((size, 2 * size), jnp.float32)],
+        functools.partial(gram_kernel, n, not earlier),
+        out_shape=(packed, kept, kept),
+        grid_spec=pltpu.PrefetchScalarGridSpec(
+            num_scalar_prefetch=1,
+            grid=(here // tile,),
+            in_specs=[pl.BlockSpec((rows, tile), lambda i, p: (0, i))] * n + ([whole, any_place, any_place] if earlier else []),
+            out_specs=(whole, column, column),
+            scratch_shapes=[pltpu.VMEM((size, 2 * size), jnp.float32)],
+        ),
+        input_output_aliases={n + 2: 1, n + 3: 2} if earlier else {},
         compiler_params=pltpu.CompilerParams(vmem_limit_bytes=32 * 2**20),
-        cost_estimate=pl.CostEstimate(flops=4 * size * size * cells, bytes_accessed=4 * size * cells, transcendentals=0),
+        cost_estimate=pl.CostEstimate(flops=4 * size * size * here, bytes_accessed=8 * size * here, transcendentals=0),
         name="gram",
-    )(s)
-
-
-def exchange(x, axis, bit):
-    n = lax.axis_size(axis)
-    return lax.ppermute(x, axis, [(i, i ^ bit) for i in range(n)])
+    )(places, *parts, *earlier)
 
 
 def bits(axis):
@@ -73,17 +87,36 @@
     return [1 << b for b in range(n.bit_length() - 1)]
 
 
+def step(x, orders, at):
+    rows, snaps = lax.axis_size("row"), lax.axis_size("snap")
+    pairs = []
+    for r in range(rows):
+        for s in range(snaps):
+            axis, bit = orders[r % 2][at]
+            to = (r ^ bit, s) if axis == "row" else (r, s ^ bit)
+            pairs.append((s * rows + r, to[1] * rows + to[0]))
+    return lax.ppermute(x, ("snap", "row"), pairs)
+
+
+def side(orders, at):
+    core = lax.axis_index("row") % 2
+    flags = [(lax.axis_index(axis) & bit) > 0 for axis, bit in (o[at] for o in orders)]
+    return jnp.where(core == 0, flags[0], flags[1])
+
+
 def sum_all(x):
-    for bit in bits("row"):
-        upper = (lax.axis_index("row") & bit) > 0
+    links = [("row", b) for b in bits("row")[1:]] + [("snap", b) for b in bits("snap")]
+    orders = [[("row", 1), *links], [("row", 1), *links[1:], links[0]]]
+    for at in (0, 1):
+        upper = side(orders, at)
         half = x.shape[0] // 2
         first, second = x[:half], x[half:]
-        x = jnp.where(upper, second, first) + exchange(jnp.where(upper, first, second), "row", bit)
-    for bit in bits("snap"):
-        x = x + exchange(x, "snap", bit)
-    for bit in reversed(bits("row")):
-        upper = (lax.axis_index("row") & bit) > 0
-        got = exchange(x, "row", bit)
+        x = jnp.where(upper, second, first) + step(jnp.where(upper, first, second), orders, at)
+    for at in range(2, len(links) + 1):
+        x = x + step(x, orders, at)
+    for at in (1, 0):
+        upper = side(orders, at)
+        got = step(x, orders, at)
         x = jnp.where(upper, jnp.concatenate([got, x]), jnp.concatenate([x, got]))
     return x
 
@@ -212,45 +245,63 @@
     )(packed)
 
 
-def modes_kernel(w_ref, s_ref, out_ref, w_hi, w_lo):
+def modes_kernel(w_ref, hi_ref, lo_ref, out_ref, w_hi, w_lo):
     size = w_ref.shape[0]
 
     @pl.when(pl.program_id(0) == 0)
     def _():
         w_hi[...], w_lo[...] = split(w_ref[...])
 
-    hi, lo = split(s_ref[...])
     half = size // 2
     for rows, depth in ((slice(0, half), half), (slice(half, size), size)):
         a, b = w_hi[rows, :depth], w_lo[rows, :depth]
+        hi, lo = hi_ref[:depth, :], lo_ref[:depth, :]
         out_ref[rows, :] = (
-            jnp.dot(a, hi[:depth], preferred_element_type=jnp.float32)
-            + jnp.dot(a, lo[:depth], preferred_element_type=jnp.float32)
-            + jnp.dot(b, hi[:depth], preferred_element_type=jnp.float32)
+            jnp.dot(a, hi, preferred_element_type=jnp.float32)
+            + jnp.dot(a, lo, preferred_element_type=jnp.float32)
+            + jnp.dot(b, hi, preferred_element_type=jnp.float32)
         )
 
 
-def whiten(w, s, tile):
-    size, cells = s.shape
+def whiten(w, hi, lo, tile):
+    size, cells = hi.shape
+    column = pl.BlockSpec((size, tile), lambda i: (0, i))
     return pl.pallas_call(
         modes_kernel,
         grid=(cells // tile,),
         out_shape=jax.ShapeDtypeStruct((size, cells), jnp.float32),
-        in_specs=[pl.BlockSpec((size, size), lambda i: (0, 0)), pl.BlockSpec((size, tile), lambda i: (0, i))],
-        out_specs=pl.BlockSpec((size, tile), lambda i: (0, i)),
+        in_specs=[pl.BlockSpec((size, size), lambda i: (0, 0)), column, column],
+        out_specs=column,
         scratch_shapes=[pltpu.VMEM((size, size), jnp.bfloat16), pltpu.VMEM((size, size), jnp.bfloat16)],
         compiler_params=pltpu.CompilerParams(vmem_limit_bytes=32 * 2**20),
         name="modes",
-    )(w, s)
+    )(w, hi, lo)
+
+
+def regroup(snapshots, start, count):
+    n = lax.axis_size("snap")
+    me = lax.axis_index("snap")
+    cells = snapshots.shape[1] // n
+    out = []
+    for d in range(n):
+        block = lax.dynamic_slice_in_dim(snapshots, (me ^ d) * cells + start, count, axis=1)
+        out.append(lax.ppermute(block, "snap", [(i, i ^ d) for i in range(n)]) if d else block)
+    return out
 
 
 def local(snapshots):
-    gathered = lax.all_to_all(snapshots, "snap", split_axis=1, concat_axis=0, tiled=True)
-    size, cells = gathered.shape
-    root = math.sqrt(cells * lax.axis_size("snap") * lax.axis_size("row"))
-    packed = sum_all(gram(gathered, cells // 4))
-    factor, white = factorize(packed, size, root)
-    return whiten(white, gathered, cells // 8), factor
+    n = lax.axis_size("snap")
+    size, cells = snapshots.shape[0] * n, snapshots.shape[1] // n
+    root = math.sqrt(cells * n * lax.axis_size("row"))
+    places = lax.axis_index("snap") ^ jnp.arange(n, dtype=jnp.int32)
+    tile = cells // 8
+    early = cells - tile
+    first = regroup(snapshots, 0, early)
+    last = regroup(snapshots, early, tile)
+    kept = gram(places, first, cells, 0, tile)
+    packed, hi, lo = gram(places, last, cells, early, tile, kept)
+    factor, white = factorize(sum_all(packed), size, root)
+    return whiten(white, hi, lo, tile), factor
 
 
 def solution(mesh):

time: 278 us -> 294 us (1.058)
  starting transfers between devices: 13 us -> 91.3 us
  waiting for transfers between devices: 211 us -> 142 us
  local copies, waits for them, and re-layouts: 7.77 us -> 14.1 us
    all_to_all x1 -> x0, waiting for transfers between devices: 183 us -> none  [local(): lax.all_to_all(snapshots, 'snap', split_axis=1, concat_axis=0, tiled=True)]
    ppermute x7 -> x21, waiting for transfers between devices: 27.7 us -> 142 us  [the longest x14 114 us: regroup(): lax.ppermute(block, 'snap', [(i, i ^ d) for i in range(n)])]
    ppermute x7 -> x21, starting transfers between devices: 5.79 us -> 91.3 us  [the longest x14 85.7 us: regroup(): lax.ppermute(block, 'snap', [(i, i ^ d) for i in range(n)])]
    dynamic_slice x0 -> x2, local copies, waits for them, and re-layouts: none -> 7.96 us  [regroup(): lax.dynamic_slice_in_dim(snapshots, (me ^ d) * cells + start, count, axis=1)]
    all_to_all x1 -> x0, local copies, waits for them, and re-layouts: 7.77 us -> none  [local(): lax.all_to_all(snapshots, 'snap', split_axis=1, concat_axis=0, tiled=True)]
    all_to_all x1 -> x0, starting transfers between devices: 7.25 us -> none  [local(): lax.all_to_all(snapshots, 'snap', split_axis=1, concat_axis=0, tiled=True)]
    unnamed x0 -> x8, local copies, waits for them, and re-layouts: none -> 6.16 us
    pallas_call x1 -> x2, Pallas kernels: 7.87 us -> 11.4 us  [gram(): pl.pallas_call(functools.partial(gram_kernel, n, not earlier), out_shape=...]
  transfers between devices with their start and end apart: 8 -> 21, of which waited for: 8 -> 11; matrix products, arithmetic and copies ran while one was open for 0% -> 1% of each run, Pallas kernels for 0% -> 3%
where the time goes in v2:
time: 294 us
  waiting for transfers between devices  142 us (48%)
  starting transfers between devices  91.3 us (31%)
  Pallas kernels  45.2 us (15%)
  local copies, waits for them, and re-layouts  14.1 us (5%)
    ppermute x14, waiting for transfers between devices, regroup(): lax.ppermute(block, 'snap', [(i, i ^ d) for i in range(n)])  114 us
    ppermute x14, starting transfers between devices, regroup(): lax.ppermute(block, 'snap', [(i, i ^ d) for i in range(n)])  85.7 us
    ppermute x7, waiting for transfers between devices, step(): return lax.ppermute(x, ('snap', 'row'), pairs)  28.3 us
    pallas_call x1, Pallas kernels, factorize(): pl.pallas_call(functools.partial(factor_kernel, root), out_shape=(out, ou...  25.5 us
    pallas_call x2, Pallas kernels, gram(): pl.pallas_call(functools.partial(gram_kernel, n, not earlier), out_shape=...  11.4 us
    pallas_call x1, Pallas kernels, whiten(): pl.pallas_call(modes_kernel, grid=(cells // tile,), out_shape=jax.ShapeDt...  8.3 us
    dynamic_slice x2, local copies, waits for them, and re-layouts, regroup(): lax.dynamic_slice_in_dim(snapshots, (me ^ d) * cells + start, count, axis=1)  7.96 us
    unnamed x8, local copies, waits for them, and re-layouts  6.16 us
  transfers between devices with their start and end apart: 21, of which 11 were waited for; matrix products, arithmetic and copies ran while one was open for 1% of the time, Pallas kernels for 3%

profile of v2, /device:TPU:0, one launch (start us, length us, event | category | flops | bytes accessed | tf_op | source)
XLA Modules:
  0.0 293.7 jit_solution(16732904100876882473)
XLA Ops:
  0.7 5.9 %constant_dynamic-slice_fusion = (f32[64,3584]{1,0:T(8,128)}, f32[64,3584]{1,0:T(8,128)}, f32[64,3584]{1,0:T(8,128)}, f32[64,3584]{1,0:T(8,128)}, f32[64,3584]{1...) fusion(f32[64,32768]{1,0:T(8,128)} %param.1, s32[]{:T(128)S(6)} %select_n.127, ...), kind=kLoop, calls=%fused_computation.6 | loop fusion | bytes 14680096 | tf_op jit(solution)/shard_map/dynamic_slice | solution.py:287
  6.6 6.0 %collective-permute-start.13 = (f32[64,3584]{1,0:T(8,128)}, f32[64,3584]{1,0:T(8,128)S(1)}, u32[]{:S(2)}, u32[]{:S(2)}) collective-permute-start(f32[64,3584]{1,0:T(8,128)} %get-tuple-element.18), channel_id=1, source_target_pairs={{0,28},{4,24},{8,20},{12,16},{16,12},{20,8},{24,4},{28,0},{1,29},{... | collective-permute-start | bytes 2752520 | tf_op jit(solution)/shard_map/ppermute | solution.py:288
  12.6 0.0 collective-permute-start.11
  12.6 2.1 constant_dynamic-slice_fusion.8
  14.6 2.8 collective-permute-start.6
  17.4 1.3 collective-permute-start.5
  18.8 1.7 collective-permute-start.10
  20.5 36.0 %collective-permute-done.6.refs_8_ = f32[64,512]{1,0:T(8,128)S(1)} collective-permute-done((f32[64,512]{1,0:T(8,128)S(1)}, f32[64,512]{1,0:T(8,128)S(1)}, u32[]{:S(2)}, u32[]{:S(2)}) %collective-permute-start.6) | collective-permute-done | bytes 131104 | tf_op jit(solution)/shard_map/ppermute | solution.py:288
  56.5 65.2 %collective-permute-start.9 = (f32[64,3584]{1,0:T(8,128)}, f32[64,3584]{1,0:T(8,128)}, u32[]{:S(2)}, u32[]{:S(2)}) collective-permute-start(f32[64,3584]{1,0:T(8,128)} %get-tuple-element.21), channel_id=1, source_target_pairs={{0,12},{4,8},{8,4},{12,0},{16,28},{20,24},{24,20},{28,16},{1,13},{... | collective-permute-start | bytes 2752520 | tf_op jit(solution)/shard_map/ppermute | solution.py:288
  121.7 0.0 collective-permute-done.5.refs_7_
  121.7 1.9 collective-permute-start.8
  123.6 0.0 collective-permute-done.13.refs_8_
  123.6 0.6 collective-permute-start.7
  124.3 2.6 collective-permute-start.12
  126.9 16.0 %collective-permute-done.10.refs_5_ = f32[64,3584]{1,0:T(8,128)} collective-permute-done((f32[64,3584]{1,0:T(8,128)}, f32[64,3584]{1,0:T(8,128)}, u32[]{:S(2)}, u32[]{:S(2)}) %collective-permute-start.10) | collective-permute-done | bytes 917536 | tf_op jit(solution)/shard_map/ppermute | solution.py:288
  142.9 0.0 collective-permute-start.4
  142.9 36.5 %collective-permute-done.9.refs_4_ = f32[64,3584]{1,0:T(8,128)} collective-permute-done((f32[64,3584]{1,0:T(8,128)}, f32[64,3584]{1,0:T(8,128)}, u32[]{:S(2)}, u32[]{:S(2)}) %collective-permute-start.9) | collective-permute-done | bytes 917536 | tf_op jit(solution)/shard_map/ppermute | solution.py:288
  179.4 0.0 collective-permute-start.3
  179.4 25.1 %collective-permute-done.8.refs_3_ = f32[64,3584]{1,0:T(8,128)} collective-permute-done((f32[64,3584]{1,0:T(8,128)}, f32[64,3584]{1,0:T(8,128)}, u32[]{:S(2)}, u32[]{:S(2)}) %collective-permute-start.8) | collective-permute-done | bytes 917536 | tf_op jit(solution)/shard_map/ppermute | solution.py:288
  204.5 0.6 collective-permute-start.2
  205.1 2.5 collective-permute-start.1
  207.5 0.4 collective-permute-start
  208.0 9.9 %gram.2 = (f32[1280,128]{1,0:T(8,128)S(1)}, bf16[512,4096]{1,0:T(8,128)(2,1)S(1)}, bf16[512,4096]{1,0:T(8,128)(2,1)S(1)}) custom-call(s32[8]{0:T(128)S(1)} %iota_xor_fusion.refs_0_, f32[64,3584]{1,0:T(8,128)S(1)} %get-tuple-element.24.refs_1_, f32[64,3584]{1,0:T(8,128)} %collective-permute-done.7.refs_2_, f32[64,3584]{1,0:T(8,128)} %collective-permute-done.8.refs_3_, ...), custom_call_target="tpu_custom_call" | custom-call | flops 3758096384 | bytes 14680064 | tf_op jit(solution)/shard_map/gram/pallas_call | solution.py:68
  217.9 0.0 collective-permute-done.4.refs_6_
  217.9 0.0 collective-permute-done.3.refs_5_
  217.9 0.0 collective-permute-done.refs_2_
  217.9 1.5 gram.3
  219.4 0.0 copy-start
  219.4 2.0 copy-done
  221.5 2.0 copy-done.2
  223.4 0.1 collective-permute-start.14
  223.5 0.0 copy-start.1
  223.6 1.6 collective-permute-done.14
  225.2 1.6 collective-permute-start.15
  226.8 3.8 %collective-permute-done.15 = f32[320,128]{1,0:T(8,128)S(1)} collective-permute-done((f32[320,128]{1,0:T(8,128)S(1)}, f32[320,128]{1,0:T(8,128)S(1)}, u32[]{:S(2)}, u32[]{:S(2)}) %collective-permute-start.15) | collective-permute-done | bytes 163872 | tf_op jit(solution)/shard_map/ppermute | solution.py:98
  230.6 1.6 collective-permute-start.16
  232.3 3.7 %collective-permute-done.16 = f32[320,128]{1,0:T(8,128)S(1)} collective-permute-done((f32[320,128]{1,0:T(8,128)S(1)}, f32[320,128]{1,0:T(8,128)S(1)}, u32[]{:S(2)}, u32[]{:S(2)}) %collective-permute-start.16) | collective-permute-done | bytes 163872 | tf_op jit(solution)/shard_map/ppermute | solution.py:98
  236.0 0.2 collective-permute-start.17
  236.2 6.8 %collective-permute-done.17 = f32[320,128]{1,0:T(8,128)S(1)} collective-permute-done((f32[320,128]{1,0:T(8,128)S(1)}, f32[320,128]{1,0:T(8,128)S(1)}, u32[]{:S(2)}, u32[]{:S(2)}) %collective-permute-start.17) | collective-permute-done | bytes 163872 | tf_op jit(solution)/shard_map/ppermute | solution.py:98
  243.0 0.5 collective-permute-start.18
  243.5 7.0 %collective-permute-done.18 = f32[320,128]{1,0:T(8,128)S(1)} collective-permute-done((f32[320,128]{1,0:T(8,128)S(1)}, f32[320,128]{1,0:T(8,128)S(1)}, u32[]{:S(2)}, u32[]{:S(2)}) %collective-permute-start.18) | collective-permute-done | bytes 163872 | tf_op jit(solution)/shard_map/ppermute | solution.py:98
  250.5 1.6 collective-permute-start.19
  252.1 3.8 %collective-permute-done.19 = f32[320,128]{1,0:T(8,128)S(1)} collective-permute-done((f32[320,128]{1,0:T(8,128)S(1)}, f32[320,128]{1,0:T(8,128)S(1)}, u32[]{:S(2)}, u32[]{:S(2)}) %collective-permute-start.19) | collective-permute-done | bytes 163872 | tf_op jit(solution)/shard_map/ppermute | solution.py:98
  255.9 0.1 collective-permute-start.20
  256.0 1.6 collective-permute-done.20
  257.7 25.5 %factor.1 = (f32[512,512]{1,0:T(8,128)}, f32[512,512]{1,0:T(8,128)S(1)}) custom-call(f32[1280,128]{1,0:T(8,128)S(1)} %maximum_select_fusion.gram_ref), custom_call_target="tpu_custom_call" | custom-call | tf_op jit(solution)/shard_map/factor/pallas_call | solution.py:232
  283.2 2.2 copy-done.3
  285.4 8.3 %modes.1 = f32[512,4096]{1,0:T(8,128)} custom-call(f32[512,512]{1,0:T(8,128)S(1)} %get-tuple-element.14.w_ref, bf16[512,4096]{1,0:T(8,128)(2,1)S(1)} %copy-done.1, bf16[512,4096]{1,0:T(8,128)(2,1)S(1)} %copy-done.3), custom_call_target="tpu_custom_call" | custom-call | tf_op jit(solution)/shard_map/modes/pallas_call | solution.py:269
  (18 shorter events, 0.3 us)
Async XLA Ops:
  6.6 117.0 %collective-permute-start.13 = (f32[64,3584]{1,0:T(8,128)}, f32[64,3584]{1,0:T(8,128)S(1)}, u32[]{:S(2)}, u32[]{:S(2)}) collective-permute-start(f32[64,3584]{1,0:T(8,128)} %get-tuple-element.18), channel_id=1, source_target_pairs={{0,28},{4,24},{8,20},{12,16},{16,12},{20,8},{24,4},{28,0},{1,29},{... | collective-permute-start | bytes 2752520 | tf_op jit(solution)/shard_map/ppermute | solution.py:288
  12.6 111.7 %collective-permute-start.11 = (f32[64,3584]{1,0:T(8,128)}, f32[64,3584]{1,0:T(8,128)S(1)}, u32[]{:S(2)}, u32[]{:S(2)}) collective-permute-start(f32[64,3584]{1,0:T(8,128)} %get-tuple-element.19), channel_id=1, source_target_pairs={{0,20},{4,16},{8,28},{12,24},{16,4},{20,0},{24,12},{28,8},{1,21},{... | collective-permute-start | bytes 2752520 | tf_op jit(solution)/shard_map/ppermute | solution.py:288
  14.6 41.9 %collective-permute-start.6 = (f32[64,512]{1,0:T(8,128)S(1)}, f32[64,512]{1,0:T(8,128)S(1)}, u32[]{:S(2)}, u32[]{:S(2)}) collective-permute-start(f32[64,512]{1,0:T(8,128)S(1)} %get-tuple-element.26), channel_id=1, source_target_pairs={{0,28},{4,24},{8,20},{12,16},{16,12},{20,8},{24,4},{28,0},{1,29},{... | collective-permute-start | bytes 393224 | tf_op jit(solution)/shard_map/ppermute | solution.py:288
  17.4 104.3 %collective-permute-start.5 = (f32[64,512]{1,0:T(8,128)S(1)}, f32[64,512]{1,0:T(8,128)S(1)}, u32[]{:S(2)}, u32[]{:S(2)}) collective-permute-start(f32[64,512]{1,0:T(8,128)S(1)} %get-tuple-element.27), channel_id=1, source_target_pairs={{0,24},{4,28},{8,16},{12,20},{16,8},{20,12},{24,0},{28,4},{1,25},{... | collective-permute-start | bytes 393224 | tf_op jit(solution)/shard_map/ppermute | solution.py:288
  18.8 124.1 %collective-permute-start.10 = (f32[64,3584]{1,0:T(8,128)}, f32[64,3584]{1,0:T(8,128)}, u32[]{:S(2)}, u32[]{:S(2)}) collective-permute-start(f32[64,3584]{1,0:T(8,128)} %get-tuple-element.20), channel_id=1, source_target_pairs={{0,16},{4,20},{8,24},{12,28},{16,0},{20,4},{24,8},{28,12},{1,17},{... | collective-permute-start | bytes 2752520 | tf_op jit(solution)/shard_map/ppermute | solution.py:288
  56.5 122.8 %collective-permute-start.9 = (f32[64,3584]{1,0:T(8,128)}, f32[64,3584]{1,0:T(8,128)}, u32[]{:S(2)}, u32[]{:S(2)}) collective-permute-start(f32[64,3584]{1,0:T(8,128)} %get-tuple-element.21), channel_id=1, source_target_pairs={{0,12},{4,8},{8,4},{12,0},{16,28},{20,24},{24,20},{28,16},{1,13},{... | collective-permute-start | bytes 2752520 | tf_op jit(solution)/shard_map/ppermute | solution.py:288
  121.7 82.8 %collective-permute-start.8 = (f32[64,3584]{1,0:T(8,128)}, f32[64,3584]{1,0:T(8,128)}, u32[]{:S(2)}, u32[]{:S(2)}) collective-permute-start(f32[64,3584]{1,0:T(8,128)} %get-tuple-element.22), channel_id=1, source_target_pairs={{0,8},{4,12},{8,0},{12,4},{16,24},{20,28},{24,16},{28,20},{1,9},{5... | collective-permute-start | bytes 2752520 | tf_op jit(solution)/shard_map/ppermute | solution.py:288
  123.6 81.4 %collective-permute-start.7 = (f32[64,3584]{1,0:T(8,128)}, f32[64,3584]{1,0:T(8,128)}, u32[]{:S(2)}, u32[]{:S(2)}) collective-permute-start(f32[64,3584]{1,0:T(8,128)} %get-tuple-element.23), channel_id=1, source_target_pairs={{0,4},{4,0},{8,12},{12,8},{16,20},{20,16},{24,28},{28,24},{1,5},{5... | collective-permute-start | bytes 2752520 | tf_op jit(solution)/shard_map/ppermute | solution.py:288
  124.3 83.3 %collective-permute-start.12 = (f32[64,3584]{1,0:T(8,128)}, f32[64,3584]{1,0:T(8,128)}, u32[]{:S(2)}, u32[]{:S(2)}) collective-permute-start(f32[64,3584]{1,0:T(8,128)} %get-tuple-element.25), channel_id=1, source_target_pairs={{0,24},{4,28},{8,16},{12,20},{16,8},{20,12},{24,0},{28,4},{1,25},{... | collective-permute-start | bytes 2752520 | tf_op jit(solution)/shard_map/ppermute | solution.py:288
  142.9 75.0 %collective-permute-start.4 = (f32[64,512]{1,0:T(8,128)}, f32[64,512]{1,0:T(8,128)S(1)}, u32[]{:S(2)}, u32[]{:S(2)}) collective-permute-start(f32[64,512]{1,0:T(8,128)} %get-tuple-element.28), channel_id=1, source_target_pairs={{0,20},{4,16},{8,28},{12,24},{16,4},{20,0},{24,12},{28,8},{1,21},{... | collective-permute-start | bytes 393224 | tf_op jit(solution)/shard_map/ppermute | solution.py:288
  179.4 38.5 %collective-permute-start.3 = (f32[64,512]{1,0:T(8,128)}, f32[64,512]{1,0:T(8,128)S(1)}, u32[]{:S(2)}, u32[]{:S(2)}) collective-permute-start(f32[64,512]{1,0:T(8,128)} %get-tuple-element.29), channel_id=1, source_target_pairs={{0,16},{4,20},{8,24},{12,28},{16,0},{20,4},{24,8},{28,12},{1,17},{... | collective-permute-start | bytes 393224 | tf_op jit(solution)/shard_map/ppermute | solution.py:288
  204.5 13.4 %collective-permute-start.2 = (f32[64,512]{1,0:T(8,128)S(1)}, f32[64,512]{1,0:T(8,128)S(1)}, u32[]{:S(2)}, u32[]{:S(2)}) collective-permute-start(f32[64,512]{1,0:T(8,128)S(1)} %get-tuple-element.30), channel_id=1, source_target_pairs={{0,12},{4,8},{8,4},{12,0},{16,28},{20,24},{24,20},{28,16},{1,13},{... | collective-permute-start | bytes 393224 | tf_op jit(solution)/shard_map/ppermute | solution.py:288
  205.1 12.8 %collective-permute-start.1 = (f32[64,512]{1,0:T(8,128)S(1)}, f32[64,512]{1,0:T(8,128)S(1)}, u32[]{:S(2)}, u32[]{:S(2)}) collective-permute-start(f32[64,512]{1,0:T(8,128)S(1)} %get-tuple-element.31), channel_id=1, source_target_pairs={{0,8},{4,12},{8,0},{12,4},{16,24},{20,28},{24,16},{28,20},{1,9},{5... | collective-permute-start | bytes 393224 | tf_op jit(solution)/shard_map/ppermute | solution.py:288
  207.5 10.4 %collective-permute-start = (f32[64,512]{1,0:T(8,128)S(1)}, f32[64,512]{1,0:T(8,128)S(1)}, u32[]{:S(2)}, u32[]{:S(2)}) collective-permute-start(f32[64,512]{1,0:T(8,128)S(1)} %get-tuple-element.32), channel_id=1, source_target_pairs={{0,4},{4,0},{8,12},{12,8},{16,20},{20,16},{24,28},{28,24},{1,5},{5... | collective-permute-start | bytes 393224 | tf_op jit(solution)/shard_map/ppermute | solution.py:288
  219.4 2.0 copy-start
  221.5 2.0 copy-start.2
  223.4 1.7 collective-permute-start.14
  223.5 59.6 %copy-start.1 = (bf16[512,4096]{1,0:T(8,128)(2,1)S(1)}, bf16[512,4096]{1,0:T(8,128)(2,1)}, u32[]{:S(2)}) copy-start(bf16[512,4096]{1,0:T(8,128)(2,1)} %copy-done) | copy-start | bytes 12582916
  225.2 5.4 %collective-permute-start.15 = (f32[320,128]{1,0:T(8,128)S(1)}, f32[320,128]{1,0:T(8,128)S(1)}, u32[]{:S(2)}, u32[]{:S(2)}) collective-permute-start(f32[320,128]{1,0:T(8,128)S(1)} %slice_select_fusion.1), channel_id=1, source_target_pairs={{0,2},{4,6},{8,10},{12,14},{16,18},{20,22},{24,26},{28,30},{1,5},{... | collective-permute-start | bytes 491528 | tf_op jit(solution)/shard_map/ppermute | solution.py:98
  230.6 5.4 %collective-permute-start.16 = (f32[320,128]{1,0:T(8,128)S(1)}, f32[320,128]{1,0:T(8,128)S(1)}, u32[]{:S(2)}, u32[]{:S(2)}) collective-permute-start(f32[320,128]{1,0:T(8,128)S(1)} %select_add_fusion.1), channel_id=1, source_target_pairs={{0,4},{4,0},{8,12},{12,8},{16,20},{20,16},{24,28},{28,24},{1,9},{5... | collective-permute-start | bytes 491528 | tf_op jit(solution)/shard_map/ppermute | solution.py:98
  236.0 7.0 %collective-permute-start.17 = (f32[320,128]{1,0:T(8,128)S(1)}, f32[320,128]{1,0:T(8,128)S(1)}, u32[]{:S(2)}, u32[]{:S(2)}) collective-permute-start(f32[320,128]{1,0:T(8,128)S(1)} %add.137), channel_id=1, source_target_pairs={{0,8},{4,12},{8,0},{12,4},{16,24},{20,28},{24,16},{28,20},{1,17},{... | collective-permute-start | bytes 491528 | tf_op jit(solution)/shard_map/ppermute | solution.py:98
  243.0 7.4 %collective-permute-start.18 = (f32[320,128]{1,0:T(8,128)S(1)}, f32[320,128]{1,0:T(8,128)S(1)}, u32[]{:S(2)}, u32[]{:S(2)}) collective-permute-start(f32[320,128]{1,0:T(8,128)S(1)} %add.138), channel_id=1, source_target_pairs={{0,16},{4,20},{8,24},{12,28},{16,0},{20,4},{24,8},{28,12},{1,3},{5... | collective-permute-start | bytes 491528 | tf_op jit(solution)/shard_map/ppermute | solution.py:98
  250.5 5.4 %collective-permute-start.19 = (f32[320,128]{1,0:T(8,128)S(1)}, f32[320,128]{1,0:T(8,128)S(1)}, u32[]{:S(2)}, u32[]{:S(2)}) collective-permute-start(f32[320,128]{1,0:T(8,128)S(1)} %add.139), channel_id=1, source_target_pairs={{0,2},{4,6},{8,10},{12,14},{16,18},{20,22},{24,26},{28,30},{1,5},{... | collective-permute-start | bytes 491528 | tf_op jit(solution)/shard_map/ppermute | solution.py:98
  255.9 1.7 collective-permute-start.20
  283.2 2.2 copy-start.3

commit v3 on v0

v3 whole, which is shorter than its diff:
```python
import functools
import math

import jax
import jax.numpy as jnp
from jax import lax
from jax.experimental import pallas as pl
from jax.experimental.pallas import tpu as pltpu
from jax.sharding import PartitionSpec as P

BLK = 128
SUB = 8
FULL = lax.Precision.HIGHEST
VMEM = pl.BlockSpec(memory_space=pltpu.VMEM)


def lower_blocks(size):
    return [(i, j) for i in range(size // BLK) for j in range(i + 1)]


def split(x):
    hi = x.astype(jnp.bfloat16)
    return hi, (x - hi.astype(jnp.float32)).astype(jnp.bfloat16)


def gram_kernel(count, places_ref, *refs):
    parts, (out_ref, hi_ref, lo_ref) = refs[:count], refs[count:]
    rows, size = parts[0].shape[0], hi_ref.shape[0]
    for d, part in enumerate(parts):
        at = pl.ds(pl.multiple_of(places_ref[d] * rows, rows), rows)
        hi_ref[at, :], lo_ref[at, :] = split(part[...])
    hi = hi_ref[...]
    both = jnp.concatenate([hi, lo_ref[...]], axis=0)
    prod = lax.dot_general(hi, both, (((1,), (1,)), ((), ())), preferred_element_type=jnp.float32)
    for n, (i, j) in enumerate(lower_blocks(size)):
        high = prod[i * BLK : (i + 1) * BLK, j * BLK : (j + 1) * BLK]
        mixed = prod[i * BLK : (i + 1) * BLK, size + j * BLK : size + (j + 1) * BLK]
        other = prod[j * BLK : (j + 1) * BLK, size + i * BLK : size + (i + 1) * BLK]
        out_ref[n * BLK : (n + 1) * BLK, :] = high + mixed + other.T


def gram(places, parts):
    rows, cells = parts[0].shape
    n = len(parts)
    size = rows * n
    kept = jax.ShapeDtypeStruct((size, cells), jnp.bfloat16)
    return pl.pallas_call(
        functools.partial(gram_kernel, n),
        out_shape=(jax.ShapeDtypeStruct((len(lower_blocks(size)) * BLK, BLK), jnp.float32), kept, kept),
        in_specs=[pl.BlockSpec(memory_space=pltpu.SMEM), *[VMEM] * n],
        out_specs=(VMEM, VMEM, VMEM),
        compiler_params=pltpu.CompilerParams(vmem_limit_bytes=48 * 2**20),
        cost_estimate=pl.CostEstimate(flops=4 * size * size * cells, bytes_accessed=8 * size * cells, transcendentals=0),
        name="gram",
    )(places, *parts)


def bits(axis):
    n = lax.axis_size(axis)
    return [1 << b for b in range(n.bit_length() - 1)]


def step(x, orders, at):
    rows, snaps = lax.axis_size("row"), lax.axis_size("snap")
    pairs = []
    for r in range(rows):
        for s in range(snaps):
            axis, bit = orders[r % 2][at]
            to = (r ^ bit, s) if axis == "row" else (r, s ^ bit)
            pairs.append((s * rows + r, to[1] * rows + to[0]))
    return lax.ppermute(x, ("snap", "row"), pairs)


def side(orders, at):
    core = lax.axis_index("row") % 2
    flags = [(lax.axis_index(axis) & bit) > 0 for axis, bit in (o[at] for o in orders)]
    return jnp.where(core == 0, flags[0], flags[1])


def sum_all(x):
    links = [("row", b) for b in bits("row")[1:]] + [("snap", b) for b in bits("snap")]
    orders = [[("row", 1), *links], [("row", 1), *links[1:], links[0]]]
    for at in (0, 1):
        upper = side(orders, at)
        half = x.shape[0] // 2
        first, second = x[:half], x[half:]
        x = jnp.where(upper, second, first) + step(jnp.where(upper, first, second), orders, at)
    for at in range(2, len(links) + 1):
        x = x + step(x, orders, at)
    for at in (1, 0):
        upper = side(orders, at)
        got = step(x, orders, at)
        x = jnp.where(upper, jnp.concatenate([got, x]), jnp.concatenate([x, got]))
    return x


def spread_columns(x, at):
    return [jnp.broadcast_to(x[:, at + j : at + j + 1], (SUB, BLK)) for j in range(SUB)]


def spread_row(x, j):
    return jnp.broadcast_to(x[j : j + 1, :], (SUB, BLK))


def tree_sum(terms):
    while len(terms) > 1:
        terms = [sum(terms[t : t + 2][1:], terms[t]) for t in range(0, len(terms), 2)]
    return terms[0]


def factor_block(rows):
    groups = len(rows)
    part = groups // 2
    lane = lax.broadcasted_iota(jnp.int32, (SUB, BLK), 1)
    sub = lax.broadcasted_iota(jnp.int32, (SUB, BLK), 0)
    rows = list(rows)
    inverse, upper = [], []

    def gather(wide):
        out = wide[0]
        for j in range(1, SUB):
            out = jnp.where(sub == j, wide[j], out)
        return out

    for k in range(groups):
        base = SUB * k
        end = (k // part + 1) * part
        near = k + 1 < end
        if k % part == 0:
            if k:
                top = jnp.concatenate(inverse[k - part : k], axis=0)
                right = jnp.concatenate(upper[k - part : k], axis=0)
                full = jnp.where(lax.broadcasted_iota(jnp.int32, top.shape, 1) < base, top, right)
                rest = lax.dot_general(
                    right[:, base:], full, (((0,), (0,)), ((), ())), precision=FULL, preferred_element_type=jnp.float32
                )
                for i in range(k, groups):
                    old = jnp.where((lane >= base - SUB * part) & (lane < base), 0.0, rows[i])
                    rows[i] = old - rest[SUB * (i - k) : SUB * (i - k + 1), :]
            spread = spread_columns(rows[k], base)
        if near:
            below = spread_columns(rows[k + 1], base)
            beyond = spread_columns(rows[k + 1], base + SUB)
        cell = {(i, j): spread_row(spread[j], i) for i in range(SUB) for j in range(i + 1)}
        in_block = (lane >= base) & (lane < base + SUB)
        up = [spread_row(rows[k], j) for j in range(SUB)]
        aug = [jnp.where(in_block, jnp.where(lane == base + j, 1.0, 0.0), up[j]) for j in range(SUB)]
        inv, ratio = [], {}
        for j in range(SUB):
            inv.append(pl.reciprocal(cell[j, j], approx=True))
            for i in range(j + 1, SUB):
                ratio[i, j] = cell[i, j] * inv[j]
            for i in range(j + 1, SUB):
                for c in range(j + 1, i + 1):
                    cell[i, c] = cell[i, c] - ratio[i, j] * cell[c, j]

        def eliminate(cols):
            cols = list(cols)
            for j in range(SUB):
                for c in range(j + 1, SUB):
                    cols[c] = cols[c] - cols[j] * ratio[c, j]
            return cols

        def update(i, m):
            rows[i] = jnp.where(in_block, 0.0, rows[i]) - tree_sum([m[j] * aug[j] for j in range(SUB)])

        if near:
            below = eliminate(below)
            m = [below[j] * inv[j] for j in range(SUB)]
            spread = [
                beyond[c] - tree_sum([m[j] * spread_row(below[j], c) for j in range(SUB)]) for c in range(SUB)
            ]
        aug, up = eliminate(aug), eliminate(up)
        if near:
            update(k + 1, m)
        for i in range(k + 2, end):
            cols = eliminate(spread_columns(rows[i], base))
            update(i, [cols[j] * inv[j] for j in range(SUB)])
        scale = lax.rsqrt(gather([cell[j, j] for j in range(SUB)]))
        inverse.append(jnp.where(lane <= base + sub, gather(aug) * scale, 0.0))
        upper.append(jnp.where(lane >= base + sub, gather(up) * scale, 0.0))
    return inverse, upper


def factor_kernel(root, gram_ref, lower_ref, white_ref, work, xs, us):
    size = lower_ref.shape[0]
    blocks = size // BLK
    for n, (i, j) in enumerate(lower_blocks(size)):
        block = gram_ref[n * BLK : (n + 1) * BLK, :]
        work[i * BLK : (i + 1) * BLK, j * BLK : (j + 1) * BLK] = block
        if i != j:
            work[j * BLK : (j + 1) * BLK, i * BLK : (i + 1) * BLK] = block.T
    eye = jnp.where(
        lax.broadcasted_iota(jnp.int32, (BLK, BLK), 0) == lax.broadcasted_iota(jnp.int32, (BLK, BLK), 1), 1.0, 0.0
    )
    zero = jnp.zeros((BLK, BLK), jnp.float32)
    for b in range(blocks):
        here = slice(b * BLK, (b + 1) * BLK)
        inverse, upper = factor_block([work[b * BLK + SUB * i : b * BLK + SUB * (i + 1), here] for i in range(BLK // SUB)])
        for k in range(BLK // SUB):
            xs[SUB * k : SUB * (k + 1), :] = inverse[k]
            us[SUB * k : SUB * (k + 1), :] = upper[k]
        work[here, here] = eye
        y = jnp.dot(xs[...], work[here, :], precision=FULL, preferred_element_type=jnp.float32)
        for i in range(b + 1, blocks):
            down = slice(i * BLK, (i + 1) * BLK)
            left = y[:, down].T
            work[down, here] = zero
            work[down, :] = work[down, :] - jnp.dot(left, y, precision=FULL, preferred_element_type=jnp.float32)
            lower_ref[down, here] = left * (1.0 / root)
            lower_ref[here, down] = zero
            white_ref[here, down] = zero
        lower_ref[here, here] = us[...].T * (1.0 / root)
        white_ref[here, : (b + 1) * BLK] = y[:, : (b + 1) * BLK] * root


def factorize(packed, size, root):
    out = jax.ShapeDtypeStruct((size, size), jnp.float32)
    return pl.pallas_call(
        functools.partial(factor_kernel, root),
        out_shape=(out, out),
        in_specs=[VMEM],
        out_specs=(VMEM, VMEM),
        scratch_shapes=[
            pltpu.VMEM((size, size), jnp.float32),
            pltpu.VMEM((BLK, BLK), jnp.float32),
            pltpu.VMEM((BLK, BLK), jnp.float32),
        ],
        compiler_params=pltpu.CompilerParams(vmem_limit_bytes=48 * 2**20),
        name="factor",
    )(packed)


def modes_kernel(w_ref, hi_ref, lo_ref, out_ref, w_hi, w_lo, tiles, sems):
    size, cells = hi_ref.shape
    slots, _, tile = tiles.shape
    half = size // 2
    w_hi[...], w_lo[...] = split(w_ref[...])
    copies = []
    for t in range(cells // tile):
        slot, here = t % slots, slice(t * tile, (t + 1) * tile)
        if t >= slots:
            copies[t - slots].wait()
        for out, depth in ((slice(0, half), half), (slice(half, size), size)):
            a, b = w_hi[out, :depth], w_lo[out, :depth]
            hi, lo = hi_ref[:depth, here], lo_ref[:depth, here]
            tiles[slot, out, :] = (
                jnp.dot(a, hi, preferred_element_type=jnp.float32)
                + jnp.dot(a, lo, preferred_element_type=jnp.float32)
                + jnp.dot(b, hi, preferred_element_type=jnp.float32)
            )
        copies.append(pltpu.make_async_copy(tiles.at[slot], out_ref.at[:, here], sems.at[slot]))
        copies[t].start()
    for copy in copies[-slots:]:
        copy.wait()


def whiten(w, hi, lo, tile, slots):
    size, cells = hi.shape
    return pl.pallas_call(
        modes_kernel,
        out_shape=jax.ShapeDtypeStruct((size, cells), jnp.float32),
        in_specs=[VMEM, VMEM, VMEM],
        out_specs=pl.BlockSpec(memory_space=pl.ANY),
        scratch_shapes=[
            pltpu.VMEM((size, size), jnp.bfloat16),
            pltpu.VMEM((size, size), jnp.bfloat16),
            pltpu.VMEM((slots, size, tile), jnp.float32),
            pltpu.SemaphoreType.DMA((slots,)),
        ],
        compiler_params=pltpu.CompilerParams(vmem_limit_bytes=48 * 2**20),
        name="modes",
    )(w, hi, lo)


def regroup(snapshots):
    n = lax.axis_size("snap")
    me = lax.axis_index("snap")
    cells = snapshots.shape[1] // n
    order = sorted(range(n), key=lambda d: (d < n // 2, (d ^ (n // 4)) if d >= n // 2 else -d))
    parts = []
    for d in order:
        block = lax.dynamic_slice_in_dim(snapshots, (me ^ d) * cells, cells, axis=1)
        parts.append(lax.ppermute(block, "snap", [(i, i ^ d) for i in range(n)]) if d else block)
    return order, parts


def local(snapshots):
    n = lax.axis_size("snap")
    size, cells = snapshots.shape[0] * n, snapshots.shape[1] // n
    root = math.sqrt(cells * n * lax.axis_size("row"))
    order, parts = regroup(snapshots)
    places = lax.axis_index("snap") ^ jnp.array(order, dtype=jnp.int32)
    packed, hi, lo = gram(places, parts)
    factor, white = factorize(sum_all(packed), size, root)
    return whiten(white, hi, lo, cells // 8, 4), factor


def solution(mesh):
    in_specs = (P("snap", "row"),)
    out_specs = (P(None, ("row", "snap")), P())
    return jax.shard_map(local, mesh=mesh, in_specs=in_specs, out_specs=out_specs, check_vma=False)
```

time: 536 us -> 261 us (0.49)
  waiting for transfers between devices: 306 us -> 153 us
  other arithmetic: 126 us -> 0.26 us
  starting transfers between devices: 7.29 us -> 67.4 us
  matrix products: 43.3 us -> 0 us
  Pallas kernels: 0 us -> 33.9 us
  local copies, waits for them, and re-layouts: 32 us -> 5.87 us
  between operations: 17 us -> 0.95 us
    all_to_all x1 -> x0, waiting for transfers between devices: 183 us -> none  [local(): lax.all_to_all(snapshots, 'snap', split_axis=1, concat_axis=0, tiled=True)]
    ppermute x0 -> x14, waiting for transfers between devices: none -> 153 us  [the longest x7 130 us: regroup(): lax.ppermute(block, 'snap', [(i, i ^ d) for i in range(n)])]
    psum x1 -> x0, waiting for transfers between devices: 123 us -> none  [local(): full_gram = lax.psum(local_gram, ('snap', 'row'))]
    another operation x16 -> x0, other arithmetic: 119 us -> none  [the longest x14 79 us: local(): factor_full = jnp.linalg.cholesky(full_gram)]
    ppermute x0 -> x14, starting transfers between devices: none -> 67.4 us  [the longest x7 53.2 us: step(): return lax.ppermute(x, ('snap', 'row'), pairs)]
    pallas_call x0 -> x3, Pallas kernels: none -> 33.9 us  [the longest x1 14.9 us: factorize(): pl.pallas_call(functools.partial(factor_kernel, root), out_shape=(out, ou...]
    another operation x13 -> x0, matrix products: 25.9 us -> none  [the longest x7 20.4 us: local(): jax.scipy.linalg.solve_triangular(factor_full, gathered, lower=True)]
    another operation x18 -> x0, local copies, waits for them, and re-layouts: 20.6 us -> none
  transfers between devices with their start and end apart: 2 -> 14, of which waited for: 2 -> 10; matrix products, arithmetic and copies ran while one was open for 1% -> 0% of each run, Pallas kernels for 0% -> 0%
where the time goes in v3:
time: 261 us
  waiting for transfers between devices  153 us (59%)
  starting transfers between devices  67.4 us (26%)
  Pallas kernels  33.9 us (13%)
  local copies, waits for them, and re-layouts  5.87 us (2%)
    ppermute x7, waiting for transfers between devices, regroup(): lax.ppermute(block, 'snap', [(i, i ^ d) for i in range(n)])  130 us
    ppermute x7, starting transfers between devices, step(): return lax.ppermute(x, ('snap', 'row'), pairs)  53.2 us
    ppermute x7, waiting for transfers between devices, step(): return lax.ppermute(x, ('snap', 'row'), pairs)  23 us
    pallas_call x1, Pallas kernels, factorize(): pl.pallas_call(functools.partial(factor_kernel, root), out_shape=(out, ou...  14.9 us
    ppermute x7, starting transfers between devices, regroup(): lax.ppermute(block, 'snap', [(i, i ^ d) for i in range(n)])  14.2 us
    pallas_call x1, Pallas kernels, gram(): pl.pallas_call(functools.partial(gram_kernel, n), out_shape=(jax.ShapeDty...  10 us
    pallas_call x1, Pallas kernels, whiten(): pl.pallas_call(modes_kernel, out_shape=jax.ShapeDtypeStruct((size, cells)...  8.92 us
    dynamic_slice x1, local copies, waits for them, and re-layouts, regroup(): block = lax.dynamic_slice_in_dim(snapshots, (me ^ d) * cells, cells, axis=1)  5.85 us
  transfers between devices with their start and end apart: 14, of which 10 were waited for; matrix products, arithmetic and copies ran while one was open for 0% of the time, Pallas kernels for 0%

profile of v3, /device:TPU:0, one launch (start us, length us, event | category | flops | bytes accessed | tf_op | source)
XLA Modules:
  0.0 260.9 jit_solution(8771423574608861479)
XLA Ops:
  0.7 0.0 copy-start.2
  0.7 5.8 %constant_dynamic-slice_fusion = (f32[64,4096]{1,0:T(8,128)}, f32[64,4096]{1,0:T(8,128)S(1)}, f32[64,4096]{1,0:T(8,128)S(1)}, f32[64,4096]{1,0:T(8,128)}, f32[64...) fusion(f32[64,32768]{1,0:T(8,128)} %param.2, s32[]{:T(128)S(6)} %select_n.95, ...), kind=kLoop, calls=%fused_computation.6 | loop fusion | bytes 16777248 | tf_op jit(solution)/shard_map/dynamic_slice | solution.py:283
  6.5 3.0 %collective-permute-start.5 = (f32[64,4096]{1,0:T(8,128)S(1)}, f32[64,4096]{1,0:T(8,128)S(1)}, u32[]{:S(2)}, u32[]{:S(2)}) collective-permute-start(f32[64,4096]{1,0:T(8,128)S(1)} %get-tuple-element.13), channel_id=1, source_target_pairs={{0,8},{4,12},{8,0},{12,4},{16,24},{20,28},{24,16},{28,20},{1,9},{5... | collective-permute-start | bytes 3145736 | tf_op jit(solution)/shard_map/ppermute | solution.py:284
  9.6 1.4 collective-permute-start.4
  10.9 2.6 collective-permute-start.3
  13.5 0.0 collective-permute-start.2
  13.5 4.8 %collective-permute-start.1 = (f32[64,4096]{1,0:T(8,128)}, f32[64,4096]{1,0:T(8,128)}, u32[]{:S(2)}, u32[]{:S(2)}) collective-permute-start(f32[64,4096]{1,0:T(8,128)} %get-tuple-element.17), channel_id=1, source_target_pairs={{0,28},{4,24},{8,20},{12,16},{16,12},{20,8},{24,4},{28,0},{1,29},{... | collective-permute-start | bytes 3145736 | tf_op jit(solution)/shard_map/ppermute | solution.py:284
  18.4 58.7 %collective-permute-done.5.refs_5_ = f32[64,4096]{1,0:T(8,128)S(1)} collective-permute-done((f32[64,4096]{1,0:T(8,128)S(1)}, f32[64,4096]{1,0:T(8,128)S(1)}, u32[]{:S(2)}, u32[]{:S(2)}) %collective-permute-start.5) | collective-permute-done | bytes 1048608 | tf_op jit(solution)/shard_map/ppermute | solution.py:284
  77.1 0.0 copy-start.1
  77.1 1.8 collective-permute-start
  78.9 20.7 %collective-permute-done.4.refs_4_ = f32[64,4096]{1,0:T(8,128)S(1)} collective-permute-done((f32[64,4096]{1,0:T(8,128)S(1)}, f32[64,4096]{1,0:T(8,128)S(1)}, u32[]{:S(2)}, u32[]{:S(2)}) %collective-permute-start.4) | collective-permute-done | bytes 1048608 | tf_op jit(solution)/shard_map/ppermute | solution.py:284
  99.7 0.0 copy-done.1
  99.7 0.5 collective-permute-start.6
  100.2 0.0 copy-done.2
  100.2 0.0 collective-permute-done.3.refs_3_
  100.2 50.1 %collective-permute-done.2.refs_2_ = f32[64,4096]{1,0:T(8,128)} collective-permute-done((f32[64,4096]{1,0:T(8,128)}, f32[64,4096]{1,0:T(8,128)}, u32[]{:S(2)}, u32[]{:S(2)}) %collective-permute-start.2) | collective-permute-done | bytes 1048608 | tf_op jit(solution)/shard_map/ppermute | solution.py:284
  150.3 0.0 collective-permute-done.1.refs_1_
  150.3 0.0 collective-permute-done.refs_0_
  150.3 0.0 collective-permute-done.6.refs_6_
  150.3 10.0 %gram.1 = (f32[1280,128]{1,0:T(8,128)S(1)}, bf16[512,4096]{1,0:T(8,128)(2,1)}, bf16[512,4096]{1,0:T(8,128)(2,1)}) custom-call(s32[8]{0:T(128)S(1)} %broadcast_xor_fusion.places_ref, f32[64,4096]{1,0:T(8,128)} %collective-permute-done.refs_0_, f32[64,4096]{1,0:T(8,128)} %collective-permute-done.1.refs_1_, f32[64,4096]{1,0:T(8,128)} %collective-permute-done.2.refs_2_, ...), custom_call_target="tpu_custom_call" | custom-call | flops 4294967296 | bytes 16777216 | tf_op jit(solution)/shard_map/gram/pallas_call | solution.py:47
  160.3 0.1 collective-permute-start.7
  160.4 0.0 copy-start
  160.4 1.6 collective-permute-done.7
  162.1 1.9 collective-permute-start.8
  164.0 3.5 %collective-permute-done.8 = f32[320,128]{1,0:T(8,128)S(1)} collective-permute-done((f32[320,128]{1,0:T(8,128)S(1)}, f32[320,128]{1,0:T(8,128)S(1)}, u32[]{:S(2)}, u32[]{:S(2)}) %collective-permute-start.8) | collective-permute-done | bytes 163872 | tf_op jit(solution)/shard_map/ppermute | solution.py:71
  167.5 1.9 collective-permute-start.9
  169.4 3.5 %collective-permute-done.9 = f32[320,128]{1,0:T(8,128)S(1)} collective-permute-done((f32[320,128]{1,0:T(8,128)S(1)}, f32[320,128]{1,0:T(8,128)S(1)}, u32[]{:S(2)}, u32[]{:S(2)}) %collective-permute-start.9) | collective-permute-done | bytes 163872 | tf_op jit(solution)/shard_map/ppermute | solution.py:71
  172.9 44.4 %collective-permute-start.10 = (f32[320,128]{1,0:T(8,128)S(1)}, f32[320,128]{1,0:T(8,128)S(1)}, u32[]{:S(2)}, u32[]{:S(2)}) collective-permute-start(f32[320,128]{1,0:T(8,128)S(1)} %add.57), channel_id=1, source_target_pairs={{0,8},{4,12},{8,0},{12,4},{16,24},{20,28},{24,16},{28,20},{1,17},{... | collective-permute-start | bytes 491528 | tf_op jit(solution)/shard_map/ppermute | solution.py:71
  217.3 4.0 %collective-permute-done.10 = f32[320,128]{1,0:T(8,128)S(1)} collective-permute-done((f32[320,128]{1,0:T(8,128)S(1)}, f32[320,128]{1,0:T(8,128)S(1)}, u32[]{:S(2)}, u32[]{:S(2)}) %collective-permute-start.10) | collective-permute-done | bytes 163872 | tf_op jit(solution)/shard_map/ppermute | solution.py:71
  221.3 3.3 %collective-permute-start.11 = (f32[320,128]{1,0:T(8,128)S(1)}, f32[320,128]{1,0:T(8,128)S(1)}, u32[]{:S(2)}, u32[]{:S(2)}) collective-permute-start(f32[320,128]{1,0:T(8,128)S(1)} %add.58), channel_id=1, source_target_pairs={{0,16},{4,20},{8,24},{12,28},{16,0},{20,4},{24,8},{28,12},{1,3},{5... | collective-permute-start | bytes 491528 | tf_op jit(solution)/shard_map/ppermute | solution.py:71
  224.6 5.1 %collective-permute-done.11 = f32[320,128]{1,0:T(8,128)S(1)} collective-permute-done((f32[320,128]{1,0:T(8,128)S(1)}, f32[320,128]{1,0:T(8,128)S(1)}, u32[]{:S(2)}, u32[]{:S(2)}) %collective-permute-start.11) | collective-permute-done | bytes 163872 | tf_op jit(solution)/shard_map/ppermute | solution.py:71
  229.7 1.6 collective-permute-start.12
  231.3 3.8 %collective-permute-done.12 = f32[320,128]{1,0:T(8,128)S(1)} collective-permute-done((f32[320,128]{1,0:T(8,128)S(1)}, f32[320,128]{1,0:T(8,128)S(1)}, u32[]{:S(2)}, u32[]{:S(2)}) %collective-permute-start.12) | collective-permute-done | bytes 163872 | tf_op jit(solution)/shard_map/ppermute | solution.py:71
  235.1 0.1 collective-permute-start.13
  235.2 1.6 collective-permute-done.13
  236.9 14.9 %factor.1 = (f32[512,512]{1,0:T(8,128)}, f32[512,512]{1,0:T(8,128)S(1)}) custom-call(f32[1280,128]{1,0:T(8,128)S(1)} %maximum_select_fusion.gram_ref), custom_call_target="tpu_custom_call" | custom-call | tf_op jit(solution)/shard_map/factor/pallas_call | solution.py:219
  251.8 0.0 copy-done
  251.8 8.9 %modes.1 = f32[512,4096]{1,0:T(8,128)} custom-call(f32[512,512]{1,0:T(8,128)S(1)} %get-tuple-element.8.w_ref, bf16[512,4096]{1,0:T(8,128)(2,1)S(1)} %copy-done, bf16[512,4096]{1,0:T(8,128)(2,1)} %get-tuple-element.10.lo_ref), custom_call_target="tpu_custom_call" | custom-call | tf_op jit(solution)/shard_map/modes/pallas_call | solution.py:260
  (10 shorter events, 0.3 us)
Async XLA Ops:
  0.7 99.5 %copy-start.2 = (s32[8]{0:T(128)S(1)}, s32[8]{0:T(128)}, u32[]{:S(2)}) copy-start(s32[8]{0:T(128)} %constant.46.clone) | copy-start | bytes 100
  6.5 70.6 %collective-permute-start.5 = (f32[64,4096]{1,0:T(8,128)S(1)}, f32[64,4096]{1,0:T(8,128)S(1)}, u32[]{:S(2)}, u32[]{:S(2)}) collective-permute-start(f32[64,4096]{1,0:T(8,128)S(1)} %get-tuple-element.13), channel_id=1, source_target_pairs={{0,8},{4,12},{8,0},{12,4},{16,24},{20,28},{24,16},{28,20},{1,9},{5... | collective-permute-start | bytes 3145736 | tf_op jit(solution)/shard_map/ppermute | solution.py:284
  9.6 90.1 %collective-permute-start.4 = (f32[64,4096]{1,0:T(8,128)S(1)}, f32[64,4096]{1,0:T(8,128)S(1)}, u32[]{:S(2)}, u32[]{:S(2)}) collective-permute-start(f32[64,4096]{1,0:T(8,128)S(1)} %get-tuple-element.14), channel_id=1, source_target_pairs={{0,12},{4,8},{8,4},{12,0},{16,28},{20,24},{24,20},{28,16},{1,13},{... | collective-permute-start | bytes 3145736 | tf_op jit(solution)/shard_map/ppermute | solution.py:284
  10.9 89.3 %collective-permute-start.3 = (f32[64,4096]{1,0:T(8,128)}, f32[64,4096]{1,0:T(8,128)S(1)}, u32[]{:S(2)}, u32[]{:S(2)}) collective-permute-start(f32[64,4096]{1,0:T(8,128)} %get-tuple-element.15), channel_id=1, source_target_pairs={{0,20},{4,16},{8,28},{12,24},{16,4},{20,0},{24,12},{28,8},{1,21},{... | collective-permute-start | bytes 3145736 | tf_op jit(solution)/shard_map/ppermute | solution.py:284
  13.5 136.8 %collective-permute-start.2 = (f32[64,4096]{1,0:T(8,128)}, f32[64,4096]{1,0:T(8,128)}, u32[]{:S(2)}, u32[]{:S(2)}) collective-permute-start(f32[64,4096]{1,0:T(8,128)} %get-tuple-element.16), channel_id=1, source_target_pairs={{0,16},{4,20},{8,24},{12,28},{16,0},{20,4},{24,8},{28,12},{1,17},{... | collective-permute-start | bytes 3145736 | tf_op jit(solution)/shard_map/ppermute | solution.py:284
  13.5 136.7 %collective-permute-start.1 = (f32[64,4096]{1,0:T(8,128)}, f32[64,4096]{1,0:T(8,128)}, u32[]{:S(2)}, u32[]{:S(2)}) collective-permute-start(f32[64,4096]{1,0:T(8,128)} %get-tuple-element.17), channel_id=1, source_target_pairs={{0,28},{4,24},{8,20},{12,16},{16,12},{20,8},{24,4},{28,0},{1,29},{... | collective-permute-start | bytes 3145736 | tf_op jit(solution)/shard_map/ppermute | solution.py:284
  77.1 22.6 %copy-start.1 = (f32[64,4096]{1,0:T(8,128)}, f32[64,4096]{1,0:T(8,128)S(1)}, u32[]{:S(2)}) copy-start(f32[64,4096]{1,0:T(8,128)S(1)} %collective-permute-done.5.refs_5_) | copy-start | bytes 3145732
  77.1 73.2 %collective-permute-start = (f32[64,4096]{1,0:T(8,128)}, f32[64,4096]{1,0:T(8,128)}, u32[]{:S(2)}, u32[]{:S(2)}) collective-permute-start(f32[64,4096]{1,0:T(8,128)} %get-tuple-element.18), channel_id=1, source_target_pairs={{0,24},{4,28},{8,16},{12,20},{16,8},{20,12},{24,0},{28,4},{1,25},{... | collective-permute-start | bytes 3145736 | tf_op jit(solution)/shard_map/ppermute | solution.py:284
  99.7 50.6 %collective-permute-start.6 = (f32[64,4096]{1,0:T(8,128)S(1)}, f32[64,4096]{1,0:T(8,128)}, u32[]{:S(2)}, u32[]{:S(2)}) collective-permute-start(f32[64,4096]{1,0:T(8,128)S(1)} %get-tuple-element.19), channel_id=1, source_target_pairs={{0,4},{4,0},{8,12},{12,8},{16,20},{20,16},{24,28},{28,24},{1,5},{5... | collective-permute-start | bytes 3145736 | tf_op jit(solution)/shard_map/ppermute | solution.py:284
  160.3 1.7 collective-permute-start.7
  160.4 91.4 %copy-start = (bf16[512,4096]{1,0:T(8,128)(2,1)S(1)}, bf16[512,4096]{1,0:T(8,128)(2,1)}, u32[]{:S(2)}) copy-start(bf16[512,4096]{1,0:T(8,128)(2,1)} %get-tuple-element.9.hi_ref) | copy-start | bytes 12582916
  162.1 5.4 %collective-permute-start.8 = (f32[320,128]{1,0:T(8,128)S(1)}, f32[320,128]{1,0:T(8,128)S(1)}, u32[]{:S(2)}, u32[]{:S(2)}) collective-permute-start(f32[320,128]{1,0:T(8,128)S(1)} %slice_select_fusion.1), channel_id=1, source_target_pairs={{0,2},{4,6},{8,10},{12,14},{16,18},{20,22},{24,26},{28,30},{1,5},{... | collective-permute-start | bytes 491528 | tf_op jit(solution)/shard_map/ppermute | solution.py:71
  167.5 5.4 %collective-permute-start.9 = (f32[320,128]{1,0:T(8,128)S(1)}, f32[320,128]{1,0:T(8,128)S(1)}, u32[]{:S(2)}, u32[]{:S(2)}) collective-permute-start(f32[320,128]{1,0:T(8,128)S(1)} %select_add_fusion.1), channel_id=1, source_target_pairs={{0,4},{4,0},{8,12},{12,8},{16,20},{20,16},{24,28},{28,24},{1,9},{5... | collective-permute-start | bytes 491528 | tf_op jit(solution)/shard_map/ppermute | solution.py:71
  172.9 48.4 %collective-permute-start.10 = (f32[320,128]{1,0:T(8,128)S(1)}, f32[320,128]{1,0:T(8,128)S(1)}, u32[]{:S(2)}, u32[]{:S(2)}) collective-permute-start(f32[320,128]{1,0:T(8,128)S(1)} %add.57), channel_id=1, source_target_pairs={{0,8},{4,12},{8,0},{12,4},{16,24},{20,28},{24,16},{28,20},{1,17},{... | collective-permute-start | bytes 491528 | tf_op jit(solution)/shard_map/ppermute | solution.py:71
  221.3 8.4 %collective-permute-start.11 = (f32[320,128]{1,0:T(8,128)S(1)}, f32[320,128]{1,0:T(8,128)S(1)}, u32[]{:S(2)}, u32[]{:S(2)}) collective-permute-start(f32[320,128]{1,0:T(8,128)S(1)} %add.58), channel_id=1, source_target_pairs={{0,16},{4,20},{8,24},{12,28},{16,0},{20,4},{24,8},{28,12},{1,3},{5... | collective-permute-start | bytes 491528 | tf_op jit(solution)/shard_map/ppermute | solution.py:71
  229.7 5.4 %collective-permute-start.12 = (f32[320,128]{1,0:T(8,128)S(1)}, f32[320,128]{1,0:T(8,128)S(1)}, u32[]{:S(2)}, u32[]{:S(2)}) collective-permute-start(f32[320,128]{1,0:T(8,128)S(1)} %add.59), channel_id=1, source_target_pairs={{0,2},{4,6},{8,10},{12,14},{16,18},{20,22},{24,26},{28,30},{1,5},{... | collective-permute-start | bytes 491528 | tf_op jit(solution)/shard_map/ppermute | solution.py:71
  235.1 1.7 collective-permute-start.13

commit v4 on v3

--- a/solution.py
+++ b/solution.py
@@ -12,6 +12,8 @@
 SUB = 8
 FULL = lax.Precision.HIGHEST
 VMEM = pl.BlockSpec(memory_space=pltpu.VMEM)
+ANY = pl.BlockSpec(memory_space=pl.ANY)
+SMEM = pl.BlockSpec(memory_space=pltpu.SMEM)
 
 
 def lower_blocks(size):
@@ -23,36 +25,91 @@
     return hi, (x - hi.astype(jnp.float32)).astype(jnp.bfloat16)
 
 
-def gram_kernel(count, places_ref, *refs):
-    parts, (out_ref, hi_ref, lo_ref) = refs[:count], refs[count:]
-    rows, size = parts[0].shape[0], hi_ref.shape[0]
-    for d, part in enumerate(parts):
-        at = pl.ds(pl.multiple_of(places_ref[d] * rows, rows), rows)
-        hi_ref[at, :], lo_ref[at, :] = split(part[...])
-    hi = hi_ref[...]
-    both = jnp.concatenate([hi, lo_ref[...]], axis=0)
-    prod = lax.dot_general(hi, both, (((1,), (1,)), ((), ())), preferred_element_type=jnp.float32)
+def nt(a, b):
+    return lax.dot_general(a, b, (((1,), (1,)), ((), ())), preferred_element_type=jnp.float32)
+
+
+def gram_kernel(count, tile, places_ref, *refs):
+    parts, (out_ref, hi_ref, lo_ref, hi_out, lo_out, acc, sems) = refs[:count], refs[count:]
+    rows, cells = parts[0].shape
+    size = hi_ref.shape[0]
+    stores = []
+    for t in range(cells // tile):
+        here = slice(t * tile, (t + 1) * tile)
+        for d in range(count + 1):
+            at = pl.ds(pl.multiple_of(places_ref[d] * rows, rows), rows)
+            if d < count:
+                hi_ref[at, here], lo_ref[at, here] = split(parts[d][:, here])
+            else:
+                hi_ref[at, here] = lo_ref[at, here] = jnp.zeros((rows, tile), jnp.bfloat16)
+        for ref, out in ((hi_ref, hi_out), (lo_ref, lo_out)):
+            stores.append(pltpu.make_async_copy(ref.at[:, here], out.at[:, here], sems.at[len(stores)]))
+            stores[-1].start()
+        hi = hi_ref[:, here]
+        prod = nt(hi, jnp.concatenate([hi, lo_ref[:, here]], axis=0))
+        acc[...] = acc[...] + prod if t else prod
     for n, (i, j) in enumerate(lower_blocks(size)):
-        high = prod[i * BLK : (i + 1) * BLK, j * BLK : (j + 1) * BLK]
-        mixed = prod[i * BLK : (i + 1) * BLK, size + j * BLK : size + (j + 1) * BLK]
-        other = prod[j * BLK : (j + 1) * BLK, size + i * BLK : size + (i + 1) * BLK]
+        high = acc[i * BLK : (i + 1) * BLK, j * BLK : (j + 1) * BLK]
+        mixed = acc[i * BLK : (i + 1) * BLK, size + j * BLK : size + (j + 1) * BLK]
+        other = acc[j * BLK : (j + 1) * BLK, size + i * BLK : size + (i + 1) * BLK]
         out_ref[n * BLK : (n + 1) * BLK, :] = high + mixed + other.T
-
-
-def gram(places, parts):
+    for store in stores:
+        store.wait()
+
+
+def gram(places, parts, tile):
     rows, cells = parts[0].shape
     n = len(parts)
-    size = rows * n
+    size = rows * (n + 1)
     kept = jax.ShapeDtypeStruct((size, cells), jnp.bfloat16)
     return pl.pallas_call(
-        functools.partial(gram_kernel, n),
-        out_shape=(jax.ShapeDtypeStruct((len(lower_blocks(size)) * BLK, BLK), jnp.float32), kept, kept),
-        in_specs=[pl.BlockSpec(memory_space=pltpu.SMEM), *[VMEM] * n],
-        out_specs=(VMEM, VMEM, VMEM),
-        compiler_params=pltpu.CompilerParams(vmem_limit_bytes=48 * 2**20),
+        functools.partial(gram_kernel, n, tile),
+        out_shape=(jax.ShapeDtypeStruct((len(lower_blocks(size)) * BLK, BLK), jnp.float32), *[kept] * 4),
+        in_specs=[SMEM, *[VMEM] * n],
+        out_specs=(VMEM, VMEM, VMEM, ANY, ANY),
+        scratch_shapes=[pltpu.VMEM((size, 2 * size), jnp.float32), pltpu.SemaphoreType.DMA((2 * (cells // tile),))],
+        compiler_params=pltpu.CompilerParams(vmem_limit_bytes=32 * 2**20),
         cost_estimate=pl.CostEstimate(flops=4 * size * size * cells, bytes_accessed=8 * size * cells, transcendentals=0),
         name="gram",
     )(places, *parts)
+
+
+def last_kernel(places_ref, before_ref, part_ref, hi_ref, lo_ref, out_ref, hi_last, lo_last, wide):
+    rows = part_ref.shape[0]
+    size = hi_ref.shape[0]
+    place = places_ref[places_ref.shape[0] - 1]
+    at = pl.ds(pl.multiple_of(place * rows, rows), rows)
+    hi, lo = hi_last[...], lo_last[...] = split(part_ref[...])
+    both = jnp.concatenate([hi, lo], axis=0)
+    cross = nt(hi_ref[...], both)
+    cross = cross[:, :rows] + cross[:, rows:] + nt(lo_ref[...], hi)
+    square = nt(hi, both)
+    square = square[:, :rows] * 0.5 + square[:, rows:]
+    wide[...] = jnp.zeros_like(wide)
+    lane = lax.broadcasted_iota(jnp.int32, (rows, size), 1)
+    inside = (lane >= place * rows) & (lane < (place + 1) * rows)
+    square = jnp.concatenate([square] * (size // rows), axis=1)
+    wide[at, :] = cross.T + jnp.where(inside, square, 0.0)
+    for n, (i, j) in enumerate(lower_blocks(size)):
+        down = wide[i * BLK : (i + 1) * BLK, j * BLK : (j + 1) * BLK]
+        across = wide[j * BLK : (j + 1) * BLK, i * BLK : (i + 1) * BLK]
+        out_ref[n * BLK : (n + 1) * BLK, :] = before_ref[n * BLK : (n + 1) * BLK, :] + (down + across.T)
+
+
+def add_last(places, before, part, hi, lo):
+    rows, cells = part.shape
+    size = hi.shape[0]
+    kept = jax.ShapeDtypeStruct((rows, cells), jnp.bfloat16)
+    return pl.pallas_call(
+        last_kernel,
+        out_shape=(jax.ShapeDtypeStruct(before.shape, jnp.float32), kept, kept),
+        in_specs=[SMEM, VMEM, VMEM, VMEM, VMEM],
+        out_specs=(VMEM, VMEM, VMEM),
+        scratch_shapes=[pltpu.VMEM((size, size), jnp.float32)],
+        compiler_params=pltpu.CompilerParams(vmem_limit_bytes=16 * 2**20),
+        cost_estimate=pl.CostEstimate(flops=6 * rows * size * cells, bytes_accessed=4 * size * cells, transcendentals=0),
+        name="gram_last",
+    )(places, before, part, hi, lo)
 
 
 def bits(axis):
@@ -226,24 +283,29 @@
             pltpu.VMEM((BLK, BLK), jnp.float32),
             pltpu.VMEM((BLK, BLK), jnp.float32),
         ],
-        compiler_params=pltpu.CompilerParams(vmem_limit_bytes=48 * 2**20),
+        compiler_params=pltpu.CompilerParams(vmem_limit_bytes=12 * 2**20),
+        cost_estimate=pl.CostEstimate(flops=100 * size**3, bytes_accessed=8 * size * size, transcendentals=size),
         name="factor",
     )(packed)
 
 
-def modes_kernel(w_ref, hi_ref, lo_ref, out_ref, w_hi, w_lo, tiles, sems):
+def modes_kernel(places_ref, w_ref, hi_ref, lo_ref, hi_last, lo_last, out_ref, w_hi, w_lo, s_hi, s_lo, tiles, sems):
     size, cells = hi_ref.shape
+    rows = hi_last.shape[0]
     slots, _, tile = tiles.shape
     half = size // 2
+    at = pl.ds(pl.multiple_of(places_ref[places_ref.shape[0] - 1] * rows, rows), rows)
     w_hi[...], w_lo[...] = split(w_ref[...])
     copies = []
     for t in range(cells // tile):
         slot, here = t % slots, slice(t * tile, (t + 1) * tile)
+        s_hi[t % 2], s_lo[t % 2] = hi_ref[:, here], lo_ref[:, here]
+        s_hi[t % 2, at, :], s_lo[t % 2, at, :] = hi_last[:, here], lo_last[:, here]
         if t >= slots:
             copies[t - slots].wait()
         for out, depth in ((slice(0, half), half), (slice(half, size), size)):
             a, b = w_hi[out, :depth], w_lo[out, :depth]
-            hi, lo = hi_ref[:depth, here], lo_ref[:depth, here]
+            hi, lo = s_hi[t % 2, :depth, :], s_lo[t % 2, :depth, :]
             tiles[slot, out, :] = (
                 jnp.dot(a, hi, preferred_element_type=jnp.float32)
                 + jnp.dot(a, lo, preferred_element_type=jnp.float32)
@@ -255,45 +317,48 @@
         copy.wait()
 
 
-def whiten(w, hi, lo, tile, slots):
+def whiten(places, w, hi, lo, hi_last, lo_last, tile, slots):
     size, cells = hi.shape
     return pl.pallas_call(
         modes_kernel,
         out_shape=jax.ShapeDtypeStruct((size, cells), jnp.float32),
-        in_specs=[VMEM, VMEM, VMEM],
-        out_specs=pl.BlockSpec(memory_space=pl.ANY),
+        in_specs=[SMEM, *[VMEM] * 5],
+        out_specs=ANY,
         scratch_shapes=[
             pltpu.VMEM((size, size), jnp.bfloat16),
             pltpu.VMEM((size, size), jnp.bfloat16),
+            pltpu.VMEM((2, size, tile), jnp.bfloat16),
+            pltpu.VMEM((2, size, tile), jnp.bfloat16),
             pltpu.VMEM((slots, size, tile), jnp.float32),
             pltpu.SemaphoreType.DMA((slots,)),
         ],
-        compiler_params=pltpu.CompilerParams(vmem_limit_bytes=48 * 2**20),
+        compiler_params=pltpu.CompilerParams(vmem_limit_bytes=16 * 2**20),
         name="modes",
-    )(w, hi, lo)
+    )(places, w, hi, lo, hi_last, lo_last)
 
 
 def regroup(snapshots):
     n = lax.axis_size("snap")
     me = lax.axis_index("snap")
     cells = snapshots.shape[1] // n
-    order = sorted(range(n), key=lambda d: (d < n // 2, (d ^ (n // 4)) if d >= n // 2 else -d))
-    parts = []
-    for d in order:
+    end = n // 2 + n // 4
+    got = {}
+    for d in sorted(range(n), key=lambda d: (d < n // 2, (d ^ (n // 4)) if d >= n // 2 else -d)):
         block = lax.dynamic_slice_in_dim(snapshots, (me ^ d) * cells, cells, axis=1)
-        parts.append(lax.ppermute(block, "snap", [(i, i ^ d) for i in range(n)]) if d else block)
-    return order, parts
+        got[d] = lax.ppermute(block, "snap", [(i, i ^ d) for i in range(n)]) if d else block
+    order = [d for d in range(n) if d != end] + [end]
+    return me ^ jnp.array(order, dtype=jnp.int32), [got[d] for d in order]
 
 
 def local(snapshots):
     n = lax.axis_size("snap")
     size, cells = snapshots.shape[0] * n, snapshots.shape[1] // n
     root = math.sqrt(cells * n * lax.axis_size("row"))
-    order, parts = regroup(snapshots)
-    places = lax.axis_index("snap") ^ jnp.array(order, dtype=jnp.int32)
-    packed, hi, lo = gram(places, parts)
+    places, parts = regroup(snapshots)
+    packed, hi, lo, hi_kept, lo_kept = gram(places, parts[:-1], cells // 8)
+    packed, hi_last, lo_last = add_last(places, packed, parts[-1], hi, lo)
     factor, white = factorize(sum_all(packed), size, root)
-    return whiten(white, hi, lo, cells // 8, 4), factor
+    return whiten(places, white, hi_kept, lo_kept, hi_last, lo_last, cells // 8, 4), factor
 
 
 def solution(mesh):

time: 261 us -> 252 us (0.966)
  waiting for transfers between devices: 153 us -> 138 us
    ppermute x7, waiting for transfers between devices: 130 us -> 115 us  [regroup(): lax.ppermute(block, 'snap', [(i, i ^ d) for i in range(n)])]
    pallas_call x1 -> x2, Pallas kernels: 10 us -> 12.7 us  [the longest x1 9.11 us: gram(): pl.pallas_call(functools.partial(gram_kernel, n, tile), out_shape=(jax.Sh...]
  transfers between devices with their start and end apart: 14 -> 14, of which waited for: 10 -> 11; matrix products, arithmetic and copies ran while one was open for 0% -> 0% of each run, Pallas kernels for 0% -> 4%
where the time goes in v4:
time: 252 us
  waiting for transfers between devices  138 us (55%)
  starting transfers between devices  68.3 us (27%)
  Pallas kernels  35.6 us (14%)
  local copies, waits for them, and re-layouts  8.15 us (3%)
    ppermute x7, waiting for transfers between devices, regroup(): lax.ppermute(block, 'snap', [(i, i ^ d) for i in range(n)])  115 us
    ppermute x7, starting transfers between devices, step(): return lax.ppermute(x, ('snap', 'row'), pairs)  53.3 us
    ppermute x7, waiting for transfers between devices, step(): return lax.ppermute(x, ('snap', 'row'), pairs)  23 us
    ppermute x7, starting transfers between devices, regroup(): lax.ppermute(block, 'snap', [(i, i ^ d) for i in range(n)])  15 us
    pallas_call x1, Pallas kernels, factorize(): pl.pallas_call(functools.partial(factor_kernel, root), out_shape=(out, ou...  15 us
    pallas_call x1, Pallas kernels, gram(): pl.pallas_call(functools.partial(gram_kernel, n, tile), out_shape=(jax.Sh...  9.11 us
    pallas_call x1, Pallas kernels, whiten(): pl.pallas_call(modes_kernel, out_shape=jax.ShapeDtypeStruct((size, cells)...  7.83 us
    dynamic_slice x1, local copies, waits for them, and re-layouts, regroup(): block = lax.dynamic_slice_in_dim(snapshots, (me ^ d) * cells, cells, axis=1)  5.85 us
  transfers between devices with their start and end apart: 14, of which 11 were waited for; matrix products, arithmetic and copies ran while one was open for 0% of the time, Pallas kernels for 4%

profile of v4, /device:TPU:0, one launch (start us, length us, event | category | flops | bytes accessed | tf_op | source)
XLA Modules:
  0.0 251.7 jit_solution(4147175015901249594)
XLA Ops:
  0.7 0.0 copy-start.5
  0.7 5.8 %constant_dynamic-slice_fusion = (f32[64,4096]{1,0:T(8,128)}, f32[64,4096]{1,0:T(8,128)S(1)}, f32[64,4096]{1,0:T(8,128)S(1)}, f32[64,4096]{1,0:T(8,128)}, f32[64...) fusion(f32[64,32768]{1,0:T(8,128)} %param.2, s32[]{:T(128)S(6)} %select_n.95, ...), kind=kLoop, calls=%fused_computation.6 | loop fusion | bytes 16777248 | tf_op jit(solution)/shard_map/dynamic_slice | solution.py:347
  6.5 5.0 %collective-permute-start.4 = (f32[64,4096]{1,0:T(8,128)S(1)}, f32[64,4096]{1,0:T(8,128)S(1)}, u32[]{:S(2)}, u32[]{:S(2)}) collective-permute-start(f32[64,4096]{1,0:T(8,128)S(1)} %get-tuple-element.23), channel_id=1, source_target_pairs={{0,20},{4,16},{8,28},{12,24},{16,4},{20,0},{24,12},{28,8},{1,21},{... | collective-permute-start | bytes 3145736 | tf_op jit(solution)/shard_map/ppermute | solution.py:348
  11.5 0.3 collective-permute-start.3
  11.8 1.5 collective-permute-start.2
  13.4 0.1 collective-permute-start.1
  13.5 1.8 collective-permute-start
  15.3 65.2 %collective-permute-done.4.refs_5_ = f32[64,4096]{1,0:T(8,128)S(1)} collective-permute-done((f32[64,4096]{1,0:T(8,128)S(1)}, f32[64,4096]{1,0:T(8,128)S(1)}, u32[]{:S(2)}, u32[]{:S(2)}) %collective-permute-start.4) | collective-permute-done | bytes 1048608 | tf_op jit(solution)/shard_map/ppermute | solution.py:348
  80.5 3.7 %collective-permute-start.5 = (f32[64,4096]{1,0:T(8,128)}, f32[64,4096]{1,0:T(8,128)}, u32[]{:S(2)}, u32[]{:S(2)}) collective-permute-start(f32[64,4096]{1,0:T(8,128)} %get-tuple-element.29), channel_id=1, source_target_pairs={{0,28},{4,24},{8,20},{12,16},{16,12},{20,8},{24,4},{28,0},{1,29},{... | collective-permute-start | bytes 3145736 | tf_op jit(solution)/shard_map/ppermute | solution.py:348
  84.2 20.2 %collective-permute-done.3.refs_4_ = f32[64,4096]{1,0:T(8,128)S(1)} collective-permute-done((f32[64,4096]{1,0:T(8,128)S(1)}, f32[64,4096]{1,0:T(8,128)S(1)}, u32[]{:S(2)}, u32[]{:S(2)}) %collective-permute-start.3) | collective-permute-done | bytes 1048608 | tf_op jit(solution)/shard_map/ppermute | solution.py:348
  104.4 0.0 copy-start.3
  104.4 1.1 copy-done.3
  105.5 2.5 collective-permute-start.6
  108.0 0.0 copy-done.5
  108.0 0.0 collective-permute-done.2.refs_3_
  108.0 0.0 collective-permute-done.1.refs_2_
  108.0 0.0 collective-permute-done.refs_1_
  108.0 19.1 %collective-permute-done.5.refs_6_ = f32[64,4096]{1,0:T(8,128)} collective-permute-done((f32[64,4096]{1,0:T(8,128)}, f32[64,4096]{1,0:T(8,128)}, u32[]{:S(2)}, u32[]{:S(2)}) %collective-permute-start.5) | collective-permute-done | bytes 1048608 | tf_op jit(solution)/shard_map/ppermute | solution.py:348
  127.1 0.0 copy-start.4
  127.1 1.2 copy-done.4
  128.3 9.1 %gram.1 = (f32[1280,128]{1,0:T(8,128)S(1)}, bf16[512,4096]{1,0:T(8,128)(2,1)S(1)}, bf16[512,4096]{1,0:T(8,128)(2,1)S(1)}, bf16[512,4096]{1,0:T(8,128)(2,1)S(1)}, bf16[512,4096]{1,0:T(8,128)(2,1)}) custom-call(s32[8]{0:T(128)S(1)} %broadcast_xor_fusion.places_ref, f32[64,4096]{1,0:T(8,128)S(1)} %get-tuple-element.28.refs_0_, ...), custom_call_target="tpu_custom_call" | custom-call | flops 4294967296 | bytes 16777216 | tf_op jit(solution)/shard_map/gram/pallas_call | solution.py:65
  137.4 0.0 copy-start
  137.4 10.9 %collective-permute-done.6.part_ref = f32[64,4096]{1,0:T(8,128)S(1)} collective-permute-done((f32[64,4096]{1,0:T(8,128)}, f32[64,4096]{1,0:T(8,128)S(1)}, u32[]{:S(2)}, u32[]{:S(2)}) %collective-permute-start.6) | collective-permute-done | bytes 1048608 | tf_op jit(solution)/shard_map/ppermute | solution.py:348
  148.3 3.6 %gram_last.1 = (f32[1280,128]{1,0:T(8,128)S(1)}, bf16[64,4096]{1,0:T(8,128)(2,1)S(1)}, bf16[64,4096]{1,0:T(8,128)(2,1)S(1)}) custom-call(s32[8]{0:T(128)S(1)} %broadcast_xor_fusion.places_ref, f32[1280,128]{1,0:T(8,128)S(1)} %get-tuple-element.12.before_ref, f32[64,4096]{1,0:T(8,128)S(1)} %collective-permute-done.6.part_ref, ...), custom_call_target="tpu_custom_call" | custom-call | flops 805306368 | bytes 8388608 | tf_op jit(solution)/shard_map/gram_last/pallas_call | solution.py:103
  152.0 0.0 copy-done
  152.0 0.1 collective-permute-start.7
  152.1 1.6 collective-permute-done.7
  153.8 1.6 collective-permute-start.8
  155.4 3.8 %collective-permute-done.8 = f32[320,128]{1,0:T(8,128)S(1)} collective-permute-done((f32[320,128]{1,0:T(8,128)S(1)}, f32[320,128]{1,0:T(8,128)S(1)}, u32[]{:S(2)}, u32[]{:S(2)}) %collective-permute-start.8) | collective-permute-done | bytes 163872 | tf_op jit(solution)/shard_map/ppermute | solution.py:128
  159.2 11.3 %collective-permute-start.9 = (f32[320,128]{1,0:T(8,128)S(1)}, f32[320,128]{1,0:T(8,128)S(1)}, u32[]{:S(2)}, u32[]{:S(2)}) collective-permute-start(f32[320,128]{1,0:T(8,128)S(1)} %select_add_fusion.1), channel_id=1, source_target_pairs={{0,4},{4,0},{8,12},{12,8},{16,20},{20,16},{24,28},{28,24},{1,9},{5... | collective-permute-start | bytes 491528 | tf_op jit(solution)/shard_map/ppermute | solution.py:128
  170.5 3.3 %collective-permute-done.9 = f32[320,128]{1,0:T(8,128)S(1)} collective-permute-done((f32[320,128]{1,0:T(8,128)S(1)}, f32[320,128]{1,0:T(8,128)S(1)}, u32[]{:S(2)}, u32[]{:S(2)}) %collective-permute-start.9) | collective-permute-done | bytes 163872 | tf_op jit(solution)/shard_map/ppermute | solution.py:128
  173.9 35.3 %collective-permute-start.10 = (f32[320,128]{1,0:T(8,128)S(1)}, f32[320,128]{1,0:T(8,128)S(1)}, u32[]{:S(2)}, u32[]{:S(2)}) collective-permute-start(f32[320,128]{1,0:T(8,128)S(1)} %add.57), channel_id=1, source_target_pairs={{0,8},{4,12},{8,0},{12,4},{16,24},{20,28},{24,16},{28,20},{1,17},{... | collective-permute-start | bytes 491528 | tf_op jit(solution)/shard_map/ppermute | solution.py:128
  209.2 3.9 %collective-permute-done.10 = f32[320,128]{1,0:T(8,128)S(1)} collective-permute-done((f32[320,128]{1,0:T(8,128)S(1)}, f32[320,128]{1,0:T(8,128)S(1)}, u32[]{:S(2)}, u32[]{:S(2)}) %collective-permute-start.10) | collective-permute-done | bytes 163872 | tf_op jit(solution)/shard_map/ppermute | solution.py:128
  213.1 3.3 %collective-permute-start.11 = (f32[320,128]{1,0:T(8,128)S(1)}, f32[320,128]{1,0:T(8,128)S(1)}, u32[]{:S(2)}, u32[]{:S(2)}) collective-permute-start(f32[320,128]{1,0:T(8,128)S(1)} %add.58), channel_id=1, source_target_pairs={{0,16},{4,20},{8,24},{12,28},{16,0},{20,4},{24,8},{28,12},{1,3},{5... | collective-permute-start | bytes 491528 | tf_op jit(solution)/shard_map/ppermute | solution.py:128
  216.4 5.1 %collective-permute-done.11 = f32[320,128]{1,0:T(8,128)S(1)} collective-permute-done((f32[320,128]{1,0:T(8,128)S(1)}, f32[320,128]{1,0:T(8,128)S(1)}, u32[]{:S(2)}, u32[]{:S(2)}) %collective-permute-start.11) | collective-permute-done | bytes 163872 | tf_op jit(solution)/shard_map/ppermute | solution.py:128
  221.5 1.6 collective-permute-start.12
  223.1 3.8 %collective-permute-done.12 = f32[320,128]{1,0:T(8,128)S(1)} collective-permute-done((f32[320,128]{1,0:T(8,128)S(1)}, f32[320,128]{1,0:T(8,128)S(1)}, u32[]{:S(2)}, u32[]{:S(2)}) %collective-permute-start.12) | collective-permute-done | bytes 163872 | tf_op jit(solution)/shard_map/ppermute | solution.py:128
  226.9 0.1 collective-permute-start.13
  227.0 1.6 collective-permute-done.13
  228.6 0.0 copy-start.1
  228.6 0.0 copy-start.2
  228.7 15.0 %factor.1 = (f32[512,512]{1,0:T(8,128)}, f32[512,512]{1,0:T(8,128)S(1)}) custom-call(f32[1280,128]{1,0:T(8,128)S(1)} %maximum_select_fusion.gram_ref), custom_call_target="tpu_custom_call" | custom-call | flops 13421772800 | bytes 2097152 | tf_op jit(solution)/shard_map/factor/pallas_call | solution.py:276
  243.6 0.0 copy-done.1
  243.6 0.0 copy-done.2
  243.6 7.8 %modes.1 = f32[512,4096]{1,0:T(8,128)} custom-call(s32[8]{0:T(128)S(1)} %broadcast_xor_fusion.places_ref, f32[512,512]{1,0:T(8,128)S(1)} %get-tuple-element.16.w_ref, bf16[512,4096]{1,0:T(8,128)(2,1)S(1)} %copy-done.1, bf16[512,4096]{1,0:T(8,128)(2,1)S(1)} %copy-done.2, bf16[64,4096]{1,0:T(8,128)(2,1)S(1)} %get-tuple-element.19.hi_last, ...), custom_call_target="tpu_custom_call" | custom-call | tf_op jit(solution)/shard_map/modes/pallas_call | solution.py:322
  (10 shorter events, 0.3 us)
Async XLA Ops:
  0.7 107.3 %copy-start.5 = (s32[8]{0:T(128)S(1)}, s32[8]{0:T(128)}, u32[]{:S(2)}) copy-start(s32[8]{0:T(128)} %constant.46.clone) | copy-start | bytes 100
  6.5 74.0 %collective-permute-start.4 = (f32[64,4096]{1,0:T(8,128)S(1)}, f32[64,4096]{1,0:T(8,128)S(1)}, u32[]{:S(2)}, u32[]{:S(2)}) collective-permute-start(f32[64,4096]{1,0:T(8,128)S(1)} %get-tuple-element.23), channel_id=1, source_target_pairs={{0,20},{4,16},{8,28},{12,24},{16,4},{20,0},{24,12},{28,8},{1,21},{... | collective-permute-start | bytes 3145736 | tf_op jit(solution)/shard_map/ppermute | solution.py:348
  11.5 92.9 %collective-permute-start.3 = (f32[64,4096]{1,0:T(8,128)S(1)}, f32[64,4096]{1,0:T(8,128)S(1)}, u32[]{:S(2)}, u32[]{:S(2)}) collective-permute-start(f32[64,4096]{1,0:T(8,128)S(1)} %get-tuple-element.24), channel_id=1, source_target_pairs={{0,16},{4,20},{8,24},{12,28},{16,0},{20,4},{24,8},{28,12},{1,17},{... | collective-permute-start | bytes 3145736 | tf_op jit(solution)/shard_map/ppermute | solution.py:348
  11.8 96.1 %collective-permute-start.2 = (f32[64,4096]{1,0:T(8,128)}, f32[64,4096]{1,0:T(8,128)}, u32[]{:S(2)}, u32[]{:S(2)}) collective-permute-start(f32[64,4096]{1,0:T(8,128)} %get-tuple-element.25), channel_id=1, source_target_pairs={{0,12},{4,8},{8,4},{12,0},{16,28},{20,24},{24,20},{28,16},{1,13},{... | collective-permute-start | bytes 3145736 | tf_op jit(solution)/shard_map/ppermute | solution.py:348
  13.4 94.6 %collective-permute-start.1 = (f32[64,4096]{1,0:T(8,128)}, f32[64,4096]{1,0:T(8,128)}, u32[]{:S(2)}, u32[]{:S(2)}) collective-permute-start(f32[64,4096]{1,0:T(8,128)} %get-tuple-element.26), channel_id=1, source_target_pairs={{0,8},{4,12},{8,0},{12,4},{16,24},{20,28},{24,16},{28,20},{1,9},{5... | collective-permute-start | bytes 3145736 | tf_op jit(solution)/shard_map/ppermute | solution.py:348
  13.5 94.5 %collective-permute-start = (f32[64,4096]{1,0:T(8,128)}, f32[64,4096]{1,0:T(8,128)}, u32[]{:S(2)}, u32[]{:S(2)}) collective-permute-start(f32[64,4096]{1,0:T(8,128)} %get-tuple-element.27), channel_id=1, source_target_pairs={{0,4},{4,0},{8,12},{12,8},{16,20},{20,16},{24,28},{28,24},{1,5},{5... | collective-permute-start | bytes 3145736 | tf_op jit(solution)/shard_map/ppermute | solution.py:348
  80.5 46.5 %collective-permute-start.5 = (f32[64,4096]{1,0:T(8,128)}, f32[64,4096]{1,0:T(8,128)}, u32[]{:S(2)}, u32[]{:S(2)}) collective-permute-start(f32[64,4096]{1,0:T(8,128)} %get-tuple-element.29), channel_id=1, source_target_pairs={{0,28},{4,24},{8,20},{12,16},{16,12},{20,8},{24,4},{28,0},{1,29},{... | collective-permute-start | bytes 3145736 | tf_op jit(solution)/shard_map/ppermute | solution.py:348
  104.4 1.1 copy-start.3
  105.5 42.8 %collective-permute-start.6 = (f32[64,4096]{1,0:T(8,128)}, f32[64,4096]{1,0:T(8,128)S(1)}, u32[]{:S(2)}, u32[]{:S(2)}) collective-permute-start(f32[64,4096]{1,0:T(8,128)} %get-tuple-element.22), channel_id=1, source_target_pairs={{0,24},{4,28},{8,16},{12,20},{16,8},{20,12},{24,0},{28,4},{1,25},{... | collective-permute-start | bytes 3145736 | tf_op jit(solution)/shard_map/ppermute | solution.py:348
  127.1 1.2 copy-start.4
  137.4 14.5 %copy-start = (bf16[512,4096]{1,0:T(8,128)(2,1)}, bf16[512,4096]{1,0:T(8,128)(2,1)S(1)}, u32[]{:S(2)}) copy-start(bf16[512,4096]{1,0:T(8,128)(2,1)S(1)} %get-tuple-element.17.hi_ref) | copy-start | bytes 12582916
  152.0 1.7 collective-permute-start.7
  153.8 5.4 %collective-permute-start.8 = (f32[320,128]{1,0:T(8,128)S(1)}, f32[320,128]{1,0:T(8,128)S(1)}, u32[]{:S(2)}, u32[]{:S(2)}) collective-permute-start(f32[320,128]{1,0:T(8,128)S(1)} %slice_select_fusion.1), channel_id=1, source_target_pairs={{0,2},{4,6},{8,10},{12,14},{16,18},{20,22},{24,26},{28,30},{1,5},{... | collective-permute-start | bytes 491528 | tf_op jit(solution)/shard_map/ppermute | solution.py:128
  159.2 14.6 %collective-permute-start.9 = (f32[320,128]{1,0:T(8,128)S(1)}, f32[320,128]{1,0:T(8,128)S(1)}, u32[]{:S(2)}, u32[]{:S(2)}) collective-permute-start(f32[320,128]{1,0:T(8,128)S(1)} %select_add_fusion.1), channel_id=1, source_target_pairs={{0,4},{4,0},{8,12},{12,8},{16,20},{20,16},{24,28},{28,24},{1,9},{5... | collective-permute-start | bytes 491528 | tf_op jit(solution)/shard_map/ppermute | solution.py:128
  173.9 39.2 %collective-permute-start.10 = (f32[320,128]{1,0:T(8,128)S(1)}, f32[320,128]{1,0:T(8,128)S(1)}, u32[]{:S(2)}, u32[]{:S(2)}) collective-permute-start(f32[320,128]{1,0:T(8,128)S(1)} %add.57), channel_id=1, source_target_pairs={{0,8},{4,12},{8,0},{12,4},{16,24},{20,28},{24,16},{28,20},{1,17},{... | collective-permute-start | bytes 491528 | tf_op jit(solution)/shard_map/ppermute | solution.py:128
  213.1 8.4 %collective-permute-start.11 = (f32[320,128]{1,0:T(8,128)S(1)}, f32[320,128]{1,0:T(8,128)S(1)}, u32[]{:S(2)}, u32[]{:S(2)}) collective-permute-start(f32[320,128]{1,0:T(8,128)S(1)} %add.58), channel_id=1, source_target_pairs={{0,16},{4,20},{8,24},{12,28},{16,0},{20,4},{24,8},{28,12},{1,3},{5... | collective-permute-start | bytes 491528 | tf_op jit(solution)/shard_map/ppermute | solution.py:128
  221.5 5.4 %collective-permute-start.12 = (f32[320,128]{1,0:T(8,128)S(1)}, f32[320,128]{1,0:T(8,128)S(1)}, u32[]{:S(2)}, u32[]{:S(2)}) collective-permute-start(f32[320,128]{1,0:T(8,128)S(1)} %add.59), channel_id=1, source_target_pairs={{0,2},{4,6},{8,10},{12,14},{16,18},{20,22},{24,26},{28,30},{1,5},{... | collective-permute-start | bytes 491528 | tf_op jit(solution)/shard_map/ppermute | solution.py:128
  226.9 1.7 collective-permute-start.13
  228.6 15.0 %copy-start.1 = (bf16[512,4096]{1,0:T(8,128)(2,1)S(1)}, bf16[512,4096]{1,0:T(8,128)(2,1)}, u32[]{:S(2)}) copy-start(bf16[512,4096]{1,0:T(8,128)(2,1)} %copy-done) | copy-start | bytes 12582916
  228.6 15.0 %copy-start.2 = (bf16[512,4096]{1,0:T(8,128)(2,1)S(1)}, bf16[512,4096]{1,0:T(8,128)(2,1)}, u32[]{:S(2)}) copy-start(bf16[512,4096]{1,0:T(8,128)(2,1)} %get-tuple-element.18.lo_ref) | copy-start | bytes 12582916

commit v5 on v4

--- a/solution.py
+++ b/solution.py
@@ -337,14 +337,50 @@
     )(places, w, hi, lo, hi_last, lo_last)
 
 
+def cut_kernel(place_ref, x_ref, out_ref, held, come, go):
+    rows, cells = held.shape
+    at = pl.ds(pl.multiple_of(place_ref[0] * cells, cells), cells)
+    pieces = [slice(SUB * n, SUB * (n + 1)) for n in range(rows // SUB)]
+    loads = [pltpu.make_async_copy(x_ref.at[p, at], held.at[p, :], come.at[n]) for n, p in enumerate(pieces)]
+    stores = [pltpu.make_async_copy(held.at[p, :], out_ref.at[p, :], go.at[n]) for n, p in enumerate(pieces)]
+    for load in loads:
+        load.start()
+    for load, store in zip(loads, stores, strict=True):
+        load.wait()
+        store.start()
+    for store in stores:
+        store.wait()
+
+
+def cut(place, x, cells):
+    rows = x.shape[0]
+    return pl.pallas_call(
+        cut_kernel,
+        out_shape=jax.ShapeDtypeStruct((rows, cells), x.dtype),
+        in_specs=[SMEM, ANY],
+        out_specs=ANY,
+        scratch_shapes=[
+            pltpu.VMEM((rows, cells), x.dtype),
+            pltpu.SemaphoreType.DMA((rows // SUB,)),
+            pltpu.SemaphoreType.DMA((rows // SUB,)),
+        ],
+        compiler_params=pltpu.CompilerParams(vmem_limit_bytes=60 * 2**20),
+        name="cut",
+    )(place[None], x)
+
+
 def regroup(snapshots):
     n = lax.axis_size("snap")
     me = lax.axis_index("snap")
     cells = snapshots.shape[1] // n
-    end = n // 2 + n // 4
+    begin, end = n // 2 + 1, n // 2 + n // 4
+    far = [d for d in reversed(range(n // 2, n)) if d not in (begin, end)]
     got = {}
-    for d in sorted(range(n), key=lambda d: (d < n // 2, (d ^ (n // 4)) if d >= n // 2 else -d)):
-        block = lax.dynamic_slice_in_dim(snapshots, (me ^ d) * cells, cells, axis=1)
+    for d in [end, *range(1, n // 2), *far, begin, 0]:
+        if d == begin:
+            block = cut(me ^ d, snapshots, cells)
+        else:
+            block = lax.dynamic_slice_in_dim(snapshots, (me ^ d) * cells, cells, axis=1)
         got[d] = lax.ppermute(block, "snap", [(i, i ^ d) for i in range(n)]) if d else block
     order = [d for d in range(n) if d != end] + [end]
     return me ^ jnp.array(order, dtype=jnp.int32), [got[d] for d in order]

time: 252 us -> 248 us (0.984)
  starting transfers between devices: 68.3 us -> 52.6 us
  waiting for transfers between devices: 138 us -> 149 us
    ppermute x7, starting transfers between devices: 53.3 us -> 37.5 us  [step(): return lax.ppermute(x, ('snap', 'row'), pairs)]
    ppermute x7, waiting for transfers between devices: 115 us -> 125 us  [regroup(): lax.ppermute(block, 'snap', [(i, i ^ d) for i in range(n)])]
  transfers between devices with their start and end apart: 14 -> 14, of which waited for: 11 -> 10; matrix products, arithmetic and copies ran while one was open for 0% -> 2% of each run, Pallas kernels for 4% -> 4%
where the time goes in v5:
time: 248 us
  waiting for transfers between devices  149 us (60%)
  starting transfers between devices  52.6 us (21%)
  Pallas kernels  37.6 us (15%)
  local copies, waits for them, and re-layouts  7.85 us (3%)
    ppermute x7, waiting for transfers between devices, regroup(): lax.ppermute(block, 'snap', [(i, i ^ d) for i in range(n)])  125 us
    ppermute x7, starting transfers between devices, step(): return lax.ppermute(x, ('snap', 'row'), pairs)  37.5 us
    ppermute x7, waiting for transfers between devices, step(): return lax.ppermute(x, ('snap', 'row'), pairs)  23.6 us
    ppermute x7, starting transfers between devices, regroup(): lax.ppermute(block, 'snap', [(i, i ^ d) for i in range(n)])  15.1 us
    pallas_call x1, Pallas kernels, factorize(): pl.pallas_call(functools.partial(factor_kernel, root), out_shape=(out, ou...  15 us
    pallas_call x1, Pallas kernels, gram(): pl.pallas_call(functools.partial(gram_kernel, n, tile), out_shape=(jax.Sh...  9.1 us
    pallas_call x1, Pallas kernels, whiten(): pl.pallas_call(modes_kernel, out_shape=jax.ShapeDtypeStruct((size, cells)...  7.8 us
    dynamic_slice x1, local copies, waits for them, and re-layouts, regroup(): block = lax.dynamic_slice_in_dim(snapshots, (me ^ d) * cells, cells, axis=1)  5.55 us
  transfers between devices with their start and end apart: 14, of which 10 were waited for; matrix products, arithmetic and copies ran while one was open for 2% of the time, Pallas kernels for 4%

profile of v5, /device:TPU:0, one launch (start us, length us, event | category | flops | bytes accessed | tf_op | source)
XLA Modules:
  0.0 248.1 jit_solution(13288857970219360312)
XLA Ops:
  0.6 2.1 cut.1
  2.7 5.0 %collective-permute-start.4 = (f32[64,4096]{1,0:T(8,128)}, f32[64,4096]{1,0:T(8,128)S(1)}, u32[]{:S(2)}, u32[]{:S(2)}) collective-permute-start(f32[64,4096]{1,0:T(8,128)} %cut.1), channel_id=1, source_target_pairs={{0,20},{4,16},{8,28},{12,24},{16,4},{20,0},{24,12},{28,8},{1,21},{... | collective-permute-start | bytes 3145736 | tf_op jit(solution)/shard_map/ppermute | solution.py:384
  7.8 0.0 copy-start.5
  7.8 5.6 %constant_dynamic-slice_fusion = (f32[64,4096]{1,0:T(8,128)}, f32[64,4096]{1,0:T(8,128)S(1)}, f32[64,4096]{1,0:T(8,128)}, f32[64,4096]{1,0:T(8,128)}, f32[64,409...) fusion(f32[64,32768]{1,0:T(8,128)} %x_ref.1, s32[]{:T(128)S(6)} %select_n.91, s32[]{:T(128)S(6)} %select_n.89, ...), kind=kLoop, calls=%fused_computation.6 | loop fusion | bytes 14680092 | tf_op jit(solution)/shard_map/dynamic_slice | solution.py:383
  13.3 0.3 collective-permute-start.3
  13.7 1.5 collective-permute-start.2
  15.2 0.2 collective-permute-start.1
  15.4 1.7 collective-permute-start
  17.2 59.9 %collective-permute-done.4.refs_5_ = f32[64,4096]{1,0:T(8,128)S(1)} collective-permute-done((f32[64,4096]{1,0:T(8,128)}, f32[64,4096]{1,0:T(8,128)S(1)}, u32[]{:S(2)}, u32[]{:S(2)}) %collective-permute-start.4) | collective-permute-done | bytes 1048608 | tf_op jit(solution)/shard_map/ppermute | solution.py:384
  77.0 3.7 %collective-permute-start.5 = (f32[64,4096]{1,0:T(8,128)}, f32[64,4096]{1,0:T(8,128)}, u32[]{:S(2)}, u32[]{:S(2)}) collective-permute-start(f32[64,4096]{1,0:T(8,128)} %get-tuple-element.28), channel_id=1, source_target_pairs={{0,28},{4,24},{8,20},{12,16},{16,12},{20,8},{24,4},{28,0},{1,29},{... | collective-permute-start | bytes 3145736 | tf_op jit(solution)/shard_map/ppermute | solution.py:384
  80.7 20.2 %collective-permute-done.3.refs_4_ = f32[64,4096]{1,0:T(8,128)S(1)} collective-permute-done((f32[64,4096]{1,0:T(8,128)S(1)}, f32[64,4096]{1,0:T(8,128)S(1)}, u32[]{:S(2)}, u32[]{:S(2)}) %collective-permute-start.3) | collective-permute-done | bytes 1048608 | tf_op jit(solution)/shard_map/ppermute | solution.py:384
  100.9 0.0 copy-start.3
  100.9 1.1 copy-done.3
  101.9 2.5 %collective-permute-start.6 = (f32[64,4096]{1,0:T(8,128)}, f32[64,4096]{1,0:T(8,128)S(1)}, u32[]{:S(2)}, u32[]{:S(2)}) collective-permute-start(f32[64,4096]{1,0:T(8,128)} %get-tuple-element.22), channel_id=1, source_target_pairs={{0,24},{4,28},{8,16},{12,20},{16,8},{20,12},{24,0},{28,4},{1,25},{... | collective-permute-start | bytes 3145736 | tf_op jit(solution)/shard_map/ppermute | solution.py:384
  104.4 0.0 copy-done.5
  104.4 0.0 collective-permute-done.2.refs_3_
  104.5 45.2 %collective-permute-done.1.refs_2_ = f32[64,4096]{1,0:T(8,128)} collective-permute-done((f32[64,4096]{1,0:T(8,128)}, f32[64,4096]{1,0:T(8,128)}, u32[]{:S(2)}, u32[]{:S(2)}) %collective-permute-start.1) | collective-permute-done | bytes 1048608 | tf_op jit(solution)/shard_map/ppermute | solution.py:384
  149.6 0.0 collective-permute-done.refs_1_
  149.6 0.0 collective-permute-done.5.refs_6_
  149.6 0.0 copy-start.4
  149.6 1.2 copy-done.4
  150.9 9.1 %gram.1 = (f32[1280,128]{1,0:T(8,128)S(1)}, bf16[512,4096]{1,0:T(8,128)(2,1)S(1)}, bf16[512,4096]{1,0:T(8,128)(2,1)S(1)}, bf16[512,4096]{1,0:T(8,128)(2,1)S(1)}, bf16[512,4096]{1,0:T(8,128)(2,1)}) custom-call(s32[8]{0:T(128)S(1)} %broadcast_xor_fusion.places_ref, f32[64,4096]{1,0:T(8,128)S(1)} %get-tuple-element.27.refs_0_, ...), custom_call_target="tpu_custom_call" | custom-call | flops 4294967296 | bytes 16777216 | tf_op jit(solution)/shard_map/gram/pallas_call | solution.py:65
  160.0 0.0 copy-start
  160.0 0.0 collective-permute-done.6.part_ref
  160.0 3.6 %gram_last.1 = (f32[1280,128]{1,0:T(8,128)S(1)}, bf16[64,4096]{1,0:T(8,128)(2,1)S(1)}, bf16[64,4096]{1,0:T(8,128)(2,1)S(1)}) custom-call(s32[8]{0:T(128)S(1)} %broadcast_xor_fusion.places_ref, f32[1280,128]{1,0:T(8,128)S(1)} %get-tuple-element.12.before_ref, f32[64,4096]{1,0:T(8,128)S(1)} %collective-permute-done.6.part_ref, ...), custom_call_target="tpu_custom_call" | custom-call | flops 805306368 | bytes 8388608 | tf_op jit(solution)/shard_map/gram_last/pallas_call | solution.py:103
  163.6 0.0 copy-done
  163.7 0.1 collective-permute-start.7
  163.8 1.6 collective-permute-done.7
  165.4 1.6 collective-permute-start.8
  167.0 3.8 %collective-permute-done.8 = f32[320,128]{1,0:T(8,128)S(1)} collective-permute-done((f32[320,128]{1,0:T(8,128)S(1)}, f32[320,128]{1,0:T(8,128)S(1)}, u32[]{:S(2)}, u32[]{:S(2)}) %collective-permute-start.8) | collective-permute-done | bytes 163872 | tf_op jit(solution)/shard_map/ppermute | solution.py:128
  170.9 1.5 collective-permute-start.9
  172.3 3.9 %collective-permute-done.9 = f32[320,128]{1,0:T(8,128)S(1)} collective-permute-done((f32[320,128]{1,0:T(8,128)S(1)}, f32[320,128]{1,0:T(8,128)S(1)}, u32[]{:S(2)}, u32[]{:S(2)}) %collective-permute-start.9) | collective-permute-done | bytes 163872 | tf_op jit(solution)/shard_map/ppermute | solution.py:128
  176.3 29.4 %collective-permute-start.10 = (f32[320,128]{1,0:T(8,128)S(1)}, f32[320,128]{1,0:T(8,128)S(1)}, u32[]{:S(2)}, u32[]{:S(2)}) collective-permute-start(f32[320,128]{1,0:T(8,128)S(1)} %add.53), channel_id=1, source_target_pairs={{0,8},{4,12},{8,0},{12,4},{16,24},{20,28},{24,16},{28,20},{1,17},{... | collective-permute-start | bytes 491528 | tf_op jit(solution)/shard_map/ppermute | solution.py:128
  205.7 3.9 %collective-permute-done.10 = f32[320,128]{1,0:T(8,128)S(1)} collective-permute-done((f32[320,128]{1,0:T(8,128)S(1)}, f32[320,128]{1,0:T(8,128)S(1)}, u32[]{:S(2)}, u32[]{:S(2)}) %collective-permute-start.10) | collective-permute-done | bytes 163872 | tf_op jit(solution)/shard_map/ppermute | solution.py:128
  209.5 3.3 %collective-permute-start.11 = (f32[320,128]{1,0:T(8,128)S(1)}, f32[320,128]{1,0:T(8,128)S(1)}, u32[]{:S(2)}, u32[]{:S(2)}) collective-permute-start(f32[320,128]{1,0:T(8,128)S(1)} %add.54), channel_id=1, source_target_pairs={{0,16},{4,20},{8,24},{12,28},{16,0},{20,4},{24,8},{28,12},{1,3},{5... | collective-permute-start | bytes 491528 | tf_op jit(solution)/shard_map/ppermute | solution.py:128
  212.9 5.1 %collective-permute-done.11 = f32[320,128]{1,0:T(8,128)S(1)} collective-permute-done((f32[320,128]{1,0:T(8,128)S(1)}, f32[320,128]{1,0:T(8,128)S(1)}, u32[]{:S(2)}, u32[]{:S(2)}) %collective-permute-start.11) | collective-permute-done | bytes 163872 | tf_op jit(solution)/shard_map/ppermute | solution.py:128
  218.0 1.6 collective-permute-start.12
  219.5 3.8 %collective-permute-done.12 = f32[320,128]{1,0:T(8,128)S(1)} collective-permute-done((f32[320,128]{1,0:T(8,128)S(1)}, f32[320,128]{1,0:T(8,128)S(1)}, u32[]{:S(2)}, u32[]{:S(2)}) %collective-permute-start.12) | collective-permute-done | bytes 163872 | tf_op jit(solution)/shard_map/ppermute | solution.py:128
  223.4 0.1 collective-permute-start.13
  223.4 1.6 collective-permute-done.13
  225.1 0.0 copy-start.1
  225.1 0.0 copy-start.2
  225.1 15.0 %factor.1 = (f32[512,512]{1,0:T(8,128)}, f32[512,512]{1,0:T(8,128)S(1)}) custom-call(f32[1280,128]{1,0:T(8,128)S(1)} %maximum_select_fusion.gram_ref), custom_call_target="tpu_custom_call" | custom-call | flops 13421772800 | bytes 2097152 | tf_op jit(solution)/shard_map/factor/pallas_call | solution.py:276
  240.1 0.0 copy-done.1
  240.1 0.0 copy-done.2
  240.1 7.8 %modes.1 = f32[512,4096]{1,0:T(8,128)} custom-call(s32[8]{0:T(128)S(1)} %broadcast_xor_fusion.places_ref, f32[512,512]{1,0:T(8,128)S(1)} %get-tuple-element.16.w_ref, bf16[512,4096]{1,0:T(8,128)(2,1)S(1)} %copy-done.1, bf16[512,4096]{1,0:T(8,128)(2,1)S(1)} %copy-done.2, bf16[64,4096]{1,0:T(8,128)(2,1)S(1)} %get-tuple-element.19.hi_last, ...), custom_call_target="tpu_custom_call" | custom-call | tf_op jit(solution)/shard_map/modes/pallas_call | solution.py:322
  (10 shorter events, 0.3 us)
Async XLA Ops:
  2.7 74.3 %collective-permute-start.4 = (f32[64,4096]{1,0:T(8,128)}, f32[64,4096]{1,0:T(8,128)S(1)}, u32[]{:S(2)}, u32[]{:S(2)}) collective-permute-start(f32[64,4096]{1,0:T(8,128)} %cut.1), channel_id=1, source_target_pairs={{0,20},{4,16},{8,28},{12,24},{16,4},{20,0},{24,12},{28,8},{1,21},{... | collective-permute-start | bytes 3145736 | tf_op jit(solution)/shard_map/ppermute | solution.py:384
  7.8 96.7 %copy-start.5 = (s32[8]{0:T(128)S(1)}, s32[8]{0:T(128)}, u32[]{:S(2)}) copy-start(s32[8]{0:T(128)} %constant.46.clone) | copy-start | bytes 100
  13.3 87.6 %collective-permute-start.3 = (f32[64,4096]{1,0:T(8,128)S(1)}, f32[64,4096]{1,0:T(8,128)S(1)}, u32[]{:S(2)}, u32[]{:S(2)}) collective-permute-start(f32[64,4096]{1,0:T(8,128)S(1)} %get-tuple-element.23), channel_id=1, source_target_pairs={{0,16},{4,20},{8,24},{12,28},{16,0},{20,4},{24,8},{28,12},{1,17},{... | collective-permute-start | bytes 3145736 | tf_op jit(solution)/shard_map/ppermute | solution.py:384
  13.7 90.8 %collective-permute-start.2 = (f32[64,4096]{1,0:T(8,128)}, f32[64,4096]{1,0:T(8,128)}, u32[]{:S(2)}, u32[]{:S(2)}) collective-permute-start(f32[64,4096]{1,0:T(8,128)} %get-tuple-element.24), channel_id=1, source_target_pairs={{0,12},{4,8},{8,4},{12,0},{16,28},{20,24},{24,20},{28,16},{1,13},{... | collective-permute-start | bytes 3145736 | tf_op jit(solution)/shard_map/ppermute | solution.py:384
  15.2 134.4 %collective-permute-start.1 = (f32[64,4096]{1,0:T(8,128)}, f32[64,4096]{1,0:T(8,128)}, u32[]{:S(2)}, u32[]{:S(2)}) collective-permute-start(f32[64,4096]{1,0:T(8,128)} %get-tuple-element.25), channel_id=1, source_target_pairs={{0,8},{4,12},{8,0},{12,4},{16,24},{20,28},{24,16},{28,20},{1,9},{5... | collective-permute-start | bytes 3145736 | tf_op jit(solution)/shard_map/ppermute | solution.py:384
  15.4 134.2 %collective-permute-start = (f32[64,4096]{1,0:T(8,128)}, f32[64,4096]{1,0:T(8,128)}, u32[]{:S(2)}, u32[]{:S(2)}) collective-permute-start(f32[64,4096]{1,0:T(8,128)} %get-tuple-element.26), channel_id=1, source_target_pairs={{0,4},{4,0},{8,12},{12,8},{16,20},{20,16},{24,28},{28,24},{1,5},{5... | collective-permute-start | bytes 3145736 | tf_op jit(solution)/shard_map/ppermute | solution.py:384
  77.0 72.6 %collective-permute-start.5 = (f32[64,4096]{1,0:T(8,128)}, f32[64,4096]{1,0:T(8,128)}, u32[]{:S(2)}, u32[]{:S(2)}) collective-permute-start(f32[64,4096]{1,0:T(8,128)} %get-tuple-element.28), channel_id=1, source_target_pairs={{0,28},{4,24},{8,20},{12,16},{16,12},{20,8},{24,4},{28,0},{1,29},{... | collective-permute-start | bytes 3145736 | tf_op jit(solution)/shard_map/ppermute | solution.py:384
  100.9 1.1 copy-start.3
  101.9 58.0 %collective-permute-start.6 = (f32[64,4096]{1,0:T(8,128)}, f32[64,4096]{1,0:T(8,128)S(1)}, u32[]{:S(2)}, u32[]{:S(2)}) collective-permute-start(f32[64,4096]{1,0:T(8,128)} %get-tuple-element.22), channel_id=1, source_target_pairs={{0,24},{4,28},{8,16},{12,20},{16,8},{20,12},{24,0},{28,4},{1,25},{... | collective-permute-start | bytes 3145736 | tf_op jit(solution)/shard_map/ppermute | solution.py:384
  149.6 1.2 copy-start.4
  160.0 3.7 %copy-start = (bf16[512,4096]{1,0:T(8,128)(2,1)}, bf16[512,4096]{1,0:T(8,128)(2,1)S(1)}, u32[]{:S(2)}) copy-start(bf16[512,4096]{1,0:T(8,128)(2,1)S(1)} %get-tuple-element.17.hi_ref) | copy-start | bytes 12582916
  163.7 1.7 collective-permute-start.7
  165.4 5.4 %collective-permute-start.8 = (f32[320,128]{1,0:T(8,128)S(1)}, f32[320,128]{1,0:T(8,128)S(1)}, u32[]{:S(2)}, u32[]{:S(2)}) collective-permute-start(f32[320,128]{1,0:T(8,128)S(1)} %slice_select_fusion.1), channel_id=1, source_target_pairs={{0,2},{4,6},{8,10},{12,14},{16,18},{20,22},{24,26},{28,30},{1,5},{... | collective-permute-start | bytes 491528 | tf_op jit(solution)/shard_map/ppermute | solution.py:128
  170.9 5.4 %collective-permute-start.9 = (f32[320,128]{1,0:T(8,128)S(1)}, f32[320,128]{1,0:T(8,128)S(1)}, u32[]{:S(2)}, u32[]{:S(2)}) collective-permute-start(f32[320,128]{1,0:T(8,128)S(1)} %select_add_fusion.1), channel_id=1, source_target_pairs={{0,4},{4,0},{8,12},{12,8},{16,20},{20,16},{24,28},{28,24},{1,9},{5... | collective-permute-start | bytes 491528 | tf_op jit(solution)/shard_map/ppermute | solution.py:128
  176.3 33.3 %collective-permute-start.10 = (f32[320,128]{1,0:T(8,128)S(1)}, f32[320,128]{1,0:T(8,128)S(1)}, u32[]{:S(2)}, u32[]{:S(2)}) collective-permute-start(f32[320,128]{1,0:T(8,128)S(1)} %add.53), channel_id=1, source_target_pairs={{0,8},{4,12},{8,0},{12,4},{16,24},{20,28},{24,16},{28,20},{1,17},{... | collective-permute-start | bytes 491528 | tf_op jit(solution)/shard_map/ppermute | solution.py:128
  209.5 8.4 %collective-permute-start.11 = (f32[320,128]{1,0:T(8,128)S(1)}, f32[320,128]{1,0:T(8,128)S(1)}, u32[]{:S(2)}, u32[]{:S(2)}) collective-permute-start(f32[320,128]{1,0:T(8,128)S(1)} %add.54), channel_id=1, source_target_pairs={{0,16},{4,20},{8,24},{12,28},{16,0},{20,4},{24,8},{28,12},{1,3},{5... | collective-permute-start | bytes 491528 | tf_op jit(solution)/shard_map/ppermute | solution.py:128
  218.0 5.4 %collective-permute-start.12 = (f32[320,128]{1,0:T(8,128)S(1)}, f32[320,128]{1,0:T(8,128)S(1)}, u32[]{:S(2)}, u32[]{:S(2)}) collective-permute-start(f32[320,128]{1,0:T(8,128)S(1)} %add.55), channel_id=1, source_target_pairs={{0,2},{4,6},{8,10},{12,14},{16,18},{20,22},{24,26},{28,30},{1,5},{... | collective-permute-start | bytes 491528 | tf_op jit(solution)/shard_map/ppermute | solution.py:128
  223.4 1.7 collective-permute-start.13
  225.1 15.0 %copy-start.1 = (bf16[512,4096]{1,0:T(8,128)(2,1)S(1)}, bf16[512,4096]{1,0:T(8,128)(2,1)}, u32[]{:S(2)}) copy-start(bf16[512,4096]{1,0:T(8,128)(2,1)} %copy-done) | copy-start | bytes 12582916
  225.1 15.0 %copy-start.2 = (bf16[512,4096]{1,0:T(8,128)(2,1)S(1)}, bf16[512,4096]{1,0:T(8,128)(2,1)}, u32[]{:S(2)}) copy-start(bf16[512,4096]{1,0:T(8,128)(2,1)} %get-tuple-element.18.lo_ref) | copy-start | bytes 12582916

commit v6 on v5

--- a/solution.py
+++ b/solution.py
@@ -136,7 +136,7 @@
 
 def sum_all(x):
     links = [("row", b) for b in bits("row")[1:]] + [("snap", b) for b in bits("snap")]
-    orders = [[("row", 1), *links], [("row", 1), *links[1:], links[0]]]
+    orders = [[("row", 1), *links], [("row", 1), *links[len(links) // 2 :], *links[: len(links) // 2]]]
     for at in (0, 1):
         upper = side(orders, at)
         half = x.shape[0] // 2

time: 248 us -> 248 us (level)
  no operation moved by 1% of the time
where the time goes in v6:
time: 248 us
  waiting for transfers between devices  148 us (60%)
  starting transfers between devices  53.1 us (21%)
  Pallas kernels  37.6 us (15%)
  local copies, waits for them, and re-layouts  7.85 us (3%)
    ppermute x7, waiting for transfers between devices, regroup(): lax.ppermute(block, 'snap', [(i, i ^ d) for i in range(n)])  125 us
    ppermute x7, starting transfers between devices, step(): return lax.ppermute(x, ('snap', 'row'), pairs)  38.1 us
    ppermute x7, waiting for transfers between devices, step(): return lax.ppermute(x, ('snap', 'row'), pairs)  23.2 us
    ppermute x7, starting transfers between devices, regroup(): lax.ppermute(block, 'snap', [(i, i ^ d) for i in range(n)])  15.1 us
    pallas_call x1, Pallas kernels, factorize(): pl.pallas_call(functools.partial(factor_kernel, root), out_shape=(out, ou...  15 us
    pallas_call x1, Pallas kernels, gram(): pl.pallas_call(functools.partial(gram_kernel, n, tile), out_shape=(jax.Sh...  9.1 us
    pallas_call x1, Pallas kernels, whiten(): pl.pallas_call(modes_kernel, out_shape=jax.ShapeDtypeStruct((size, cells)...  7.8 us
    dynamic_slice x1, local copies, waits for them, and re-layouts, regroup(): block = lax.dynamic_slice_in_dim(snapshots, (me ^ d) * cells, cells, axis=1)  5.55 us
  transfers between devices with their start and end apart: 14, of which 10 were waited for; matrix products, arithmetic and copies ran while one was open for 2% of the time, Pallas kernels for 4%

profile of v6, /device:TPU:0, one launch (start us, length us, event | category | flops | bytes accessed | tf_op | source)
XLA Modules:
  0.0 248.2 jit_solution(11787313812572062334)
XLA Ops:
  0.6 2.1 cut.1
  2.7 5.0 %collective-permute-start.4 = (f32[64,4096]{1,0:T(8,128)}, f32[64,4096]{1,0:T(8,128)S(1)}, u32[]{:S(2)}, u32[]{:S(2)}) collective-permute-start(f32[64,4096]{1,0:T(8,128)} %cut.1), channel_id=1, source_target_pairs={{0,20},{4,16},{8,28},{12,24},{16,4},{20,0},{24,12},{28,8},{1,21},{... | collective-permute-start | bytes 3145736 | tf_op jit(solution)/shard_map/ppermute | solution.py:384
  7.8 0.0 copy-start.5
  7.8 5.6 %constant_dynamic-slice_fusion = (f32[64,4096]{1,0:T(8,128)}, f32[64,4096]{1,0:T(8,128)S(1)}, f32[64,4096]{1,0:T(8,128)}, f32[64,4096]{1,0:T(8,128)}, f32[64,409...) fusion(f32[64,32768]{1,0:T(8,128)} %x_ref.1, s32[]{:T(128)S(6)} %select_n.91, s32[]{:T(128)S(6)} %select_n.89, ...), kind=kLoop, calls=%fused_computation.6 | loop fusion | bytes 14680092 | tf_op jit(solution)/shard_map/dynamic_slice | solution.py:383
  13.3 0.3 collective-permute-start.3
  13.7 1.5 collective-permute-start.2
  15.2 0.2 collective-permute-start.1
  15.4 1.7 collective-permute-start
  17.2 59.9 %collective-permute-done.4.refs_5_ = f32[64,4096]{1,0:T(8,128)S(1)} collective-permute-done((f32[64,4096]{1,0:T(8,128)}, f32[64,4096]{1,0:T(8,128)S(1)}, u32[]{:S(2)}, u32[]{:S(2)}) %collective-permute-start.4) | collective-permute-done | bytes 1048608 | tf_op jit(solution)/shard_map/ppermute | solution.py:384
  77.0 3.7 %collective-permute-start.5 = (f32[64,4096]{1,0:T(8,128)}, f32[64,4096]{1,0:T(8,128)}, u32[]{:S(2)}, u32[]{:S(2)}) collective-permute-start(f32[64,4096]{1,0:T(8,128)} %get-tuple-element.28), channel_id=1, source_target_pairs={{0,28},{4,24},{8,20},{12,16},{16,12},{20,8},{24,4},{28,0},{1,29},{... | collective-permute-start | bytes 3145736 | tf_op jit(solution)/shard_map/ppermute | solution.py:384
  80.7 20.2 %collective-permute-done.3.refs_4_ = f32[64,4096]{1,0:T(8,128)S(1)} collective-permute-done((f32[64,4096]{1,0:T(8,128)S(1)}, f32[64,4096]{1,0:T(8,128)S(1)}, u32[]{:S(2)}, u32[]{:S(2)}) %collective-permute-start.3) | collective-permute-done | bytes 1048608 | tf_op jit(solution)/shard_map/ppermute | solution.py:384
  100.9 0.0 copy-start.3
  100.9 1.1 copy-done.3
  101.9 2.5 %collective-permute-start.6 = (f32[64,4096]{1,0:T(8,128)}, f32[64,4096]{1,0:T(8,128)S(1)}, u32[]{:S(2)}, u32[]{:S(2)}) collective-permute-start(f32[64,4096]{1,0:T(8,128)} %get-tuple-element.22), channel_id=1, source_target_pairs={{0,24},{4,28},{8,16},{12,20},{16,8},{20,12},{24,0},{28,4},{1,25},{... | collective-permute-start | bytes 3145736 | tf_op jit(solution)/shard_map/ppermute | solution.py:384
  104.4 0.0 copy-done.5
  104.4 0.0 collective-permute-done.2.refs_3_
  104.5 45.2 %collective-permute-done.1.refs_2_ = f32[64,4096]{1,0:T(8,128)} collective-permute-done((f32[64,4096]{1,0:T(8,128)}, f32[64,4096]{1,0:T(8,128)}, u32[]{:S(2)}, u32[]{:S(2)}) %collective-permute-start.1) | collective-permute-done | bytes 1048608 | tf_op jit(solution)/shard_map/ppermute | solution.py:384
  149.6 0.0 collective-permute-done.refs_1_
  149.6 0.0 collective-permute-done.5.refs_6_
  149.6 0.0 copy-start.4
  149.6 1.2 copy-done.4
  150.9 9.1 %gram.1 = (f32[1280,128]{1,0:T(8,128)S(1)}, bf16[512,4096]{1,0:T(8,128)(2,1)S(1)}, bf16[512,4096]{1,0:T(8,128)(2,1)S(1)}, bf16[512,4096]{1,0:T(8,128)(2,1)S(1)}, bf16[512,4096]{1,0:T(8,128)(2,1)}) custom-call(s32[8]{0:T(128)S(1)} %broadcast_xor_fusion.places_ref, f32[64,4096]{1,0:T(8,128)S(1)} %get-tuple-element.27.refs_0_, ...), custom_call_target="tpu_custom_call" | custom-call | flops 4294967296 | bytes 16777216 | tf_op jit(solution)/shard_map/gram/pallas_call | solution.py:65
  160.0 0.0 copy-start
  160.0 0.0 collective-permute-done.6.part_ref
  160.0 3.6 %gram_last.1 = (f32[1280,128]{1,0:T(8,128)S(1)}, bf16[64,4096]{1,0:T(8,128)(2,1)S(1)}, bf16[64,4096]{1,0:T(8,128)(2,1)S(1)}) custom-call(s32[8]{0:T(128)S(1)} %broadcast_xor_fusion.places_ref, f32[1280,128]{1,0:T(8,128)S(1)} %get-tuple-element.12.before_ref, f32[64,4096]{1,0:T(8,128)S(1)} %collective-permute-done.6.part_ref, ...), custom_call_target="tpu_custom_call" | custom-call | flops 805306368 | bytes 8388608 | tf_op jit(solution)/shard_map/gram_last/pallas_call | solution.py:103
  163.6 0.0 copy-done
  163.7 0.1 collective-permute-start.7
  163.8 1.6 collective-permute-done.7
  165.4 1.6 collective-permute-start.8
  167.0 3.8 %collective-permute-done.8 = f32[320,128]{1,0:T(8,128)S(1)} collective-permute-done((f32[320,128]{1,0:T(8,128)S(1)}, f32[320,128]{1,0:T(8,128)S(1)}, u32[]{:S(2)}, u32[]{:S(2)}) %collective-permute-start.8) | collective-permute-done | bytes 163872 | tf_op jit(solution)/shard_map/ppermute | solution.py:128
  170.9 1.5 collective-permute-start.9
  172.3 3.9 %collective-permute-done.9 = f32[320,128]{1,0:T(8,128)S(1)} collective-permute-done((f32[320,128]{1,0:T(8,128)S(1)}, f32[320,128]{1,0:T(8,128)S(1)}, u32[]{:S(2)}, u32[]{:S(2)}) %collective-permute-start.9) | collective-permute-done | bytes 163872 | tf_op jit(solution)/shard_map/ppermute | solution.py:128
  176.3 29.4 %collective-permute-start.10 = (f32[320,128]{1,0:T(8,128)S(1)}, f32[320,128]{1,0:T(8,128)S(1)}, u32[]{:S(2)}, u32[]{:S(2)}) collective-permute-start(f32[320,128]{1,0:T(8,128)S(1)} %add.53), channel_id=1, source_target_pairs={{0,8},{4,12},{8,0},{12,4},{16,24},{20,28},{24,16},{28,20},{1,3},{5... | collective-permute-start | bytes 491528 | tf_op jit(solution)/shard_map/ppermute | solution.py:128
  205.7 3.3 %collective-permute-done.10 = f32[320,128]{1,0:T(8,128)S(1)} collective-permute-done((f32[320,128]{1,0:T(8,128)S(1)}, f32[320,128]{1,0:T(8,128)S(1)}, u32[]{:S(2)}, u32[]{:S(2)}) %collective-permute-start.10) | collective-permute-done | bytes 163872 | tf_op jit(solution)/shard_map/ppermute | solution.py:128
  209.0 3.9 %collective-permute-start.11 = (f32[320,128]{1,0:T(8,128)S(1)}, f32[320,128]{1,0:T(8,128)S(1)}, u32[]{:S(2)}, u32[]{:S(2)}) collective-permute-start(f32[320,128]{1,0:T(8,128)S(1)} %add.54), channel_id=1, source_target_pairs={{0,16},{4,20},{8,24},{12,28},{16,0},{20,4},{24,8},{28,12},{1,5},{5... | collective-permute-start | bytes 491528 | tf_op jit(solution)/shard_map/ppermute | solution.py:128
  212.9 5.2 %collective-permute-done.11 = f32[320,128]{1,0:T(8,128)S(1)} collective-permute-done((f32[320,128]{1,0:T(8,128)S(1)}, f32[320,128]{1,0:T(8,128)S(1)}, u32[]{:S(2)}, u32[]{:S(2)}) %collective-permute-start.11) | collective-permute-done | bytes 163872 | tf_op jit(solution)/shard_map/ppermute | solution.py:128
  218.1 1.6 collective-permute-start.12
  219.6 3.8 %collective-permute-done.12 = f32[320,128]{1,0:T(8,128)S(1)} collective-permute-done((f32[320,128]{1,0:T(8,128)S(1)}, f32[320,128]{1,0:T(8,128)S(1)}, u32[]{:S(2)}, u32[]{:S(2)}) %collective-permute-start.12) | collective-permute-done | bytes 163872 | tf_op jit(solution)/shard_map/ppermute | solution.py:128
  223.5 0.1 collective-permute-start.13
  223.6 1.6 collective-permute-done.13
  225.2 0.0 copy-start.1
  225.2 0.0 copy-start.2
  225.2 15.0 %factor.1 = (f32[512,512]{1,0:T(8,128)}, f32[512,512]{1,0:T(8,128)S(1)}) custom-call(f32[1280,128]{1,0:T(8,128)S(1)} %maximum_select_fusion.gram_ref), custom_call_target="tpu_custom_call" | custom-call | flops 13421772800 | bytes 2097152 | tf_op jit(solution)/shard_map/factor/pallas_call | solution.py:276
  240.2 0.0 copy-done.1
  240.2 0.0 copy-done.2
  240.2 7.8 %modes.1 = f32[512,4096]{1,0:T(8,128)} custom-call(s32[8]{0:T(128)S(1)} %broadcast_xor_fusion.places_ref, f32[512,512]{1,0:T(8,128)S(1)} %get-tuple-element.16.w_ref, bf16[512,4096]{1,0:T(8,128)(2,1)S(1)} %copy-done.1, bf16[512,4096]{1,0:T(8,128)(2,1)S(1)} %copy-done.2, bf16[64,4096]{1,0:T(8,128)(2,1)S(1)} %get-tuple-element.19.hi_last, ...), custom_call_target="tpu_custom_call" | custom-call | tf_op jit(solution)/shard_map/modes/pallas_call | solution.py:322
  (10 shorter events, 0.3 us)
Async XLA Ops:
  2.7 74.3 %collective-permute-start.4 = (f32[64,4096]{1,0:T(8,128)}, f32[64,4096]{1,0:T(8,128)S(1)}, u32[]{:S(2)}, u32[]{:S(2)}) collective-permute-start(f32[64,4096]{1,0:T(8,128)} %cut.1), channel_id=1, source_target_pairs={{0,20},{4,16},{8,28},{12,24},{16,4},{20,0},{24,12},{28,8},{1,21},{... | collective-permute-start | bytes 3145736 | tf_op jit(solution)/shard_map/ppermute | solution.py:384
  7.8 96.7 %copy-start.5 = (s32[8]{0:T(128)S(1)}, s32[8]{0:T(128)}, u32[]{:S(2)}) copy-start(s32[8]{0:T(128)} %constant.46.clone) | copy-start | bytes 100
  13.3 87.6 %collective-permute-start.3 = (f32[64,4096]{1,0:T(8,128)S(1)}, f32[64,4096]{1,0:T(8,128)S(1)}, u32[]{:S(2)}, u32[]{:S(2)}) collective-permute-start(f32[64,4096]{1,0:T(8,128)S(1)} %get-tuple-element.23), channel_id=1, source_target_pairs={{0,16},{4,20},{8,24},{12,28},{16,0},{20,4},{24,8},{28,12},{1,17},{... | collective-permute-start | bytes 3145736 | tf_op jit(solution)/shard_map/ppermute | solution.py:384
  13.7 90.8 %collective-permute-start.2 = (f32[64,4096]{1,0:T(8,128)}, f32[64,4096]{1,0:T(8,128)}, u32[]{:S(2)}, u32[]{:S(2)}) collective-permute-start(f32[64,4096]{1,0:T(8,128)} %get-tuple-element.24), channel_id=1, source_target_pairs={{0,12},{4,8},{8,4},{12,0},{16,28},{20,24},{24,20},{28,16},{1,13},{... | collective-permute-start | bytes 3145736 | tf_op jit(solution)/shard_map/ppermute | solution.py:384
  15.2 134.4 %collective-permute-start.1 = (f32[64,4096]{1,0:T(8,128)}, f32[64,4096]{1,0:T(8,128)}, u32[]{:S(2)}, u32[]{:S(2)}) collective-permute-start(f32[64,4096]{1,0:T(8,128)} %get-tuple-element.25), channel_id=1, source_target_pairs={{0,8},{4,12},{8,0},{12,4},{16,24},{20,28},{24,16},{28,20},{1,9},{5... | collective-permute-start | bytes 3145736 | tf_op jit(solution)/shard_map/ppermute | solution.py:384
  15.4 134.2 %collective-permute-start = (f32[64,4096]{1,0:T(8,128)}, f32[64,4096]{1,0:T(8,128)}, u32[]{:S(2)}, u32[]{:S(2)}) collective-permute-start(f32[64,4096]{1,0:T(8,128)} %get-tuple-element.26), channel_id=1, source_target_pairs={{0,4},{4,0},{8,12},{12,8},{16,20},{20,16},{24,28},{28,24},{1,5},{5... | collective-permute-start | bytes 3145736 | tf_op jit(solution)/shard_map/ppermute | solution.py:384
  77.0 72.6 %collective-permute-start.5 = (f32[64,4096]{1,0:T(8,128)}, f32[64,4096]{1,0:T(8,128)}, u32[]{:S(2)}, u32[]{:S(2)}) collective-permute-start(f32[64,4096]{1,0:T(8,128)} %get-tuple-element.28), channel_id=1, source_target_pairs={{0,28},{4,24},{8,20},{12,16},{16,12},{20,8},{24,4},{28,0},{1,29},{... | collective-permute-start | bytes 3145736 | tf_op jit(solution)/shard_map/ppermute | solution.py:384
  100.9 1.1 copy-start.3
  101.9 58.0 %collective-permute-start.6 = (f32[64,4096]{1,0:T(8,128)}, f32[64,4096]{1,0:T(8,128)S(1)}, u32[]{:S(2)}, u32[]{:S(2)}) collective-permute-start(f32[64,4096]{1,0:T(8,128)} %get-tuple-element.22), channel_id=1, source_target_pairs={{0,24},{4,28},{8,16},{12,20},{16,8},{20,12},{24,0},{28,4},{1,25},{... | collective-permute-start | bytes 3145736 | tf_op jit(solution)/shard_map/ppermute | solution.py:384
  149.6 1.2 copy-start.4
  160.0 3.7 %copy-start = (bf16[512,4096]{1,0:T(8,128)(2,1)}, bf16[512,4096]{1,0:T(8,128)(2,1)S(1)}, u32[]{:S(2)}) copy-start(bf16[512,4096]{1,0:T(8,128)(2,1)S(1)} %get-tuple-element.17.hi_ref) | copy-start | bytes 12582916
  163.7 1.7 collective-permute-start.7
  165.4 5.4 %collective-permute-start.8 = (f32[320,128]{1,0:T(8,128)S(1)}, f32[320,128]{1,0:T(8,128)S(1)}, u32[]{:S(2)}, u32[]{:S(2)}) collective-permute-start(f32[320,128]{1,0:T(8,128)S(1)} %slice_select_fusion.1), channel_id=1, source_target_pairs={{0,2},{4,6},{8,10},{12,14},{16,18},{20,22},{24,26},{28,30},{1,9},{... | collective-permute-start | bytes 491528 | tf_op jit(solution)/shard_map/ppermute | solution.py:128
  170.9 5.4 %collective-permute-start.9 = (f32[320,128]{1,0:T(8,128)S(1)}, f32[320,128]{1,0:T(8,128)S(1)}, u32[]{:S(2)}, u32[]{:S(2)}) collective-permute-start(f32[320,128]{1,0:T(8,128)S(1)} %select_add_fusion.1), channel_id=1, source_target_pairs={{0,4},{4,0},{8,12},{12,8},{16,20},{20,16},{24,28},{28,24},{1,17},{... | collective-permute-start | bytes 491528 | tf_op jit(solution)/shard_map/ppermute | solution.py:128
  176.3 32.7 %collective-permute-start.10 = (f32[320,128]{1,0:T(8,128)S(1)}, f32[320,128]{1,0:T(8,128)S(1)}, u32[]{:S(2)}, u32[]{:S(2)}) collective-permute-start(f32[320,128]{1,0:T(8,128)S(1)} %add.53), channel_id=1, source_target_pairs={{0,8},{4,12},{8,0},{12,4},{16,24},{20,28},{24,16},{28,20},{1,3},{5... | collective-permute-start | bytes 491528 | tf_op jit(solution)/shard_map/ppermute | solution.py:128
  209.0 9.1 %collective-permute-start.11 = (f32[320,128]{1,0:T(8,128)S(1)}, f32[320,128]{1,0:T(8,128)S(1)}, u32[]{:S(2)}, u32[]{:S(2)}) collective-permute-start(f32[320,128]{1,0:T(8,128)S(1)} %add.54), channel_id=1, source_target_pairs={{0,16},{4,20},{8,24},{12,28},{16,0},{20,4},{24,8},{28,12},{1,5},{5... | collective-permute-start | bytes 491528 | tf_op jit(solution)/shard_map/ppermute | solution.py:128
  218.1 5.4 %collective-permute-start.12 = (f32[320,128]{1,0:T(8,128)S(1)}, f32[320,128]{1,0:T(8,128)S(1)}, u32[]{:S(2)}, u32[]{:S(2)}) collective-permute-start(f32[320,128]{1,0:T(8,128)S(1)} %add.55), channel_id=1, source_target_pairs={{0,2},{4,6},{8,10},{12,14},{16,18},{20,22},{24,26},{28,30},{1,9},{... | collective-permute-start | bytes 491528 | tf_op jit(solution)/shard_map/ppermute | solution.py:128
  223.5 1.7 collective-permute-start.13
  225.2 15.0 %copy-start.1 = (bf16[512,4096]{1,0:T(8,128)(2,1)S(1)}, bf16[512,4096]{1,0:T(8,128)(2,1)}, u32[]{:S(2)}) copy-start(bf16[512,4096]{1,0:T(8,128)(2,1)} %copy-done) | copy-start | bytes 12582916
  225.2 15.0 %copy-start.2 = (bf16[512,4096]{1,0:T(8,128)(2,1)S(1)}, bf16[512,4096]{1,0:T(8,128)(2,1)}, u32[]{:S(2)}) copy-start(bf16[512,4096]{1,0:T(8,128)(2,1)} %get-tuple-element.18.lo_ref) | copy-start | bytes 12582916

commit v7 on v5

--- a/solution.py
+++ b/solution.py
@@ -373,7 +373,7 @@
     n = lax.axis_size("snap")
     me = lax.axis_index("snap")
     cells = snapshots.shape[1] // n
-    begin, end = n // 2 + 1, n // 2 + n // 4
+    begin, end = n // 2, n // 2 + n // 4
     far = [d for d in reversed(range(n // 2, n)) if d not in (begin, end)]
     got = {}
     for d in [end, *range(1, n // 2), *far, begin, 0]:

time: 248 us -> 247 us (level)
  no operation moved by 1% of the time
where the time goes in v7:
time: 247 us
  waiting for transfers between devices  148 us (60%)
  starting transfers between devices  52.9 us (21%)
  Pallas kernels  37.6 us (15%)
  local copies, waits for them, and re-layouts  7.85 us (3%)
    ppermute x7, waiting for transfers between devices, regroup(): lax.ppermute(block, 'snap', [(i, i ^ d) for i in range(n)])  124 us
    ppermute x7, starting transfers between devices, step(): return lax.ppermute(x, ('snap', 'row'), pairs)  36.8 us
    ppermute x7, waiting for transfers between devices, step(): return lax.ppermute(x, ('snap', 'row'), pairs)  23.5 us
    ppermute x7, starting transfers between devices, regroup(): lax.ppermute(block, 'snap', [(i, i ^ d) for i in range(n)])  16.1 us
    pallas_call x1, Pallas kernels, factorize(): pl.pallas_call(functools.partial(factor_kernel, root), out_shape=(out, ou...  15 us
    pallas_call x1, Pallas kernels, gram(): pl.pallas_call(functools.partial(gram_kernel, n, tile), out_shape=(jax.Sh...  9.1 us
    pallas_call x1, Pallas kernels, whiten(): pl.pallas_call(modes_kernel, out_shape=jax.ShapeDtypeStruct((size, cells)...  7.8 us
    dynamic_slice x1, local copies, waits for them, and re-layouts, regroup(): block = lax.dynamic_slice_in_dim(snapshots, (me ^ d) * cells, cells, axis=1)  5.55 us
  transfers between devices with their start and end apart: 14, of which 10 were waited for; matrix products, arithmetic and copies ran while one was open for 2% of the time, Pallas kernels for 4%

profile of v7, /device:TPU:0, one launch (start us, length us, event | category | flops | bytes accessed | tf_op | source)
XLA Modules:
  0.0 247.2 jit_solution(6933119167616419703)
XLA Ops:
  0.6 2.1 cut.1
  2.7 4.1 %collective-permute-start.3 = (f32[64,4096]{1,0:T(8,128)}, f32[64,4096]{1,0:T(8,128)S(1)}, u32[]{:S(2)}, u32[]{:S(2)}) collective-permute-start(f32[64,4096]{1,0:T(8,128)} %cut.1), channel_id=1, source_target_pairs={{0,16},{4,20},{8,24},{12,28},{16,0},{20,4},{24,8},{28,12},{1,17},{... | collective-permute-start | bytes 3145736 | tf_op jit(solution)/shard_map/ppermute | solution.py:384
  6.8 0.0 copy-start.5
  6.8 5.6 %constant_dynamic-slice_fusion = (f32[64,4096]{1,0:T(8,128)}, f32[64,4096]{1,0:T(8,128)S(1)}, f32[64,4096]{1,0:T(8,128)}, f32[64,4096]{1,0:T(8,128)}, f32[64,409...) fusion(f32[64,32768]{1,0:T(8,128)} %x_ref.1, s32[]{:T(128)S(6)} %select_n.91, s32[]{:T(128)S(6)} %select_n.89, ...), kind=kLoop, calls=%fused_computation.6 | loop fusion | bytes 14680092 | tf_op jit(solution)/shard_map/dynamic_slice | solution.py:383
  12.4 1.3 collective-permute-start.4
  13.7 1.5 collective-permute-start.2
  15.2 0.2 collective-permute-start.1
  15.4 1.8 collective-permute-start
  17.2 58.9 %collective-permute-done.3.refs_4_ = f32[64,4096]{1,0:T(8,128)S(1)} collective-permute-done((f32[64,4096]{1,0:T(8,128)}, f32[64,4096]{1,0:T(8,128)S(1)}, u32[]{:S(2)}, u32[]{:S(2)}) %collective-permute-start.3) | collective-permute-done | bytes 1048608 | tf_op jit(solution)/shard_map/ppermute | solution.py:384
  76.1 3.7 %collective-permute-start.5 = (f32[64,4096]{1,0:T(8,128)}, f32[64,4096]{1,0:T(8,128)}, u32[]{:S(2)}, u32[]{:S(2)}) collective-permute-start(f32[64,4096]{1,0:T(8,128)} %get-tuple-element.28), channel_id=1, source_target_pairs={{0,28},{4,24},{8,20},{12,16},{16,12},{20,8},{24,4},{28,0},{1,29},{... | collective-permute-start | bytes 3145736 | tf_op jit(solution)/shard_map/ppermute | solution.py:384
  79.8 20.1 %collective-permute-done.4.refs_5_ = f32[64,4096]{1,0:T(8,128)S(1)} collective-permute-done((f32[64,4096]{1,0:T(8,128)S(1)}, f32[64,4096]{1,0:T(8,128)S(1)}, u32[]{:S(2)}, u32[]{:S(2)}) %collective-permute-start.4) | collective-permute-done | bytes 1048608 | tf_op jit(solution)/shard_map/ppermute | solution.py:384
  99.9 0.0 copy-start.3
  99.9 1.1 copy-done.3
  100.9 3.5 %collective-permute-start.6 = (f32[64,4096]{1,0:T(8,128)}, f32[64,4096]{1,0:T(8,128)S(1)}, u32[]{:S(2)}, u32[]{:S(2)}) collective-permute-start(f32[64,4096]{1,0:T(8,128)} %get-tuple-element.22), channel_id=1, source_target_pairs={{0,24},{4,28},{8,16},{12,20},{16,8},{20,12},{24,0},{28,4},{1,25},{... | collective-permute-start | bytes 3145736 | tf_op jit(solution)/shard_map/ppermute | solution.py:384
  104.4 0.0 copy-done.5
  104.5 0.0 collective-permute-done.2.refs_3_
  104.5 45.1 %collective-permute-done.1.refs_2_ = f32[64,4096]{1,0:T(8,128)} collective-permute-done((f32[64,4096]{1,0:T(8,128)}, f32[64,4096]{1,0:T(8,128)}, u32[]{:S(2)}, u32[]{:S(2)}) %collective-permute-start.1) | collective-permute-done | bytes 1048608 | tf_op jit(solution)/shard_map/ppermute | solution.py:384
  149.5 0.0 collective-permute-done.refs_1_
  149.5 0.0 collective-permute-done.5.refs_6_
  149.5 0.0 copy-start.4
  149.6 1.2 copy-done.4
  150.8 9.1 %gram.1 = (f32[1280,128]{1,0:T(8,128)S(1)}, bf16[512,4096]{1,0:T(8,128)(2,1)S(1)}, bf16[512,4096]{1,0:T(8,128)(2,1)S(1)}, bf16[512,4096]{1,0:T(8,128)(2,1)S(1)}, bf16[512,4096]{1,0:T(8,128)(2,1)}) custom-call(s32[8]{0:T(128)S(1)} %broadcast_xor_fusion.places_ref, f32[64,4096]{1,0:T(8,128)S(1)} %get-tuple-element.27.refs_0_, ...), custom_call_target="tpu_custom_call" | custom-call | flops 4294967296 | bytes 16777216 | tf_op jit(solution)/shard_map/gram/pallas_call | solution.py:65
  159.9 0.0 copy-start
  159.9 0.0 collective-permute-done.6.part_ref
  159.9 3.6 %gram_last.1 = (f32[1280,128]{1,0:T(8,128)S(1)}, bf16[64,4096]{1,0:T(8,128)(2,1)S(1)}, bf16[64,4096]{1,0:T(8,128)(2,1)S(1)}) custom-call(s32[8]{0:T(128)S(1)} %broadcast_xor_fusion.places_ref, f32[1280,128]{1,0:T(8,128)S(1)} %get-tuple-element.12.before_ref, f32[64,4096]{1,0:T(8,128)S(1)} %collective-permute-done.6.part_ref, ...), custom_call_target="tpu_custom_call" | custom-call | flops 805306368 | bytes 8388608 | tf_op jit(solution)/shard_map/gram_last/pallas_call | solution.py:103
  163.5 0.0 copy-done
  163.6 0.1 collective-permute-start.7
  163.7 1.6 collective-permute-done.7
  165.4 1.6 collective-permute-start.8
  167.0 3.7 %collective-permute-done.8 = f32[320,128]{1,0:T(8,128)S(1)} collective-permute-done((f32[320,128]{1,0:T(8,128)S(1)}, f32[320,128]{1,0:T(8,128)S(1)}, u32[]{:S(2)}, u32[]{:S(2)}) %collective-permute-start.8) | collective-permute-done | bytes 163872 | tf_op jit(solution)/shard_map/ppermute | solution.py:128
  170.8 1.6 collective-permute-start.9
  172.4 3.8 %collective-permute-done.9 = f32[320,128]{1,0:T(8,128)S(1)} collective-permute-done((f32[320,128]{1,0:T(8,128)S(1)}, f32[320,128]{1,0:T(8,128)S(1)}, u32[]{:S(2)}, u32[]{:S(2)}) %collective-permute-start.9) | collective-permute-done | bytes 163872 | tf_op jit(solution)/shard_map/ppermute | solution.py:128
  176.2 28.5 %collective-permute-start.10 = (f32[320,128]{1,0:T(8,128)S(1)}, f32[320,128]{1,0:T(8,128)S(1)}, u32[]{:S(2)}, u32[]{:S(2)}) collective-permute-start(f32[320,128]{1,0:T(8,128)S(1)} %add.53), channel_id=1, source_target_pairs={{0,8},{4,12},{8,0},{12,4},{16,24},{20,28},{24,16},{28,20},{1,17},{... | collective-permute-start | bytes 491528 | tf_op jit(solution)/shard_map/ppermute | solution.py:128
  204.7 3.9 %collective-permute-done.10 = f32[320,128]{1,0:T(8,128)S(1)} collective-permute-done((f32[320,128]{1,0:T(8,128)S(1)}, f32[320,128]{1,0:T(8,128)S(1)}, u32[]{:S(2)}, u32[]{:S(2)}) %collective-permute-start.10) | collective-permute-done | bytes 163872 | tf_op jit(solution)/shard_map/ppermute | solution.py:128
  208.6 3.3 %collective-permute-start.11 = (f32[320,128]{1,0:T(8,128)S(1)}, f32[320,128]{1,0:T(8,128)S(1)}, u32[]{:S(2)}, u32[]{:S(2)}) collective-permute-start(f32[320,128]{1,0:T(8,128)S(1)} %add.54), channel_id=1, source_target_pairs={{0,16},{4,20},{8,24},{12,28},{16,0},{20,4},{24,8},{28,12},{1,3},{5... | collective-permute-start | bytes 491528 | tf_op jit(solution)/shard_map/ppermute | solution.py:128
  211.9 5.1 %collective-permute-done.11 = f32[320,128]{1,0:T(8,128)S(1)} collective-permute-done((f32[320,128]{1,0:T(8,128)S(1)}, f32[320,128]{1,0:T(8,128)S(1)}, u32[]{:S(2)}, u32[]{:S(2)}) %collective-permute-start.11) | collective-permute-done | bytes 163872 | tf_op jit(solution)/shard_map/ppermute | solution.py:128
  217.0 1.6 collective-permute-start.12
  218.6 3.8 %collective-permute-done.12 = f32[320,128]{1,0:T(8,128)S(1)} collective-permute-done((f32[320,128]{1,0:T(8,128)S(1)}, f32[320,128]{1,0:T(8,128)S(1)}, u32[]{:S(2)}, u32[]{:S(2)}) %collective-permute-start.12) | collective-permute-done | bytes 163872 | tf_op jit(solution)/shard_map/ppermute | solution.py:128
  222.4 0.1 collective-permute-start.13
  222.5 1.6 collective-permute-done.13
  224.2 0.0 copy-start.1
  224.2 0.0 copy-start.2
  224.2 15.0 %factor.1 = (f32[512,512]{1,0:T(8,128)}, f32[512,512]{1,0:T(8,128)S(1)}) custom-call(f32[1280,128]{1,0:T(8,128)S(1)} %maximum_select_fusion.gram_ref), custom_call_target="tpu_custom_call" | custom-call | flops 13421772800 | bytes 2097152 | tf_op jit(solution)/shard_map/factor/pallas_call | solution.py:276
  239.2 0.0 copy-done.1
  239.2 0.0 copy-done.2
  239.2 7.8 %modes.1 = f32[512,4096]{1,0:T(8,128)} custom-call(s32[8]{0:T(128)S(1)} %broadcast_xor_fusion.places_ref, f32[512,512]{1,0:T(8,128)S(1)} %get-tuple-element.16.w_ref, bf16[512,4096]{1,0:T(8,128)(2,1)S(1)} %copy-done.1, bf16[512,4096]{1,0:T(8,128)(2,1)S(1)} %copy-done.2, bf16[64,4096]{1,0:T(8,128)(2,1)S(1)} %get-tuple-element.19.hi_last, ...), custom_call_target="tpu_custom_call" | custom-call | tf_op jit(solution)/shard_map/modes/pallas_call | solution.py:322
  (10 shorter events, 0.3 us)
Async XLA Ops:
  2.7 73.3 %collective-permute-start.3 = (f32[64,4096]{1,0:T(8,128)}, f32[64,4096]{1,0:T(8,128)S(1)}, u32[]{:S(2)}, u32[]{:S(2)}) collective-permute-start(f32[64,4096]{1,0:T(8,128)} %cut.1), channel_id=1, source_target_pairs={{0,16},{4,20},{8,24},{12,28},{16,0},{20,4},{24,8},{28,12},{1,17},{... | collective-permute-start | bytes 3145736 | tf_op jit(solution)/shard_map/ppermute | solution.py:384
  6.8 97.6 %copy-start.5 = (s32[8]{0:T(128)S(1)}, s32[8]{0:T(128)}, u32[]{:S(2)}) copy-start(s32[8]{0:T(128)} %constant.46.clone) | copy-start | bytes 100
  12.4 87.5 %collective-permute-start.4 = (f32[64,4096]{1,0:T(8,128)S(1)}, f32[64,4096]{1,0:T(8,128)S(1)}, u32[]{:S(2)}, u32[]{:S(2)}) collective-permute-start(f32[64,4096]{1,0:T(8,128)S(1)} %get-tuple-element.23), channel_id=1, source_target_pairs={{0,20},{4,16},{8,28},{12,24},{16,4},{20,0},{24,12},{28,8},{1,21},{... | collective-permute-start | bytes 3145736 | tf_op jit(solution)/shard_map/ppermute | solution.py:384
  13.7 90.8 %collective-permute-start.2 = (f32[64,4096]{1,0:T(8,128)}, f32[64,4096]{1,0:T(8,128)}, u32[]{:S(2)}, u32[]{:S(2)}) collective-permute-start(f32[64,4096]{1,0:T(8,128)} %get-tuple-element.24), channel_id=1, source_target_pairs={{0,12},{4,8},{8,4},{12,0},{16,28},{20,24},{24,20},{28,16},{1,13},{... | collective-permute-start | bytes 3145736 | tf_op jit(solution)/shard_map/ppermute | solution.py:384
  15.2 134.3 %collective-permute-start.1 = (f32[64,4096]{1,0:T(8,128)}, f32[64,4096]{1,0:T(8,128)}, u32[]{:S(2)}, u32[]{:S(2)}) collective-permute-start(f32[64,4096]{1,0:T(8,128)} %get-tuple-element.25), channel_id=1, source_target_pairs={{0,8},{4,12},{8,0},{12,4},{16,24},{20,28},{24,16},{28,20},{1,9},{5... | collective-permute-start | bytes 3145736 | tf_op jit(solution)/shard_map/ppermute | solution.py:384
  15.4 134.1 %collective-permute-start = (f32[64,4096]{1,0:T(8,128)}, f32[64,4096]{1,0:T(8,128)}, u32[]{:S(2)}, u32[]{:S(2)}) collective-permute-start(f32[64,4096]{1,0:T(8,128)} %get-tuple-element.26), channel_id=1, source_target_pairs={{0,4},{4,0},{8,12},{12,8},{16,20},{20,16},{24,28},{28,24},{1,5},{5... | collective-permute-start | bytes 3145736 | tf_op jit(solution)/shard_map/ppermute | solution.py:384
  76.1 73.5 %collective-permute-start.5 = (f32[64,4096]{1,0:T(8,128)}, f32[64,4096]{1,0:T(8,128)}, u32[]{:S(2)}, u32[]{:S(2)}) collective-permute-start(f32[64,4096]{1,0:T(8,128)} %get-tuple-element.28), channel_id=1, source_target_pairs={{0,28},{4,24},{8,20},{12,16},{16,12},{20,8},{24,4},{28,0},{1,29},{... | collective-permute-start | bytes 3145736 | tf_op jit(solution)/shard_map/ppermute | solution.py:384
  99.9 1.1 copy-start.3
  100.9 59.0 %collective-permute-start.6 = (f32[64,4096]{1,0:T(8,128)}, f32[64,4096]{1,0:T(8,128)S(1)}, u32[]{:S(2)}, u32[]{:S(2)}) collective-permute-start(f32[64,4096]{1,0:T(8,128)} %get-tuple-element.22), channel_id=1, source_target_pairs={{0,24},{4,28},{8,16},{12,20},{16,8},{20,12},{24,0},{28,4},{1,25},{... | collective-permute-start | bytes 3145736 | tf_op jit(solution)/shard_map/ppermute | solution.py:384
  149.5 1.2 copy-start.4
  159.9 3.7 %copy-start = (bf16[512,4096]{1,0:T(8,128)(2,1)}, bf16[512,4096]{1,0:T(8,128)(2,1)S(1)}, u32[]{:S(2)}) copy-start(bf16[512,4096]{1,0:T(8,128)(2,1)S(1)} %get-tuple-element.17.hi_ref) | copy-start | bytes 12582916
  163.6 1.7 collective-permute-start.7
  165.4 5.4 %collective-permute-start.8 = (f32[320,128]{1,0:T(8,128)S(1)}, f32[320,128]{1,0:T(8,128)S(1)}, u32[]{:S(2)}, u32[]{:S(2)}) collective-permute-start(f32[320,128]{1,0:T(8,128)S(1)} %slice_select_fusion.1), channel_id=1, source_target_pairs={{0,2},{4,6},{8,10},{12,14},{16,18},{20,22},{24,26},{28,30},{1,5},{... | collective-permute-start | bytes 491528 | tf_op jit(solution)/shard_map/ppermute | solution.py:128
  170.8 5.4 %collective-permute-start.9 = (f32[320,128]{1,0:T(8,128)S(1)}, f32[320,128]{1,0:T(8,128)S(1)}, u32[]{:S(2)}, u32[]{:S(2)}) collective-permute-start(f32[320,128]{1,0:T(8,128)S(1)} %select_add_fusion.1), channel_id=1, source_target_pairs={{0,4},{4,0},{8,12},{12,8},{16,20},{20,16},{24,28},{28,24},{1,9},{5... | collective-permute-start | bytes 491528 | tf_op jit(solution)/shard_map/ppermute | solution.py:128
  176.2 32.4 %collective-permute-start.10 = (f32[320,128]{1,0:T(8,128)S(1)}, f32[320,128]{1,0:T(8,128)S(1)}, u32[]{:S(2)}, u32[]{:S(2)}) collective-permute-start(f32[320,128]{1,0:T(8,128)S(1)} %add.53), channel_id=1, source_target_pairs={{0,8},{4,12},{8,0},{12,4},{16,24},{20,28},{24,16},{28,20},{1,17},{... | collective-permute-start | bytes 491528 | tf_op jit(solution)/shard_map/ppermute | solution.py:128
  208.6 8.4 %collective-permute-start.11 = (f32[320,128]{1,0:T(8,128)S(1)}, f32[320,128]{1,0:T(8,128)S(1)}, u32[]{:S(2)}, u32[]{:S(2)}) collective-permute-start(f32[320,128]{1,0:T(8,128)S(1)} %add.54), channel_id=1, source_target_pairs={{0,16},{4,20},{8,24},{12,28},{16,0},{20,4},{24,8},{28,12},{1,3},{5... | collective-permute-start | bytes 491528 | tf_op jit(solution)/shard_map/ppermute | solution.py:128
  217.0 5.4 %collective-permute-start.12 = (f32[320,128]{1,0:T(8,128)S(1)}, f32[320,128]{1,0:T(8,128)S(1)}, u32[]{:S(2)}, u32[]{:S(2)}) collective-permute-start(f32[320,128]{1,0:T(8,128)S(1)} %add.55), channel_id=1, source_target_pairs={{0,2},{4,6},{8,10},{12,14},{16,18},{20,22},{24,26},{28,30},{1,5},{... | collective-permute-start | bytes 491528 | tf_op jit(solution)/shard_map/ppermute | solution.py:128
  222.4 1.7 collective-permute-start.13
  224.2 15.0 %copy-start.1 = (bf16[512,4096]{1,0:T(8,128)(2,1)S(1)}, bf16[512,4096]{1,0:T(8,128)(2,1)}, u32[]{:S(2)}) copy-start(bf16[512,4096]{1,0:T(8,128)(2,1)} %copy-done) | copy-start | bytes 12582916
  224.2 15.0 %copy-start.2 = (bf16[512,4096]{1,0:T(8,128)(2,1)S(1)}, bf16[512,4096]{1,0:T(8,128)(2,1)}, u32[]{:S(2)}) copy-start(bf16[512,4096]{1,0:T(8,128)(2,1)} %get-tuple-element.18.lo_ref) | copy-start | bytes 12582916

commit v8 on v7

--- a/solution.py
+++ b/solution.py
@@ -239,7 +239,7 @@
     return inverse, upper
 
 
-def factor_kernel(root, gram_ref, lower_ref, white_ref, work, xs, us):
+def factor_kernel(root, gram_ref, lower_ref, white_hi, white_lo, work, xs, us):
     size = lower_ref.shape[0]
     blocks = size // BLK
     for n, (i, j) in enumerate(lower_blocks(size)):
@@ -266,18 +266,20 @@
             work[down, :] = work[down, :] - jnp.dot(left, y, precision=FULL, preferred_element_type=jnp.float32)
             lower_ref[down, here] = left * (1.0 / root)
             lower_ref[here, down] = zero
-            white_ref[here, down] = zero
+            white_hi[here, down] = white_lo[here, down] = zero.astype(jnp.bfloat16)
         lower_ref[here, here] = us[...].T * (1.0 / root)
-        white_ref[here, : (b + 1) * BLK] = y[:, : (b + 1) * BLK] * root
+        done = slice(0, (b + 1) * BLK)
+        white_hi[here, done], white_lo[here, done] = split(y[:, done] * root)
 
 
 def factorize(packed, size, root):
     out = jax.ShapeDtypeStruct((size, size), jnp.float32)
+    part = jax.ShapeDtypeStruct((size, size), jnp.bfloat16)
     return pl.pallas_call(
         functools.partial(factor_kernel, root),
-        out_shape=(out, out),
+        out_shape=(out, part, part),
         in_specs=[VMEM],
-        out_specs=(VMEM, VMEM),
+        out_specs=(VMEM, VMEM, VMEM),
         scratch_shapes=[
             pltpu.VMEM((size, size), jnp.float32),
             pltpu.VMEM((BLK, BLK), jnp.float32),
@@ -289,13 +291,12 @@
     )(packed)
 
 
-def modes_kernel(places_ref, w_ref, hi_ref, lo_ref, hi_last, lo_last, out_ref, w_hi, w_lo, s_hi, s_lo, tiles, sems):
+def modes_kernel(places_ref, w_hi, w_lo, hi_ref, lo_ref, hi_last, lo_last, out_ref, s_hi, s_lo, tiles, sems):
     size, cells = hi_ref.shape
     rows = hi_last.shape[0]
     slots, _, tile = tiles.shape
     half = size // 2
     at = pl.ds(pl.multiple_of(places_ref[places_ref.shape[0] - 1] * rows, rows), rows)
-    w_hi[...], w_lo[...] = split(w_ref[...])
     copies = []
     for t in range(cells // tile):
         slot, here = t % slots, slice(t * tile, (t + 1) * tile)
@@ -317,16 +318,14 @@
         copy.wait()
 
 
-def whiten(places, w, hi, lo, hi_last, lo_last, tile, slots):
+def whiten(places, w_hi, w_lo, hi, lo, hi_last, lo_last, tile, slots):
     size, cells = hi.shape
     return pl.pallas_call(
         modes_kernel,
         out_shape=jax.ShapeDtypeStruct((size, cells), jnp.float32),
-        in_specs=[SMEM, *[VMEM] * 5],
+        in_specs=[SMEM, *[VMEM] * 6],
         out_specs=ANY,
         scratch_shapes=[
-            pltpu.VMEM((size, size), jnp.bfloat16),
-            pltpu.VMEM((size, size), jnp.bfloat16),
             pltpu.VMEM((2, size, tile), jnp.bfloat16),
             pltpu.VMEM((2, size, tile), jnp.bfloat16),
             pltpu.VMEM((slots, size, tile), jnp.float32),
@@ -334,7 +333,7 @@
         ],
         compiler_params=pltpu.CompilerParams(vmem_limit_bytes=16 * 2**20),
         name="modes",
-    )(places, w, hi, lo, hi_last, lo_last)
+    )(places, w_hi, w_lo, hi, lo, hi_last, lo_last)
 
 
 def cut_kernel(place_ref, x_ref, out_ref, held, come, go):
@@ -393,8 +392,8 @@
     places, parts = regroup(snapshots)
     packed, hi, lo, hi_kept, lo_kept = gram(places, parts[:-1], cells // 8)
     packed, hi_last, lo_last = add_last(places, packed, parts[-1], hi, lo)
-    factor, white = factorize(sum_all(packed), size, root)
-    return whiten(places, white, hi_kept, lo_kept, hi_last, lo_last, cells // 8, 4), factor
+    factor, w_hi, w_lo = factorize(sum_all(packed), size, root)
+    return whiten(places, w_hi, w_lo, hi_kept, lo_kept, hi_last, lo_last, cells // 8, 4), factor
 
 
 def solution(mesh):

time: 247 us -> 247 us (level)
  no operation moved by 1% of the time
where the time goes in v8:
time: 247 us
  waiting for transfers between devices  148 us (60%)
  starting transfers between devices  52.9 us (21%)
  Pallas kernels  37.7 us (15%)
  local copies, waits for them, and re-layouts  7.85 us (3%)
    ppermute x7, waiting for transfers between devices, regroup(): lax.ppermute(block, 'snap', [(i, i ^ d) for i in range(n)])  124 us
    ppermute x7, starting transfers between devices, step(): return lax.ppermute(x, ('snap', 'row'), pairs)  36.8 us
    ppermute x7, waiting for transfers between devices, step(): return lax.ppermute(x, ('snap', 'row'), pairs)  23.5 us
    ppermute x7, starting transfers between devices, regroup(): lax.ppermute(block, 'snap', [(i, i ^ d) for i in range(n)])  16.1 us
    pallas_call x1, Pallas kernels, factorize(): pl.pallas_call(functools.partial(factor_kernel, root), out_shape=(out, pa...  15 us
    pallas_call x1, Pallas kernels, gram(): pl.pallas_call(functools.partial(gram_kernel, n, tile), out_shape=(jax.Sh...  9.1 us
    pallas_call x1, Pallas kernels, whiten(): pl.pallas_call(modes_kernel, out_shape=jax.ShapeDtypeStruct((size, cells)...  7.85 us
    dynamic_slice x1, local copies, waits for them, and re-layouts, regroup(): block = lax.dynamic_slice_in_dim(snapshots, (me ^ d) * cells, cells, axis=1)  5.55 us
  transfers between devices with their start and end apart: 14, of which 10 were waited for; matrix products, arithmetic and copies ran while one was open for 2% of the time, Pallas kernels for 4%

profile of v8, /device:TPU:0, one launch (start us, length us, event | category | flops | bytes accessed | tf_op | source)
XLA Modules:
  0.0 247.3 jit_solution(8184472537683529457)
XLA Ops:
  0.6 2.1 cut.1
  2.7 4.1 %collective-permute-start.3 = (f32[64,4096]{1,0:T(8,128)}, f32[64,4096]{1,0:T(8,128)S(1)}, u32[]{:S(2)}, u32[]{:S(2)}) collective-permute-start(f32[64,4096]{1,0:T(8,128)} %cut.1), channel_id=1, source_target_pairs={{0,16},{4,20},{8,24},{12,28},{16,0},{20,4},{24,8},{28,12},{1,17},{... | collective-permute-start | bytes 3145736 | tf_op jit(solution)/shard_map/ppermute | solution.py:383
  6.8 0.0 copy-start.5
  6.8 5.6 %constant_dynamic-slice_fusion = (f32[64,4096]{1,0:T(8,128)}, f32[64,4096]{1,0:T(8,128)S(1)}, f32[64,4096]{1,0:T(8,128)}, f32[64,4096]{1,0:T(8,128)}, f32[64,409...) fusion(f32[64,32768]{1,0:T(8,128)} %x_ref.1, s32[]{:T(128)S(6)} %select_n.91, s32[]{:T(128)S(6)} %select_n.89, ...), kind=kLoop, calls=%fused_computation.6 | loop fusion | bytes 14680092 | tf_op jit(solution)/shard_map/dynamic_slice | solution.py:382
  12.4 1.3 collective-permute-start.4
  13.7 1.5 collective-permute-start.2
  15.2 0.2 collective-permute-start.1
  15.4 1.8 collective-permute-start
  17.2 58.9 %collective-permute-done.3.refs_4_ = f32[64,4096]{1,0:T(8,128)S(1)} collective-permute-done((f32[64,4096]{1,0:T(8,128)}, f32[64,4096]{1,0:T(8,128)S(1)}, u32[]{:S(2)}, u32[]{:S(2)}) %collective-permute-start.3) | collective-permute-done | bytes 1048608 | tf_op jit(solution)/shard_map/ppermute | solution.py:383
  76.1 3.7 %collective-permute-start.5 = (f32[64,4096]{1,0:T(8,128)}, f32[64,4096]{1,0:T(8,128)}, u32[]{:S(2)}, u32[]{:S(2)}) collective-permute-start(f32[64,4096]{1,0:T(8,128)} %get-tuple-element.30), channel_id=1, source_target_pairs={{0,28},{4,24},{8,20},{12,16},{16,12},{20,8},{24,4},{28,0},{1,29},{... | collective-permute-start | bytes 3145736 | tf_op jit(solution)/shard_map/ppermute | solution.py:383
  79.8 20.1 %collective-permute-done.4.refs_5_ = f32[64,4096]{1,0:T(8,128)S(1)} collective-permute-done((f32[64,4096]{1,0:T(8,128)S(1)}, f32[64,4096]{1,0:T(8,128)S(1)}, u32[]{:S(2)}, u32[]{:S(2)}) %collective-permute-start.4) | collective-permute-done | bytes 1048608 | tf_op jit(solution)/shard_map/ppermute | solution.py:383
  99.9 0.0 copy-start.3
  99.9 1.1 copy-done.3
  100.9 3.5 %collective-permute-start.6 = (f32[64,4096]{1,0:T(8,128)}, f32[64,4096]{1,0:T(8,128)S(1)}, u32[]{:S(2)}, u32[]{:S(2)}) collective-permute-start(f32[64,4096]{1,0:T(8,128)} %get-tuple-element.24), channel_id=1, source_target_pairs={{0,24},{4,28},{8,16},{12,20},{16,8},{20,12},{24,0},{28,4},{1,25},{... | collective-permute-start | bytes 3145736 | tf_op jit(solution)/shard_map/ppermute | solution.py:383
  104.4 0.0 copy-done.5
  104.5 0.0 collective-permute-done.2.refs_3_
  104.5 45.1 %collective-permute-done.1.refs_2_ = f32[64,4096]{1,0:T(8,128)} collective-permute-done((f32[64,4096]{1,0:T(8,128)}, f32[64,4096]{1,0:T(8,128)}, u32[]{:S(2)}, u32[]{:S(2)}) %collective-permute-start.1) | collective-permute-done | bytes 1048608 | tf_op jit(solution)/shard_map/ppermute | solution.py:383
  149.5 0.0 collective-permute-done.refs_1_
  149.5 0.0 collective-permute-done.5.refs_6_
  149.5 0.0 copy-start.4
  149.6 1.2 copy-done.4
  150.8 9.1 %gram.1 = (f32[1280,128]{1,0:T(8,128)S(1)}, bf16[512,4096]{1,0:T(8,128)(2,1)S(1)}, bf16[512,4096]{1,0:T(8,128)(2,1)S(1)}, bf16[512,4096]{1,0:T(8,128)(2,1)S(1)}, bf16[512,4096]{1,0:T(8,128)(2,1)}) custom-call(s32[8]{0:T(128)S(1)} %broadcast_xor_fusion.places_ref, f32[64,4096]{1,0:T(8,128)S(1)} %get-tuple-element.29.refs_0_, ...), custom_call_target="tpu_custom_call" | custom-call | flops 4294967296 | bytes 16777216 | tf_op jit(solution)/shard_map/gram/pallas_call | solution.py:65
  159.9 0.0 copy-start
  159.9 0.0 collective-permute-done.6.part_ref
  159.9 3.6 %gram_last.1 = (f32[1280,128]{1,0:T(8,128)S(1)}, bf16[64,4096]{1,0:T(8,128)(2,1)S(1)}, bf16[64,4096]{1,0:T(8,128)(2,1)S(1)}) custom-call(s32[8]{0:T(128)S(1)} %broadcast_xor_fusion.places_ref, f32[1280,128]{1,0:T(8,128)S(1)} %get-tuple-element.13.before_ref, f32[64,4096]{1,0:T(8,128)S(1)} %collective-permute-done.6.part_ref, ...), custom_call_target="tpu_custom_call" | custom-call | flops 805306368 | bytes 8388608 | tf_op jit(solution)/shard_map/gram_last/pallas_call | solution.py:103
  163.5 0.0 copy-done
  163.6 0.1 collective-permute-start.7
  163.7 1.6 collective-permute-done.7
  165.4 1.6 collective-permute-start.8
  167.0 3.7 %collective-permute-done.8 = f32[320,128]{1,0:T(8,128)S(1)} collective-permute-done((f32[320,128]{1,0:T(8,128)S(1)}, f32[320,128]{1,0:T(8,128)S(1)}, u32[]{:S(2)}, u32[]{:S(2)}) %collective-permute-start.8) | collective-permute-done | bytes 163872 | tf_op jit(solution)/shard_map/ppermute | solution.py:128
  170.8 1.6 collective-permute-start.9
  172.4 3.8 %collective-permute-done.9 = f32[320,128]{1,0:T(8,128)S(1)} collective-permute-done((f32[320,128]{1,0:T(8,128)S(1)}, f32[320,128]{1,0:T(8,128)S(1)}, u32[]{:S(2)}, u32[]{:S(2)}) %collective-permute-start.9) | collective-permute-done | bytes 163872 | tf_op jit(solution)/shard_map/ppermute | solution.py:128
  176.2 28.5 %collective-permute-start.10 = (f32[320,128]{1,0:T(8,128)S(1)}, f32[320,128]{1,0:T(8,128)S(1)}, u32[]{:S(2)}, u32[]{:S(2)}) collective-permute-start(f32[320,128]{1,0:T(8,128)S(1)} %add.53), channel_id=1, source_target_pairs={{0,8},{4,12},{8,0},{12,4},{16,24},{20,28},{24,16},{28,20},{1,17},{... | collective-permute-start | bytes 491528 | tf_op jit(solution)/shard_map/ppermute | solution.py:128
  204.7 3.9 %collective-permute-done.10 = f32[320,128]{1,0:T(8,128)S(1)} collective-permute-done((f32[320,128]{1,0:T(8,128)S(1)}, f32[320,128]{1,0:T(8,128)S(1)}, u32[]{:S(2)}, u32[]{:S(2)}) %collective-permute-start.10) | collective-permute-done | bytes 163872 | tf_op jit(solution)/shard_map/ppermute | solution.py:128
  208.6 3.3 %collective-permute-start.11 = (f32[320,128]{1,0:T(8,128)S(1)}, f32[320,128]{1,0:T(8,128)S(1)}, u32[]{:S(2)}, u32[]{:S(2)}) collective-permute-start(f32[320,128]{1,0:T(8,128)S(1)} %add.54), channel_id=1, source_target_pairs={{0,16},{4,20},{8,24},{12,28},{16,0},{20,4},{24,8},{28,12},{1,3},{5... | collective-permute-start | bytes 491528 | tf_op jit(solution)/shard_map/ppermute | solution.py:128
  211.9 5.1 %collective-permute-done.11 = f32[320,128]{1,0:T(8,128)S(1)} collective-permute-done((f32[320,128]{1,0:T(8,128)S(1)}, f32[320,128]{1,0:T(8,128)S(1)}, u32[]{:S(2)}, u32[]{:S(2)}) %collective-permute-start.11) | collective-permute-done | bytes 163872 | tf_op jit(solution)/shard_map/ppermute | solution.py:128
  217.0 1.6 collective-permute-start.12
  218.6 3.8 %collective-permute-done.12 = f32[320,128]{1,0:T(8,128)S(1)} collective-permute-done((f32[320,128]{1,0:T(8,128)S(1)}, f32[320,128]{1,0:T(8,128)S(1)}, u32[]{:S(2)}, u32[]{:S(2)}) %collective-permute-start.12) | collective-permute-done | bytes 163872 | tf_op jit(solution)/shard_map/ppermute | solution.py:128
  222.4 0.1 collective-permute-start.13
  222.5 1.6 collective-permute-done.13
  224.2 0.0 copy-start.1
  224.2 0.0 copy-start.2
  224.2 15.0 %factor.1 = (f32[512,512]{1,0:T(8,128)}, bf16[512,512]{1,0:T(8,128)(2,1)S(1)}, bf16[512,512]{1,0:T(8,128)(2,1)S(1)}) custom-call(f32[1280,128]{1,0:T(8,128)S(1)} %maximum_select_fusion.gram_ref), custom_call_target="tpu_custom_call" | custom-call | flops 13421772800 | bytes 2097152 | tf_op jit(solution)/shard_map/factor/pallas_call | solution.py:278
  239.2 0.0 copy-done.1
  239.2 0.0 copy-done.2
  239.2 7.8 %modes.1 = f32[512,4096]{1,0:T(8,128)} custom-call(s32[8]{0:T(128)S(1)} %broadcast_xor_fusion.places_ref, bf16[512,512]{1,0:T(8,128)(2,1)S(1)} %get-tuple-element.17.w_hi, bf16[512,512]{1,0:T(8,128)(2,1)S(1)} %get-tuple-element.18.w_lo, bf16[512,4096]{1,0:T(8,128)(2,1)S(1)} %copy-done.1, bf16[512,4096]{1,0:T(8,128)(2,1)S(1)} %copy-done.2, ...), custom_call_target="tpu_custom_call" | custom-call | tf_op jit(solution)/shard_map/modes/pallas_call | solution.py:323
  (10 shorter events, 0.3 us)
Async XLA Ops:
  2.7 73.3 %collective-permute-start.3 = (f32[64,4096]{1,0:T(8,128)}, f32[64,4096]{1,0:T(8,128)S(1)}, u32[]{:S(2)}, u32[]{:S(2)}) collective-permute-start(f32[64,4096]{1,0:T(8,128)} %cut.1), channel_id=1, source_target_pairs={{0,16},{4,20},{8,24},{12,28},{16,0},{20,4},{24,8},{28,12},{1,17},{... | collective-permute-start | bytes 3145736 | tf_op jit(solution)/shard_map/ppermute | solution.py:383
  6.8 97.6 %copy-start.5 = (s32[8]{0:T(128)S(1)}, s32[8]{0:T(128)}, u32[]{:S(2)}) copy-start(s32[8]{0:T(128)} %constant.46.clone) | copy-start | bytes 100
  12.4 87.5 %collective-permute-start.4 = (f32[64,4096]{1,0:T(8,128)S(1)}, f32[64,4096]{1,0:T(8,128)S(1)}, u32[]{:S(2)}, u32[]{:S(2)}) collective-permute-start(f32[64,4096]{1,0:T(8,128)S(1)} %get-tuple-element.25), channel_id=1, source_target_pairs={{0,20},{4,16},{8,28},{12,24},{16,4},{20,0},{24,12},{28,8},{1,21},{... | collective-permute-start | bytes 3145736 | tf_op jit(solution)/shard_map/ppermute | solution.py:383
  13.7 90.8 %collective-permute-start.2 = (f32[64,4096]{1,0:T(8,128)}, f32[64,4096]{1,0:T(8,128)}, u32[]{:S(2)}, u32[]{:S(2)}) collective-permute-start(f32[64,4096]{1,0:T(8,128)} %get-tuple-element.26), channel_id=1, source_target_pairs={{0,12},{4,8},{8,4},{12,0},{16,28},{20,24},{24,20},{28,16},{1,13},{... | collective-permute-start | bytes 3145736 | tf_op jit(solution)/shard_map/ppermute | solution.py:383
  15.2 134.3 %collective-permute-start.1 = (f32[64,4096]{1,0:T(8,128)}, f32[64,4096]{1,0:T(8,128)}, u32[]{:S(2)}, u32[]{:S(2)}) collective-permute-start(f32[64,4096]{1,0:T(8,128)} %get-tuple-element.27), channel_id=1, source_target_pairs={{0,8},{4,12},{8,0},{12,4},{16,24},{20,28},{24,16},{28,20},{1,9},{5... | collective-permute-start | bytes 3145736 | tf_op jit(solution)/shard_map/ppermute | solution.py:383
  15.4 134.1 %collective-permute-start = (f32[64,4096]{1,0:T(8,128)}, f32[64,4096]{1,0:T(8,128)}, u32[]{:S(2)}, u32[]{:S(2)}) collective-permute-start(f32[64,4096]{1,0:T(8,128)} %get-tuple-element.28), channel_id=1, source_target_pairs={{0,4},{4,0},{8,12},{12,8},{16,20},{20,16},{24,28},{28,24},{1,5},{5... | collective-permute-start | bytes 3145736 | tf_op jit(solution)/shard_map/ppermute | solution.py:383
  76.1 73.5 %collective-permute-start.5 = (f32[64,4096]{1,0:T(8,128)}, f32[64,4096]{1,0:T(8,128)}, u32[]{:S(2)}, u32[]{:S(2)}) collective-permute-start(f32[64,4096]{1,0:T(8,128)} %get-tuple-element.30), channel_id=1, source_target_pairs={{0,28},{4,24},{8,20},{12,16},{16,12},{20,8},{24,4},{28,0},{1,29},{... | collective-permute-start | bytes 3145736 | tf_op jit(solution)/shard_map/ppermute | solution.py:383
  99.9 1.1 copy-start.3
  100.9 59.0 %collective-permute-start.6 = (f32[64,4096]{1,0:T(8,128)}, f32[64,4096]{1,0:T(8,128)S(1)}, u32[]{:S(2)}, u32[]{:S(2)}) collective-permute-start(f32[64,4096]{1,0:T(8,128)} %get-tuple-element.24), channel_id=1, source_target_pairs={{0,24},{4,28},{8,16},{12,20},{16,8},{20,12},{24,0},{28,4},{1,25},{... | collective-permute-start | bytes 3145736 | tf_op jit(solution)/shard_map/ppermute | solution.py:383
  149.5 1.2 copy-start.4
  159.9 3.7 %copy-start = (bf16[512,4096]{1,0:T(8,128)(2,1)}, bf16[512,4096]{1,0:T(8,128)(2,1)S(1)}, u32[]{:S(2)}) copy-start(bf16[512,4096]{1,0:T(8,128)(2,1)S(1)} %get-tuple-element.19.hi_ref) | copy-start | bytes 12582916
  163.6 1.7 collective-permute-start.7
  165.4 5.4 %collective-permute-start.8 = (f32[320,128]{1,0:T(8,128)S(1)}, f32[320,128]{1,0:T(8,128)S(1)}, u32[]{:S(2)}, u32[]{:S(2)}) collective-permute-start(f32[320,128]{1,0:T(8,128)S(1)} %slice_select_fusion.1), channel_id=1, source_target_pairs={{0,2},{4,6},{8,10},{12,14},{16,18},{20,22},{24,26},{28,30},{1,5},{... | collective-permute-start | bytes 491528 | tf_op jit(solution)/shard_map/ppermute | solution.py:128
  170.8 5.4 %collective-permute-start.9 = (f32[320,128]{1,0:T(8,128)S(1)}, f32[320,128]{1,0:T(8,128)S(1)}, u32[]{:S(2)}, u32[]{:S(2)}) collective-permute-start(f32[320,128]{1,0:T(8,128)S(1)} %select_add_fusion.1), channel_id=1, source_target_pairs={{0,4},{4,0},{8,12},{12,8},{16,20},{20,16},{24,28},{28,24},{1,9},{5... | collective-permute-start | bytes 491528 | tf_op jit(solution)/shard_map/ppermute | solution.py:128
  176.2 32.4 %collective-permute-start.10 = (f32[320,128]{1,0:T(8,128)S(1)}, f32[320,128]{1,0:T(8,128)S(1)}, u32[]{:S(2)}, u32[]{:S(2)}) collective-permute-start(f32[320,128]{1,0:T(8,128)S(1)} %add.53), channel_id=1, source_target_pairs={{0,8},{4,12},{8,0},{12,4},{16,24},{20,28},{24,16},{28,20},{1,17},{... | collective-permute-start | bytes 491528 | tf_op jit(solution)/shard_map/ppermute | solution.py:128
  208.6 8.4 %collective-permute-start.11 = (f32[320,128]{1,0:T(8,128)S(1)}, f32[320,128]{1,0:T(8,128)S(1)}, u32[]{:S(2)}, u32[]{:S(2)}) collective-permute-start(f32[320,128]{1,0:T(8,128)S(1)} %add.54), channel_id=1, source_target_pairs={{0,16},{4,20},{8,24},{12,28},{16,0},{20,4},{24,8},{28,12},{1,3},{5... | collective-permute-start | bytes 491528 | tf_op jit(solution)/shard_map/ppermute | solution.py:128
  217.0 5.4 %collective-permute-start.12 = (f32[320,128]{1,0:T(8,128)S(1)}, f32[320,128]{1,0:T(8,128)S(1)}, u32[]{:S(2)}, u32[]{:S(2)}) collective-permute-start(f32[320,128]{1,0:T(8,128)S(1)} %add.55), channel_id=1, source_target_pairs={{0,2},{4,6},{8,10},{12,14},{16,18},{20,22},{24,26},{28,30},{1,5},{... | collective-permute-start | bytes 491528 | tf_op jit(solution)/shard_map/ppermute | solution.py:128
  222.4 1.7 collective-permute-start.13
  224.2 15.1 %copy-start.1 = (bf16[512,4096]{1,0:T(8,128)(2,1)S(1)}, bf16[512,4096]{1,0:T(8,128)(2,1)}, u32[]{:S(2)}) copy-start(bf16[512,4096]{1,0:T(8,128)(2,1)} %copy-done) | copy-start | bytes 12582916
  224.2 15.0 %copy-start.2 = (bf16[512,4096]{1,0:T(8,128)(2,1)S(1)}, bf16[512,4096]{1,0:T(8,128)(2,1)}, u32[]{:S(2)}) copy-start(bf16[512,4096]{1,0:T(8,128)(2,1)} %get-tuple-element.20.lo_ref) | copy-start | bytes 12582916
